TPU v7x, 512 devices: a whole 4x4x16 slice. The times are simulated.
512 devices in a mesh: dp: 32 (over y, x, core), group: 16 (over z).
Axes of the slice: x: 4, y: 4, z: 16, core: 2. Of those that a mesh axis runs over, the one named last changes fastest.
Arguments:
- patches: bfloat16 [65536, 2048], P(('dp', 'group')), may hold values from -6 to 6
- codes: float32 [65536, 8], P(('dp', 'group')), may hold values from -2 to 2
- support: int32 [65536, 8], P(('dp', 'group')), may hold values from 0 to 255
- block_shards: int32 [2048, 2], P(('dp', 'group')), may hold values from 0 to 15, all different within a row; in each aligned block of 4 rows (0 to 3, 4 to 7, ...) at most 2 rows name the same one
- dictionary: bfloat16 [2048, 2048], P('group'), may hold values from -6 to 6
Outputs:
- new_dictionary: bfloat16 [2048, 2048], P('group')
- new_codes: float32 [65536, 8], P(('dp', 'group'))
- residual: bfloat16 [65536, 2048], P(('dp', 'group'))
Inputs may be any that keep to these rules, and one draw needn't show every extreme that they name: `block_shards`: the two shards of a row differ; within the 4 rows of one device no shard is named more than 2 times, a bound that some block reaches.
All inputs are finite; a program needn't handle non-finite values.
Results may differ from a plain program's by a relative error of at most 0.0077.
Values may be sent and summed in bfloat16 or wider, within the bound.
No kernel may reach another device: no remote copies, remote signals or barrier semaphores. Data moves between devices by JAX's collectives and lax.ppermute only.
A program may use at most 64 MiB of HBM per device.

v0:
```python
import jax
import jax.numpy as jnp
from jax import lax
from jax.sharding import PartitionSpec as P

CAP = 2
ITERS = 2


def renew(atom_rows, stats, usage):
    moved = atom_rows.astype(jnp.float32) + 3.0 * stats / (usage + 1.0)[:, None]
    return (moved * lax.rsqrt(jnp.mean(moved * moved, axis=1, keepdims=True) + 1e-05)).astype(
        jnp.bfloat16
    )


def body(patches, codes, support, block_shards, dictionary):
    row_count, patch_len = patches.shape
    per_dev = dictionary.shape[0]
    group_count = lax.axis_size("group")
    atoms_all = per_dev * group_count
    blocks = block_shards.shape[0]
    blk_rows = row_count // blocks
    slots = support.shape[1]
    whole = lax.all_gather(dictionary, "group", axis=0, tiled=True)
    shard_rows = jnp.repeat(block_shards, blk_rows, axis=0)
    which_shard = support // per_dev
    local_atom = support % per_dev
    owner_shard = jnp.where(which_shard == 0, shard_rows[:, 0:1], shard_rows[:, 1:2])
    atom_index = owner_shard * per_dev + local_atom
    columns = lax.broadcasted_iota(jnp.int32, (row_count, atoms_all), 1)
    signal = patches.astype(jnp.float32)

    def code_matrix(values):
        summed = jnp.zeros((row_count, atoms_all), jnp.float32)
        for position in range(slots):
            summed = summed + jnp.where(
                atom_index[:, position : position + 1] == columns,
                values[:, position : position + 1],
                0.0,
            )
        return summed.astype(jnp.bfloat16)

    def resid_of(values):
        matrix = code_matrix(values)
        rebuilt = jnp.dot(matrix, whole, preferred_element_type=jnp.float32)
        return (matrix, (signal - rebuilt).astype(jnp.bfloat16))

    current = codes
    for iteration in range(ITERS):
        matrix, residual_rows = resid_of(current)
        scores = lax.dot_general(
            residual_rows, whole, (((1,), (1,)), ((), ())), preferred_element_type=jnp.float32
        )
        picked = [
            jnp.sum(
                jnp.where(atom_index[:, position : position + 1] == columns, scores, 0.0), axis=1
            )
            for position in range(slots)
        ]
        current = current + 1.5 * (jnp.stack(picked, axis=1) / patch_len)
    matrix, residual_rows = resid_of(current)
    block_ids = lax.broadcasted_iota(jnp.int32, (blocks, 2, blocks, 2), 0)
    other_ids = lax.broadcasted_iota(jnp.int32, (blocks, 2, blocks, 2), 2)
    same_shard = block_shards[:, :, None, None] == block_shards[None, None, :, :]
    rank = jnp.sum((same_shard & (other_ids < block_ids)).astype(jnp.int32), axis=(2, 3))
    shard_ids = lax.broadcasted_iota(jnp.int32, (group_count, CAP, blocks, 2), 0)
    slot_ids = lax.broadcasted_iota(jnp.int32, (group_count, CAP, blocks, 2), 1)
    chosen = (block_shards[None, None, :, :] == shard_ids) & (rank[None, None, :, :] == slot_ids)
    selector = jnp.sum(chosen.astype(jnp.float32), axis=3).astype(jnp.bfloat16)
    resid_blocks = residual_rows.reshape(blocks, blk_rows, patch_len)
    send_resid = jnp.einsum(
        "jcb,bip->jcip", selector, resid_blocks, preferred_element_type=jnp.float32
    ).astype(jnp.bfloat16)
    matrix_blocks = matrix.reshape(blocks, blk_rows, group_count, per_dev)
    send_codes = jnp.einsum(
        "jcb,bija->jcia", selector, matrix_blocks, preferred_element_type=jnp.float32
    ).astype(jnp.bfloat16)
    got_resid, got_codes = (
        lax.all_to_all(send_resid, "group", split_axis=0, concat_axis=0, tiled=True),
        lax.all_to_all(send_codes, "group", split_axis=0, concat_axis=0, tiled=True),
    )
    flat_codes = got_codes.reshape(-1, per_dev)
    flat_resid = got_resid.reshape(-1, patch_len)
    stats = lax.dot_general(
        flat_codes, flat_resid, (((0,), (0,)), ((), ())), preferred_element_type=jnp.float32
    )
    wide_codes = flat_codes.astype(jnp.float32)
    usage = jnp.sum(wide_codes * wide_codes, axis=0)
    full_stats, full_usage = lax.psum((stats, usage), "dp")
    new_dictionary = renew(dictionary, full_stats, full_usage)
    return (new_dictionary, current, residual_rows)


def solution(mesh):
    placed = (
        P(("dp", "group"), None),
        P(("dp", "group"), None),
        P(("dp", "group"), None),
        P(("dp", "group"), None),
        P("group", None),
    )
    return jax.shard_map(
        body,
        mesh=mesh,
        in_specs=placed,
        out_specs=(P("group", None), P(("dp", "group"), None), P(("dp", "group"), None)),
        check_vma=False,
    )
```

profile of v0, /device:TPU:1, one launch (start us, length us, event | category | flops | bytes accessed | tf_op | source)
XLA Modules:
  0.0 511.5 jit_solution(14493771705486085433)
XLA Ops:
  7.2 0.7 all-gather.2.cloned.1.call-update
  7.9 0.8 broadcast_in_dim.278
  8.7 0.7 fusion.114
  10.9 1.0 convert_reduce_fusion.1
  11.8 0.8 convert_reduce_fusion
  12.7 1.0 slice_bitcast_fusion.15
  13.7 107.7 %all-gather.2.cloned.1.call-done = bf16[2048,2048]{1,0:T(8,128)(2,1)} async-done(((bf16[128,2048]{1,0:T(8,128)(2,1)}), bf16[2048,2048]{1,0:T(8,128)(2,1)}) %all-gather.2.cloned.1.call-update) | async-done | bytes 8388624 | tf_op jit(solution)/shard_map/all_gather | solution.py:25
  121.4 5.8 %fusion.clone.1.clone.4 = bf16[128,2048]{1,0:T(8,128)(2,1)S(1)} fusion(bf16[2048,2048]{1,0:T(8,128)(2,1)} %all-gather.2.cloned.1.call-done, bf16[128,2048]{1,0:T(8,128)(2,1)} %param.5, f32[128]{0:T(128)S(1)} %get-tuple-element.74, s32[128]{0:T(128)S(1)} %get-tuple-element.52, f32[128]{0:T(128)S(1)} %get-tuple-element.68, ...), kind=kOutput, calls=%fused_computation.5.clone.clone.clone.clone.clone.1 | convolution fusion | flops 1080819712 | bytes 9445376 | tf_op jit(solution)/shard_map/dot_general | solution.py:46
  127.3 3.8 select_reduce_fusion.8
  131.2 5.6 %fusion.1.clone.1.clone.4 = bf16[128,2048]{1,0:T(8,128)(2,1)S(1)} fusion(bf16[2048,2048]{1,0:T(8,128)(2,1)} %all-gather.2.cloned.1.call-done, bf16[128,2048]{1,0:T(8,128)(2,1)S(1)} %copy-done.5, f32[128]{0:T(128)S(1)} %get-tuple-element.60, f32[128]{0:T(128)S(1)} %get-tuple-element.61, f32[128]{0:T(128)S(1)} %get-tuple-element.62, ...), kind=kOutput, calls=%fused_computation.6.clone.clone.clone.clone.clone.1 | convolution fusion | flops 1080819712 | bytes 9445376 | tf_op jit(solution)/shard_map/dot_general | solution.py:46
  136.8 7.2 %select_reduce_fusion = (f32[128]{0:T(128)S(1)}, f32[128]{0:T(128)S(1)}, f32[128]{0:T(128)S(1)}, f32[128]{0:T(128)S(1)}, f32[128]{0:T(128)S(1)}, /*index=5*/f32[128]{0:T(128)S(1)}, f32[128]{0:T(128)S(1)}, f32[128]{0:T(128)S(1)}) fusion(s32[128]{0:T(128)S(1)} %get-tuple-element.52, s32[128]{0:T(128)S(1)} %get-tuple-element.53, ...), kind=kOutput, calls=%fused_computation.14 | convolution fusion | flops 1080032256 | bytes 8921088 | tf_op jit(solution)/shard_map/dot_general | solution.py:52
  145.5 2.9 convolution_convert_fusion
  148.4 8.8 %all-to-all-start = ((bf16[16,2,32,128]{3,1,2,0:T(2,128)(2,1)}), bf16[16,2,32,128]{3,1,2,0:T(2,128)(2,1)S(1)}, u32[]{:S(2)}, u32[]{:S(2)}) async-start(bf16[16,2,32,128]{3,1,2,0:T(2,128)(2,1)} %convolution_convert_fusion), calls=%async_computation | async-start | bytes 524288 | tf_op jit(solution)/shard_map/all_to_all | solution.py:81
  157.2 5.6 %fusion.2 = bf16[128,2048]{1,0:T(8,128)(2,1)S(1)} fusion(bf16[2048,2048]{1,0:T(8,128)(2,1)} %all-gather.2.cloned.1.call-done, bf16[128,2048]{1,0:T(8,128)(2,1)S(1)} %copy-done.5, f32[128]{0:T(128)S(1)} %get-tuple-element.36, f32[128]{0:T(128)S(1)} %get-tuple-element.42, f32[128]{0:T(128)S(1)} %get-tuple-element.41, f32[128]{0:T(128)S(1)} %get-tuple-element.40, ...), kind=kOutput, calls=%fused_computation.7 | convolution fusion | flops 1080819712 | bytes 9445376 | tf_op jit(solution)/shard_map/dot_general | solution.py:46
  162.9 1.6 fusion.5
  164.5 4.2 copy.58
  168.7 1.6 all-to-all-done
  170.3 191.1 %all_to_all.10 = bf16[16,2,32,2048]{3,2,1,0:T(8,128)(2,1)S(1)} all-to-all(bf16[16,2,32,2048]{3,2,1,0:T(8,128)(2,1)} %copy.58), channel_id=1, replica_groups=mesh['dp'=32,'group'=16] {'group'}, dimensions={0} | all-to-all | bytes 8388608 | tf_op jit(solution)/shard_map/all_to_all | solution.py:80
  361.4 1.8 convolution_bitcast_fusion
  363.2 0.6 multiply_reduce_fusion.1
  363.8 69.3 %psum.15 = f32[128]{0:T(128)S(1)} all-reduce(f32[128]{0:T(128)S(1)} %multiply_reduce_fusion.1), channel_id=1, replica_groups=mesh['dp'=32,'group'=16] {'dp'}, use_global_device_ids=true, to_apply=%region_20.21 | all-reduce | flops 128 | bytes 1024 | tf_op jit(solution)/shard_map/psum | solution.py:90
  433.1 67.7 %all-reduce.2.cloned.1.call-done = f32[128,2048]{1,0:T(8,128)} async-done(((f32[128,2048]{1,0:T(8,128)}), f32[128,2048]{1,0:T(8,128)}) %all-reduce.2.cloned.1.call-update) | async-done | bytes 1048592 | tf_op jit(solution)/shard_map/psum | solution.py:90
  500.8 1.6 multiply_reduce_fusion
  502.4 2.3 multiply_convert_fusion
  (60 shorter events, 3.4 us)
Async XLA Ops:
  7.2 114.3 %all-gather.2.cloned.1.call-start = ((), (), s32[]{:S(2)}) async-start(), calls=%async_computation.2 | async-start | bytes 8912896 | tf_op jit(solution)/shard_map/all_gather | solution.py:25
  121.4 5.9 %copy-start.4 = (bf16[2048,2048]{1,0:T(8,128)(2,1)S(1)}, bf16[2048,2048]{1,0:T(8,128)(2,1)}, u32[]{:S(2)}) copy-start(bf16[2048,2048]{1,0:T(8,128)(2,1)} %all-gather.2.cloned.1.call-done) | copy-start | bytes 25165828
  127.3 3.8 copy-start.3
  127.3 3.9 copy-start.5
  144.1 4.3 copy-start.2
  148.4 21.9 %all-to-all-start = ((bf16[16,2,32,128]{3,1,2,0:T(2,128)(2,1)}), bf16[16,2,32,128]{3,1,2,0:T(2,128)(2,1)S(1)}, u32[]{:S(2)}, u32[]{:S(2)}) async-start(bf16[16,2,32,128]{3,1,2,0:T(2,128)(2,1)} %convolution_convert_fusion), calls=%async_computation | async-start | bytes 524288 | tf_op jit(solution)/shard_map/all_to_all | solution.py:81
  157.2 343.6 %all-reduce.2.cloned.1.call-start = ((), (), s32[]{:S(2)}) async-start(), calls=%async_computation.3 | async-start | bytes 2097152 | tf_op jit(solution)/shard_map/psum | solution.py:90
  162.9 198.5 %copy-start.1 = (bf16[128,2048]{1,0:T(8,128)(2,1)}, bf16[128,2048]{1,0:T(8,128)(2,1)S(1)}, u32[]{:S(2)}) copy-start(bf16[128,2048]{1,0:T(8,128)(2,1)S(1)} %fusion.2) | copy-start | bytes 1572868
  168.7 332.0 %copy-start = (bf16[128,2048]{1,0:T(8,128)(2,1)S(1)}, bf16[128,2048]{1,0:T(8,128)(2,1)}, u32[]{:S(2)}) copy-start(bf16[128,2048]{1,0:T(8,128)(2,1)} %param.9) | copy-start | bytes 1572868
Sparse Core Ops, SparseCore 0:
  10.1 111.2 all-gather.1
  363.3 137.3 all-reduce.1
where the time goes:
time: 512 us
  blocking collectives  260 us (51%)
  waiting for transfers between devices  178 us (35%)
  matrix products  34.3 us (7%)
  between operations  14.2 us (3%)
  local copies, waits for them, and re-layouts  9.18 us (2%)
  starting transfers between devices  8.85 us (2%)
  other arithmetic  6.92 us (1%)
    all_to_all x1, blocking collectives, body(): lax.all_to_all(send_resid, 'group', split_axis=0, concat_axis=0, tiled=True)  191 us
    all_gather x1, waiting for transfers between devices, body(): whole = lax.all_gather(dictionary, 'group', axis=0, tiled=True)  108 us
    psum x1, blocking collectives, body(): full_stats, full_usage = lax.psum((stats, usage), 'dp')  69.3 us
    psum x1, waiting for transfers between devices, body(): full_stats, full_usage = lax.psum((stats, usage), 'dp')  67.7 us
    dot_general x3, matrix products, resid_of(): rebuilt = jnp.dot(matrix, whole, preferred_element_type=jnp.float32)  17 us
    dot_general x2, matrix products, body(): lax.dot_general(residual_rows, whole, (((1,), (1,)), ((), ())), preferred...  11 us
  transfers between devices with their start and end apart: 3, of which 3 were waited for; matrix products, arithmetic and copies ran while one was open for 3% of the time, Pallas kernels for 0%

commit v1 on v0

v1 whole, which is shorter than its diff:
```python
import functools

import jax
import jax.numpy as jnp
from jax import lax
from jax.experimental import pallas as pl
from jax.experimental.pallas import tpu as pltpu
from jax.sharding import PartitionSpec as P

ITERS = 2
F32 = jnp.float32
BF16 = jnp.bfloat16
NT = (((1,), (1,)), ((), ()))
VMEM_LIMIT = 56 * 1024 * 1024
MAIN = 64
MSG = 80


def refine_kernel(
    blocks, chunk, shards_ref, core_ref, x_ref, codes_ref, sup_ref, mine_ref, other_ref,
    codes_out, resid_out, msg_ref, usage_ref, rebuilt_scr,
):
    rows, plen = x_ref.shape
    half = plen // 2
    blk = rows // blocks
    slots = codes_ref.shape[1]
    chunks = half // chunk
    lane = lax.broadcasted_iota(jnp.int32, (blk, 256), 1)
    slot_lane = lax.broadcasted_iota(jnp.int32, (blk, slots), 1)
    usage_ref[...] = jnp.zeros_like(usage_ref)
    side = jnp.zeros((rows, 128), F32)
    side_parts = []
    my_off = core_ref[0] * half
    for b in range(blocks):
        r0 = b * blk
        sup = sup_ref[r0 : r0 + blk, :]
        row_a = pl.multiple_of(shards_ref[b, 0] * 128, 128)
        row_b = pl.multiple_of(shards_ref[b, 1] * 128, 128)
        hits = [sup[:, k : k + 1] == lane for k in range(slots)]

        def code_matrix(values):
            summed = jnp.zeros((blk, 256), F32)
            for k in range(slots):
                summed = summed + jnp.where(hits[k], values[:, k : k + 1], 0.0)
            return summed.astype(BF16)

        def pick(matrix):
            out = jnp.zeros((blk, slots), F32)
            for k in range(slots):
                col = jnp.sum(jnp.where(hits[k], matrix, 0.0), axis=1, keepdims=True)
                out = jnp.where(slot_lane == k, col, out)
            return out

        def atoms(ref, c0):
            return jnp.concatenate(
                [ref[pl.ds(row_a, 128), c0 : c0 + chunk], ref[pl.ds(row_b, 128), c0 : c0 + chunk]],
                axis=0,
            )

        def resid_chunk(matrix, ref, off, c0):
            d = atoms(ref, c0)
            rebuilt = jnp.dot(matrix, d, preferred_element_type=F32)
            at = pl.multiple_of(off + c0, 128)
            x = x_ref[r0 : r0 + blk, pl.ds(at, chunk)].astype(F32)
            return d, at, (x - rebuilt).astype(BF16)

        current = codes_ref[r0 : r0 + blk, :]
        for _ in range(ITERS):
            matrix = code_matrix(current)
            scores = jnp.zeros((blk, 256), F32)
            for ref, off in ((mine_ref, my_off), (other_ref, half - my_off)):
                for j in range(chunks):
                    d, _at, r = resid_chunk(matrix, ref, off, j * chunk)
                    scores = scores + lax.dot_general(r, d, NT, preferred_element_type=F32)
            current = current + 1.5 * (pick(scores) / plen)
        codes_out[r0 : r0 + blk, :] = current
        matrix = code_matrix(current)
        for ref, off in ((mine_ref, my_off), (other_ref, half - my_off)):
            for j in range(chunks):
                _d, at, r = resid_chunk(matrix, ref, off, j * chunk)
                resid_out[r0 : r0 + blk, pl.ds(at, chunk)] = r
        wide = matrix.astype(F32)
        squares = jnp.sum(wide * wide, axis=0, keepdims=True)
        usage_ref[pl.ds(shards_ref[b, 0], 1), :] += squares[:, :128]
        usage_ref[pl.ds(shards_ref[b, 1], 1), :] += squares[:, 128:]
        side_parts.append(
            jnp.concatenate(
                [pick(wide), sup.astype(F32), jnp.zeros((blk, 128 - 2 * slots), F32)], axis=1
            )
        )
    side = jnp.concatenate(side_parts, axis=0)
    side_t = jnp.transpose(side)[: 2 * slots, :].astype(BF16)
    low = lax.broadcasted_iota(jnp.int32, (MAIN, 128), 1) < 64
    for t in range(plen // 128):
        top = resid_out[:MAIN, t * 128 : (t + 1) * 128].astype(F32)
        bottom = resid_out[MAIN:, t * 128 : (t + 1) * 128].astype(F32)
        even = jnp.where(low, top, pltpu.roll(bottom, 64, 1))
        odd = jnp.where(low, pltpu.roll(top, 64, 1), bottom)
        msg_ref[2 * t, :MAIN, :] = even.astype(BF16)
        msg_ref[2 * t + 1, :MAIN, :] = odd.astype(BF16)
        msg_ref[2 * t, MAIN:, :] = side_t
        msg_ref[2 * t + 1, MAIN:, :] = side_t


def stats_kernel(sources, shards_ref, msg_ref, usage_ref, out_ref, acc_ref):
    groups = out_ref.shape[0]
    acc_ref[...] = jnp.zeros_like(acc_ref)
    atom = lax.broadcasted_iota(jnp.int32, (256, 128), 0)
    low = lax.broadcasted_iota(jnp.int32, (32, 128), 1) < 64
    low_all = lax.broadcasted_iota(jnp.int32, (128, 128), 1) < 64

    def one(q, carry):
        weights = msg_ref[q, MAIN : MAIN + 8, :].astype(F32)
        places = msg_ref[q, MAIN + 8 : MAIN + 16, :].astype(F32).astype(jnp.int32)
        matrix = jnp.zeros((256, 128), F32)
        for k in range(8):
            matrix = jnp.where(places[k : k + 1, :] == atom, weights[k : k + 1, :], matrix)
        matrix = matrix.astype(BF16)
        x0 = msg_ref[q, :32, :].astype(F32)
        x1 = msg_ref[q, 32:MAIN, :].astype(F32)
        none = jnp.zeros((32, 128), F32)
        for pair, x in ((0, x0), (1, x1)):
            first, second = jnp.where(low, x, 0.0), jnp.where(low, 0.0, x)
            parts = [none, none, none, none]
            parts[pair], parts[pair + 2] = first, second
            wide = jnp.concatenate(parts, axis=0).astype(BF16)
            out = jnp.dot(matrix, wide, preferred_element_type=F32)
            for h in range(2):
                piece = out[h * 128 : (h + 1) * 128, :]
                at0 = pl.multiple_of(shards_ref[q * 8 + pair * 2 + h] * 128, 128)
                at1 = pl.multiple_of(shards_ref[q * 8 + (pair + 2) * 2 + h] * 128, 128)
                acc_ref[pl.ds(at0, 128), :] += jnp.where(low_all, piece, 0.0)
                acc_ref[pl.ds(at1, 128), :] += jnp.where(low_all, 0.0, piece)
        return carry

    lax.fori_loop(0, sources, one, 0)
    low = lax.broadcasted_iota(jnp.int32, (MAIN, 128), 1) < 64
    row = lax.broadcasted_iota(jnp.int32, (16, 128), 0)
    for s in range(groups):
        full = acc_ref[s * 128 : (s + 1) * 128, :]
        full = full + pltpu.roll(full, 64, 1)
        out_ref[s, :MAIN, :] = jnp.where(low, full[:MAIN], full[MAIN:]).astype(BF16)
        used = usage_ref[s : s + 1, :]
        high = used.astype(BF16).astype(F32)
        rest = used - high
        out_ref[s, MAIN:, :] = jnp.where(
            row == 0, high, jnp.where(row == 1, rest, 0.0)
        ).astype(BF16)


def total_kernel(parts_ref, out_ref):
    total = parts_ref[0].astype(F32)
    for z in range(1, parts_ref.shape[0]):
        total = total + parts_ref[z].astype(F32)
    used = total[MAIN : MAIN + 1, :] + total[MAIN + 1 : MAIN + 2, :]
    high = used.astype(BF16).astype(F32)
    rest = used - high
    row = lax.broadcasted_iota(jnp.int32, (16, 128), 0)
    side = jnp.where(row == 0, high, jnp.where(row == 1, rest, 0.0))
    message = jnp.concatenate([total[:MAIN], side], axis=0).astype(BF16)
    for q in range(out_ref.shape[0]):
        out_ref[q] = message


def renew_kernel(parts_ref, dict_ref, out_ref, moved_ref):
    count = parts_ref.shape[0]
    plen = dict_ref.shape[1]
    used = jnp.zeros((16, 128), F32)
    for q in range(count):
        used = used + parts_ref[q, MAIN:, :].astype(F32)
    used = used[0:1, :] + used[1:2, :]
    column = jnp.transpose(jnp.broadcast_to(used, (128, 128)))
    gain = 3.0 / (column + 1.0)
    low = lax.broadcasted_iota(jnp.int32, (MAIN, 128), 1) < 64
    squares = jnp.zeros((128, 128), F32)
    for t in range(plen // 128):
        even = parts_ref[2 * t, :MAIN, :].astype(F32)
        odd = parts_ref[2 * t + 1, :MAIN, :].astype(F32)
        top = jnp.where(low, even, pltpu.roll(odd, 64, 1))
        bottom = jnp.where(low, pltpu.roll(even, 64, 1), odd)
        stats = jnp.concatenate([top, bottom], axis=0)
        moved = dict_ref[:, t * 128 : (t + 1) * 128].astype(F32) + gain * stats
        moved_ref[:, t * 128 : (t + 1) * 128] = moved
        squares = squares + moved * moved
    scale = lax.rsqrt(jnp.sum(squares, axis=1, keepdims=True) / plen + 1e-05)
    for t in range(plen // 128):
        out_ref[:, t * 128 : (t + 1) * 128] = (
            moved_ref[:, t * 128 : (t + 1) * 128] * scale
        ).astype(BF16)


def vmem():
    return pl.BlockSpec(memory_space=pltpu.VMEM)


def smem():
    return pl.BlockSpec(memory_space=pltpu.SMEM)


def call(kernel, ins, outs, scratch, *args):
    return pl.pallas_call(
        kernel,
        out_shape=outs,
        in_specs=ins,
        out_specs=jax.tree.map(lambda _: vmem(), outs),
        scratch_shapes=scratch,
        compiler_params=pltpu.CompilerParams(vmem_limit_bytes=VMEM_LIMIT),
    )(*args)


def body(patches, codes, support, block_shards, dictionary):
    rows, plen = patches.shape
    n_dp = lax.axis_size("dp")
    n_z = lax.axis_size("group")
    blocks = block_shards.shape[0]
    half = plen // 2
    core = lax.axis_index("dp") % 2
    part = lax.dynamic_slice(dictionary, (0, core * half), (dictionary.shape[0], half))
    mine = lax.all_gather(part, "group", axis=0, tiled=True)
    shards_all = lax.all_gather(block_shards.reshape(-1), "dp", axis=0, tiled=True)
    other = lax.ppermute(mine, "dp", [(i, i ^ 1) for i in range(n_dp)])
    sds = jax.ShapeDtypeStruct
    new_codes, resid, msg, usage = call(
        functools.partial(refine_kernel, blocks, min(256, half)),
        [smem(), smem(), vmem(), vmem(), vmem(), vmem(), vmem()],
        (
            sds(codes.shape, F32),
            sds(patches.shape, BF16),
            sds((n_dp, MSG, 128), BF16),
            sds((n_z, 128), F32),
        ),
        [pltpu.VMEM((8, 128), F32)],
        block_shards, core.reshape(1), patches, codes, support, mine, other,
    )
    got = lax.all_to_all(msg, "dp", split_axis=0, concat_axis=0, tiled=True)
    to_owner = call(
        functools.partial(stats_kernel, n_dp),
        [smem(), vmem(), vmem()],
        sds((n_z, MSG, 128), BF16),
        [pltpu.VMEM((n_z * 128, 128), F32)],
        shards_all, got, usage,
    )
    at_owner = lax.all_to_all(to_owner, "group", split_axis=0, concat_axis=0, tiled=True)
    spread = call(total_kernel, [vmem()], sds((n_dp, MSG, 128), BF16), [], at_owner)
    parts = lax.all_to_all(spread, "dp", split_axis=0, concat_axis=0, tiled=True)
    new_dictionary = call(
        renew_kernel,
        [vmem(), vmem()],
        sds(dictionary.shape, BF16),
        [pltpu.VMEM(dictionary.shape, F32)],
        parts, dictionary,
    )
    return (new_dictionary, new_codes, resid)


def solution(mesh):
    row = P(("dp", "group"), None)
    placed = (row, row, row, row, P("group", None))
    return jax.shard_map(
        body,
        mesh=mesh,
        in_specs=placed,
        out_specs=(P("group", None), row, row),
        check_vma=False,
    )
```

time: 512 us -> 214 us (0.42)
  blocking collectives: 260 us -> 37.3 us
  waiting for transfers between devices: 178 us -> 92.3 us
  matrix products: 34.3 us -> 0 us
  Pallas kernels: 0 us -> 28.3 us
  starting transfers between devices: 8.85 us -> 30.6 us
  other arithmetic: 6.92 us -> 0 us
    all_to_all x1, blocking collectives: 191 us -> 20.7 us  [body(): lax.all_to_all(to_owner, 'group', split_axis=0, concat_axis=0, tiled=True)]
    psum x1 -> x0, blocking collectives: 69.3 us -> none  [body(): full_stats, full_usage = lax.psum((stats, usage), 'dp')]
    psum x1 -> x0, waiting for transfers between devices: 67.7 us -> none  [body(): full_stats, full_usage = lax.psum((stats, usage), 'dp')]
    dot_general x8 -> x0, matrix products: 34.3 us -> none  [the longest x3 17 us: resid_of(): rebuilt = jnp.dot(matrix, whole, preferred_element_type=jnp.float32)]
    all_gather x1, waiting for transfers between devices: 108 us -> 77 us  [body(): mine = lax.all_gather(part, 'group', axis=0, tiled=True)]
    pallas_call x0 -> x4, Pallas kernels: none -> 28.3 us  [call(): pl.pallas_call(kernel, out_shape=outs, in_specs=ins, out_specs=jax.tree.m...]
    unnamed x0 -> x1, blocking collectives: none -> 16.6 us
    ppermute x0 -> x1, starting transfers between devices: none -> 11.4 us  [body(): other = lax.ppermute(mine, 'dp', [(i, i ^ 1) for i in range(n_dp)])]
  transfers between devices with their start and end apart: 3 -> 4, of which waited for: 3 -> 3; matrix products, arithmetic and copies ran while one was open for 3% -> 3% of each run, Pallas kernels for 0% -> 0%
where the time goes in v1:
time: 214 us; the launch traced here: 213 us
  waiting for transfers between devices  92.3 us (43%)
  blocking collectives  37.3 us (17%)
  starting transfers between devices  30.6 us (14%)
  Pallas kernels  28.3 us (13%)
  between operations  14.8 us (7%)
  local copies, waits for them, and re-layouts  9.8 us (5%)
    all_gather x1, waiting for transfers between devices, body(): mine = lax.all_gather(part, 'group', axis=0, tiled=True)  77 us
    pallas_call x4, Pallas kernels, call(): pl.pallas_call(kernel, out_shape=outs, in_specs=ins, out_specs=jax.tree.m...  28.3 us
    all_to_all x1, blocking collectives, body(): lax.all_to_all(to_owner, 'group', split_axis=0, concat_axis=0, tiled=True)  20.7 us
    unnamed x1, blocking collectives  16.6 us
    all_to_all x1, waiting for transfers between devices, body(): lax.all_to_all(spread, 'dp', split_axis=0, concat_axis=0, tiled=True)  12.3 us
    all_to_all x1, starting transfers between devices, body(): lax.all_to_all(spread, 'dp', split_axis=0, concat_axis=0, tiled=True)  11.8 us
    ppermute x1, starting transfers between devices, body(): other = lax.ppermute(mine, 'dp', [(i, i ^ 1) for i in range(n_dp)])  11.4 us
    unnamed x15, local copies, waits for them, and re-layouts  8.05 us
  transfers between devices with their start and end apart: 4, of which 3 were waited for; matrix products, arithmetic and copies ran while one was open for 3% of the time, Pallas kernels for 0%

profile of v1, /device:TPU:1, one launch (start us, length us, event | category | flops | bytes accessed | tf_op | source)
XLA Modules:
  0.0 213.1 jit_solution(12567764995798227392)
XLA Ops:
  7.2 0.0 all-gather.2.cloned.1.call-start
  7.2 1.7 constant_dynamic-slice_fusion
  8.9 0.0 all-gather.2.cloned.1.call-update
  8.9 77.0 %all-gather.2.cloned.1.call-done.mine_ref = bf16[2048,1024]{1,0:T(8,128)(2,1)} async-done(((bf16[128,1024]{1,0:T(8,128)(2,1)}), bf16[2048,1024]{1,0:T(8,128)(2,1)}) %all-gather.2.cloned.1.call-update) | async-done | bytes 4194320 | tf_op jit(solution)/shard_map/all_gather | solution.py:219
  85.9 11.4 %collective-permute-start = (bf16[2048,1024]{1,0:T(8,128)(2,1)}, bf16[2048,1024]{1,0:T(8,128)(2,1)}, u32[]{:S(2)}, u32[]{:S(2)}) collective-permute-start(bf16[2048,1024]{1,0:T(8,128)(2,1)} %all-gather.2.cloned.1.call-done.mine_ref), channel_id=1, source_target_pairs={{0,16},{16,0},{32,48},{48,32},{64,80},{80,64},{96,112},{112,96},{1... | collective-permute-start | bytes 12582920 | tf_op jit(solution)/shard_map/ppermute | solution.py:221
  97.4 1.3 copy.13.shards_ref
  98.7 1.4 copy.15.codes_ref
  100.1 1.4 copy.16.sup_ref
  101.5 2.9 %collective-permute-done.other_ref = bf16[2048,1024]{1,0:T(8,128)(2,1)} collective-permute-done((bf16[2048,1024]{1,0:T(8,128)(2,1)}, bf16[2048,1024]{1,0:T(8,128)(2,1)}, u32[]{:S(2)}, u32[]{:S(2)}) %collective-permute-start) | collective-permute-done | bytes 4194336 | tf_op jit(solution)/shard_map/ppermute | solution.py:221
  104.5 14.0 %shard_map.76 = (f32[128,8]{1,0:T(8,128)}, bf16[128,2048]{1,0:T(8,128)(2,1)}, bf16[32,80,128]{2,1,0:T(8,128)(2,1)}, f32[16,128]{1,0:T(8,128)}) custom-call(s32[4,2]{1,0:T(4,128)} %copy.13.shards_ref, s32[1]{0:T(128)} %bitcast.1.core_ref, bf16[128,2048]{1,0:T(8,128)(2,1)} %x_ref.1, f32[128,8]{1,0:T(8,128)} %copy.15.codes_ref, s32[128,8]{1,0:T(8,128)} %copy.16.sup_ref, ...), custom_call_target="tpu_custom_call" | custom-call | tf_op jit(solution)/shard_map/pallas_call | solution.py:201
  118.5 7.4 %all-to-all-start = ((bf16[32,80,128]{2,1,0:T(8,128)(2,1)}), bf16[32,80,128]{2,1,0:T(8,128)(2,1)S(1)}, u32[]{:S(2)}, u32[]{:S(2)}) async-start(bf16[32,80,128]{2,1,0:T(8,128)(2,1)} %get-tuple-element.7), calls=%async_computation | async-start | bytes 1310720 | tf_op jit(solution)/shard_map/all_to_all | solution.py:235
  125.9 0.1 reshape.14
  126.0 1.3 dynamic-slice
  127.9 0.2 dynamic-update-slice
  128.1 16.6 %all-reduce.shards_ref = s32[256]{0:T(256)} all-reduce(s32[256]{0:T(256)S(1)} %dynamic-update-slice), channel_id=1, replica_groups=mesh['dp'=32,'group'=16] {'dp'}, use_global_device_ids=true, to_apply=%add | all-reduce | flops 256 | bytes 2048
  144.7 0.8 copy-done
  145.6 9.8 %shard_map.77 = bf16[16,80,128]{2,1,0:T(8,128)(2,1)} custom-call(s32[256]{0:T(256)} %all-reduce.shards_ref, bf16[32,80,128]{2,1,0:T(8,128)(2,1)} %copy-done, f32[16,128]{1,0:T(8,128)} %get-tuple-element.8.usage_ref), custom_call_target="tpu_custom_call" | custom-call | tf_op jit(solution)/shard_map/pallas_call | solution.py:201
  155.4 20.7 %all_to_all.15.parts_ref = bf16[16,80,128]{2,1,0:T(8,128)(2,1)} all-to-all(bf16[16,80,128]{2,1,0:T(8,128)(2,1)} %shard_map.77), channel_id=1, replica_groups=mesh['dp'=32,'group'=16] {'group'}, dimensions={0} | all-to-all | bytes 655360 | tf_op jit(solution)/shard_map/all_to_all | solution.py:243
  176.1 1.9 shard_map.78
  178.0 11.8 %all-to-all-start.2 = ((bf16[32,80,128]{2,1,0:T(8,128)(2,1)}), bf16[32,80,128]{2,1,0:T(8,128)(2,1)S(1)}, u32[]{:S(2)}, u32[]{:S(2)}) async-start(bf16[32,80,128]{2,1,0:T(8,128)(2,1)} %shard_map.78), calls=%async_computation.2 | async-start | bytes 1310720 | tf_op jit(solution)/shard_map/all_to_all | solution.py:245
  189.8 0.7 copy.17
  190.4 12.3 %all-to-all-done.2.parts_ref = bf16[32,80,128]{2,1,0:T(8,128)(2,1)S(1)} async-done(((bf16[32,80,128]{2,1,0:T(8,128)(2,1)}), bf16[32,80,128]{2,1,0:T(8,128)(2,1)S(1)}, u32[]{:S(2)}, u32[]{:S(2)}) %all-to-all-start.2) | async-done | bytes 655392 | tf_op jit(solution)/shard_map/all_to_all | solution.py:245
  202.8 0.8 copy-done.1
  203.6 2.6 %shard_map.79 = bf16[128,2048]{1,0:T(8,128)(2,1)} custom-call(bf16[32,80,128]{2,1,0:T(8,128)(2,1)} %copy-done.1, bf16[128,2048]{1,0:T(8,128)(2,1)} %dict_ref.1), custom_call_target="tpu_custom_call" | custom-call | tf_op jit(solution)/shard_map/pallas_call | solution.py:201
  (8 shorter events, 0.0 us)
Async XLA Ops:
  7.2 78.7 %all-gather.2.cloned.1.call-start = ((), (), s32[]{:S(2)}) async-start(), calls=%async_computation.3 | async-start | bytes 4456448 | tf_op jit(solution)/shard_map/all_gather | solution.py:219
  85.9 18.6 %collective-permute-start = (bf16[2048,1024]{1,0:T(8,128)(2,1)}, bf16[2048,1024]{1,0:T(8,128)(2,1)}, u32[]{:S(2)}, u32[]{:S(2)}) collective-permute-start(bf16[2048,1024]{1,0:T(8,128)(2,1)} %all-gather.2.cloned.1.call-done.mine_ref), channel_id=1, source_target_pairs={{0,16},{16,0},{32,48},{48,32},{64,80},{80,64},{96,112},{112,96},{1... | collective-permute-start | bytes 12582920 | tf_op jit(solution)/shard_map/ppermute | solution.py:221
  104.5 21.4 %copy-start.3 = (s32[4,2]{1,0:T(4,128)S(1)}, s32[4,2]{1,0:T(4,128)}, u32[]{:S(2)}) copy-start(s32[4,2]{1,0:T(4,128)} %copy.13.shards_ref) | copy-start | bytes 100
  118.5 71.2 %copy-start.2 = (f32[128,8]{1,0:T(8,128)S(1)}, f32[128,8]{1,0:T(8,128)}, u32[]{:S(2)}) copy-start(f32[128,8]{1,0:T(8,128)} %get-tuple-element.15) | copy-start | bytes 12292
  118.5 26.2 %all-to-all-start = ((bf16[32,80,128]{2,1,0:T(8,128)(2,1)}), bf16[32,80,128]{2,1,0:T(8,128)(2,1)S(1)}, u32[]{:S(2)}, u32[]{:S(2)}) async-start(bf16[32,80,128]{2,1,0:T(8,128)(2,1)} %get-tuple-element.7), calls=%async_computation | async-start | bytes 1310720 | tf_op jit(solution)/shard_map/all_to_all | solution.py:235
  144.7 0.8 copy-start
  178.0 24.8 %all-to-all-start.2 = ((bf16[32,80,128]{2,1,0:T(8,128)(2,1)}), bf16[32,80,128]{2,1,0:T(8,128)(2,1)S(1)}, u32[]{:S(2)}, u32[]{:S(2)}) async-start(bf16[32,80,128]{2,1,0:T(8,128)(2,1)} %shard_map.78), calls=%async_computation.2 | async-start | bytes 1310720 | tf_op jit(solution)/shard_map/all_to_all | solution.py:245
  202.8 0.8 copy-start.1
Sparse Core Ops, SparseCore 0:
  10.7 75.2 all-gather.1

commit v2 on v0

v2 whole, which is shorter than its diff:
```python
import functools

import jax
import jax.numpy as jnp
from jax import lax
from jax.experimental import pallas as pl
from jax.experimental.pallas import tpu as pltpu
from jax.sharding import Mesh, PartitionSpec as P

F32 = jnp.float32
BF16 = jnp.bfloat16
NT = (((1,), (1,)), ((), ()))
VMEM_LIMIT = 56 * 1024 * 1024
DP_SPLIT = (4, 4, 2)
GROUP_SPLIT = (4, 4)
SHARD = 128
SLOTS = 8
MAIN = 64
MSG = 80


def pack_kernel(x_ref, codes_ref, sup_ref, names_ref, out_ref):
    rows = x_ref.shape[0]
    count, _height, width = out_ref.shape
    for j in range(count):
        out_ref[j, :rows, :] = x_ref[:, j * width : (j + 1) * width]
    side = jnp.concatenate(
        [codes_ref[...], sup_ref[...].astype(F32), jnp.zeros((rows, 128 - 2 * SLOTS), F32)], axis=1
    )
    side = jnp.transpose(side)
    codes, sup = side[:SLOTS], side[SLOTS : 2 * SLOTS]
    first = codes.astype(BF16)
    rest = codes - first.astype(F32)
    second = rest.astype(BF16)
    third = (rest - second.astype(F32)).astype(BF16)
    top = jnp.concatenate([first.astype(F32), second.astype(F32)], axis=0).astype(BF16)
    low = jnp.concatenate([third.astype(F32), sup], axis=0).astype(BF16)
    for j in range(count):
        out_ref[j, rows : rows + 16, :128] = top
        out_ref[j, rows : rows + 16, 128:256] = low
        out_ref[j, rows : rows + 16, 256:384] = names_ref[...].astype(BF16)
        for t in range(384, width, 128):
            out_ref[j, rows : rows + 16, t : t + 128] = jnp.zeros((16, 128), BF16)


def read_side(x_ref, src, rows):
    top = x_ref[src, rows : rows + 16, :128].astype(F32)
    low = x_ref[src, rows : rows + 16, 128:256].astype(F32)
    return top[:SLOTS] + top[SLOTS:] + low[:SLOTS], low[SLOTS:]


def to_rows(codes_t, sup_t):
    side = jnp.concatenate([codes_t, sup_t, jnp.zeros((128 - 2 * SLOTS, 128), F32)], axis=0)
    return jnp.transpose(side)


def atom_lanes(rows, core, piece):
    lane = lax.broadcasted_iota(jnp.int32, (rows, 256), 1)
    shift = piece.bit_length() - 1
    spot = lane & 127
    other = spot >> 6
    half = spot & 63
    place = ((half >> shift) * 2 + (core ^ other)) * piece + (half & (piece - 1))
    return ((lane & 128) + place).astype(F32)


def masks_of(side, lanes):
    return [side[:, SLOTS + k : SLOTS + k + 1] == lanes for k in range(SLOTS)]


def code_matrix(values, hits):
    summed = jnp.where(hits[0], values[:, 0:1], 0.0)
    for k in range(1, SLOTS):
        summed = summed + jnp.where(hits[k], values[:, k : k + 1], 0.0)
    return summed.astype(BF16)


def pick(matrix, hits, slot_lane):
    out = jnp.zeros(slot_lane.shape, F32)
    for k in range(SLOTS):
        col = jnp.sum(jnp.where(hits[k], matrix, 0.0), axis=1, keepdims=True)
        out = jnp.where(slot_lane == k, col, out)
    return out


def shard_row(shard, zh, zl):
    shift = zl.bit_length() - 1
    return (shard & (zl - 1)) * zh + (shard >> shift)


def refine_kernel(step, sizes, shards_ref, ids_ref, x_ref, mine_ref, other_ref, *refs):
    ny, zh, zl, plen = sizes
    count, height, width = x_ref.shape
    rows = height - 16
    piece = mine_ref.shape[2]
    blocks = rows // 32
    chunk = min(256, width)
    core = ids_ref[2]
    lanes = atom_lanes(rows, core, piece)
    slot_lane = lax.broadcasted_iota(jnp.int32, (rows, 128), 1)
    if step == 0:
        (grad_out,) = refs
    elif step == 1:
        parts_ref, grad_out, codes_out = refs
    else:
        parts_ref, codes_ref, home_out, msg_out, usage_out, codes_out = refs
        usage_out[...] = jnp.zeros_like(usage_out)
    if step > 0:
        moved = parts_ref[0]
        for j in range(1, count):
            moved = moved + parts_ref[j]
        moved = 1.5 * (moved / plen)
    low = lax.broadcasted_iota(jnp.int32, (MAIN, 128), 1) < 64
    for s in range(count):
        codes_t, sup_t = read_side(x_ref, s, rows)
        if step == 1:
            codes_t = codes_t + moved[:, s * 128 : (s + 1) * 128]
            codes_out[:, s * 128 : (s + 1) * 128] = codes_t
        if step == 2:
            codes_t = codes_ref[:, s * 128 : (s + 1) * 128] + moved[:, s * 128 : (s + 1) * 128]
            codes_out[s] = codes_t
        side = to_rows(codes_t, sup_t)
        hits = masks_of(side, lanes)
        matrix = code_matrix(side, hits)
        scores = []
        outs = [[] for _ in range(width // chunk)]
        for b in range(blocks):
            base = (ids_ref[0] * count + s) * 2 * blocks + 2 * b
            at_a = shard_row(shards_ref[base], zh, zl)
            at_b = shard_row(shards_ref[base + 1], zh, zl)
            part = matrix[b * 32 : (b + 1) * 32]
            total = None
            for j in range(width // chunk):
                c0 = j * chunk
                atoms = jnp.concatenate(
                    [
                        ref[:, at, :, c0 : c0 + chunk].reshape(ny * piece, chunk)
                        for at in (at_a, at_b)
                        for ref in (mine_ref, other_ref)
                    ],
                    axis=0,
                )
                rebuilt = jnp.dot(part, atoms, preferred_element_type=F32)
                x = x_ref[s, b * 32 : (b + 1) * 32, c0 : c0 + chunk].astype(F32)
                resid = (x - rebuilt).astype(BF16)
                if step < 2:
                    score = lax.dot_general(resid, atoms, NT, preferred_element_type=F32)
                    total = score if total is None else total + score
                else:
                    outs[j].append(resid)
            scores.append(total)
        if step < 2:
            grad = pick(jnp.concatenate(scores, axis=0), hits, slot_lane)
            grad_t = jnp.transpose(grad)[:SLOTS]
            for j in range(count):
                grad_out[j, :, s * 128 : (s + 1) * 128] = grad_t
            continue
        merged = pick(matrix.astype(F32), hits, slot_lane)
        merged_t = jnp.transpose(merged)[:SLOTS]
        side_t = jnp.concatenate([merged_t, sup_t], axis=0).astype(BF16)
        for j in range(width // chunk):
            full = jnp.concatenate(outs[j], axis=0)
            home_out[s, :, j * chunk : (j + 1) * chunk] = full
            for t in range(chunk // 128):
                u = (j * chunk) // 128 + t
                tile = full[:, t * 128 : (t + 1) * 128].astype(F32)
                top, bottom = tile[:MAIN], tile[MAIN:]
                even = jnp.where(low, top, pltpu.roll(bottom, 64, 1))
                odd = jnp.where(low, pltpu.roll(top, 64, 1), bottom)
                msg_out[2 * u, s, :MAIN, :] = even.astype(BF16)
                msg_out[2 * u + 1, s, :MAIN, :] = odd.astype(BF16)
                msg_out[2 * u, s, MAIN:, :] = side_t
                msg_out[2 * u + 1, s, MAIN:, :] = side_t

        @pl.when(ids_ref[1] == s)
        def _(side=side):
            plain = lax.broadcasted_iota(jnp.int32, (rows, 256), 1).astype(F32)
            wide = code_matrix(side, masks_of(side, plain)).astype(F32)
            wide = wide * wide
            for b in range(blocks):
                base = (ids_ref[0] * count + s) * 2 * blocks + 2 * b
                squares = jnp.sum(wide[b * 32 : (b + 1) * 32], axis=0, keepdims=True)
                usage_out[pl.ds(shards_ref[base], 1), :] += squares[:, :128]
                usage_out[pl.ds(shards_ref[base + 1], 1), :] += squares[:, 128:]


def stats_kernel(sizes, shards_ref, ids_ref, msg_ref, usage_ref, out_ref, acc_ref):
    ny, nx, zh, zl = sizes
    acc_ref[...] = jnp.zeros_like(acc_ref)
    atom = lax.broadcasted_iota(jnp.int32, (256, 128), 0).astype(F32)
    low = lax.broadcasted_iota(jnp.int32, (32, 128), 1) < 64
    low_all = lax.broadcasted_iota(jnp.int32, (128, 128), 1) < 64
    core = ids_ref[2]

    def one(q, carry):
        weights = msg_ref[q, MAIN : MAIN + 16, :].astype(F32)
        matrix = jnp.zeros((256, 128), F32)
        for k in range(SLOTS):
            matrix = jnp.where(
                weights[SLOTS + k : SLOTS + k + 1, :] == atom, weights[k : k + 1, :], matrix
            )
        matrix = matrix.astype(BF16)
        source = q // nx
        base = ((((source & 1) ^ core) * ny + (source >> 1)) * nx + q % nx) * 8
        none = jnp.zeros((32, 128), F32)
        for pair in range(2):
            x = msg_ref[q, pair * 32 : pair * 32 + 32, :].astype(F32)
            parts = [none, none, none, none]
            parts[pair], parts[pair + 2] = jnp.where(low, x, 0.0), jnp.where(low, 0.0, x)
            wide = jnp.concatenate(parts, axis=0).astype(BF16)
            out = jnp.dot(matrix, wide, preferred_element_type=F32)
            for h in range(2):
                values = out[h * 128 : (h + 1) * 128, :]
                at0 = pl.multiple_of(shards_ref[base + pair * 2 + h] * 128, 128)
                at1 = pl.multiple_of(shards_ref[base + pair * 2 + 4 + h] * 128, 128)
                acc_ref[pl.ds(at0, 128), :] += jnp.where(low_all, values, 0.0)
                acc_ref[pl.ds(at1, 128), :] += jnp.where(low_all, 0.0, values)
        return carry

    lax.fori_loop(0, msg_ref.shape[0], one, 0)
    low = lax.broadcasted_iota(jnp.int32, (MAIN, 128), 1) < 64
    row = lax.broadcasted_iota(jnp.int32, (16, 128), 0)
    for lo in range(zl):
        for hi in range(zh):
            s = hi * zl + lo
            full = acc_ref[s * 128 : (s + 1) * 128, :]
            full = full + pltpu.roll(full, 64, 1)
            out_ref[lo, hi, :MAIN, :] = jnp.where(low, full[:MAIN], full[MAIN:]).astype(BF16)
            out_ref[lo, hi, MAIN:, :] = two_parts(usage_ref[s : s + 1, :], row)


def two_parts(used, row):
    high = used.astype(BF16).astype(F32)
    return jnp.where(row == 0, high, jnp.where(row == 1, used - high, 0.0)).astype(BF16)


def summed(parts_ref, at):
    total = parts_ref[(0,) + at].astype(F32)
    for z in range(1, parts_ref.shape[0]):
        total = total + parts_ref[(z,) + at].astype(F32)
    return total


def partial_kernel(parts_ref, out_ref):
    row = lax.broadcasted_iota(jnp.int32, (16, 128), 0)
    for hi in range(out_ref.shape[0]):
        total = summed(parts_ref, (hi,))
        out_ref[hi, :MAIN, :] = total[:MAIN].astype(BF16)
        out_ref[hi, MAIN:, :] = two_parts(total[MAIN : MAIN + 1] + total[MAIN + 1 : MAIN + 2], row)


def total_kernel(parts_ref, out_ref):
    total = summed(parts_ref, ())
    row = lax.broadcasted_iota(jnp.int32, (16, 128), 0)
    main = total[:MAIN].astype(BF16)
    side = two_parts(total[MAIN : MAIN + 1] + total[MAIN + 1 : MAIN + 2], row)
    for q in range(out_ref.shape[0]):
        out_ref[q, :MAIN, :] = main
        out_ref[q, MAIN:, :] = side


def renew_kernel(sizes, parts_ref, dict_ref, out_ref, moved_ref):
    ny, nx = sizes
    plen = dict_ref.shape[1]
    used = jnp.zeros((16, 128), F32)
    for q in range(parts_ref.shape[0]):
        used = used + parts_ref[q, MAIN:, :].astype(F32)
    column = jnp.transpose(jnp.broadcast_to(used[0:1, :] + used[1:2, :], (128, 128)))
    gain = 3.0 / (column + 1.0)
    low = lax.broadcasted_iota(jnp.int32, (MAIN, 128), 1) < 64
    squares = jnp.zeros((128, 128), F32)
    for t in range(plen // 128):
        q = ((t % ny) * nx + t // ny) * 2
        even = parts_ref[q, :MAIN, :].astype(F32)
        odd = parts_ref[q + 1, :MAIN, :].astype(F32)
        top = jnp.where(low, even, pltpu.roll(odd, 64, 1))
        bottom = jnp.where(low, pltpu.roll(even, 64, 1), odd)
        stats = jnp.concatenate([top, bottom], axis=0)
        moved = dict_ref[:, t * 128 : (t + 1) * 128].astype(F32) + gain * stats
        moved_ref[:, t * 128 : (t + 1) * 128] = moved
        squares = squares + moved * moved
    scale = lax.rsqrt(jnp.sum(squares, axis=1, keepdims=True) / plen + 1e-05)
    for t in range(plen // 128):
        out_ref[:, t * 128 : (t + 1) * 128] = (
            moved_ref[:, t * 128 : (t + 1) * 128] * scale
        ).astype(BF16)


def call(kernel, ins, outs, scratch, *args, us=1):
    spaces = {"v": pltpu.VMEM, "s": pltpu.SMEM}
    return pl.pallas_call(
        kernel,
        out_shape=outs,
        in_specs=[pl.BlockSpec(memory_space=spaces[i]) for i in ins],
        out_specs=jax.tree.map(lambda _: pl.BlockSpec(memory_space=pltpu.VMEM), outs),
        scratch_shapes=scratch,
        cost_estimate=pl.CostEstimate(
            flops=us * 10**9, bytes_accessed=us * 3 * 10**6, transcendentals=0
        ),
        compiler_params=pltpu.CompilerParams(vmem_limit_bytes=VMEM_LIMIT),
    )(*args)


def exchange(x, axes):
    return lax.all_to_all(x, axes, split_axis=0, concat_axis=0, tiled=True)


def spread(x, axes, count):
    return exchange(jnp.broadcast_to(x[None], (count, *x.shape)), axes)


def body(ny, nx, zh, zl, patches, codes, support, block_shards, dictionary):
    rows, plen = patches.shape
    blocks = block_shards.shape[0]
    width = plen // nx
    nc = 2
    piece = SHARD // (ny * nc)
    sds = jax.ShapeDtypeStruct
    y, x, c = (lax.axis_index(a) for a in ("y", "x", "c"))
    ids = jnp.stack([y, x, c]).astype(jnp.int32)
    names = jnp.pad(block_shards.reshape(1, -1), ((0, 15), (0, 128 - 2 * blocks))).astype(F32)
    packed = call(
        pack_kernel,
        "vvvv",
        sds((nx, rows + 16, width), BF16),
        [],
        patches, codes, support, names,
    )
    held = exchange(packed, "x")
    names = held[:, rows, 256 : 256 + 2 * blocks].reshape(1, -1)
    own = lax.dynamic_slice(dictionary, ((y * nc + c) * piece, x * width), (piece, width))
    by_hi = spread(own, "zh", zh)
    by_z = spread(by_hi, "zl", zl).reshape(zh * zl, piece, width)
    extra = jnp.pad(names, ((0, piece - 1), (0, width - names.shape[1])))
    mine = spread(jnp.concatenate([by_z, extra[None]], axis=0), "y", ny)
    other = lax.ppermute(mine, "c", [(0, 1), (1, 0)])
    cut = 2 * blocks * nx
    shards = jnp.concatenate([mine[:, zh * zl, 0, :cut], other[:, zh * zl, 0, :cut]], axis=0)
    shards = shards.astype(jnp.int32).reshape(-1)
    common = (shards, ids, held, mine, other)
    grads = sds((nx, SLOTS, nx * rows), F32)
    first = call(
        lambda *r: refine_kernel(0, (ny, zh, zl, plen), *r), "ssvvv", grads, [], *common
    )
    second, codes_1 = call(
        lambda *r: refine_kernel(1, (ny, zh, zl, plen), *r),
        "ssvvvv",
        (grads, sds((SLOTS, nx * rows), F32)),
        [],
        *common,
        exchange(first, "x"),
    )
    home, msg, usage, codes_2 = call(
        lambda *r: refine_kernel(2, (ny, zh, zl, plen), *r),
        "ssvvvvv",
        (
            sds((nx, rows, width), BF16),
            sds((ny * nc, nx, MSG, 128), BF16),
            sds((zh * zl, 128), F32),
            sds((nx, SLOTS, rows), F32),
        ),
        [],
        *common,
        exchange(second, "x"),
        codes_1,
    )
    new_codes = jnp.transpose(lax.dynamic_index_in_dim(codes_2, x, 0, keepdims=False))
    got = exchange(msg, ("y", "c")).reshape(ny * nc * nx, MSG, 128)
    resid = jnp.transpose(exchange(home, "x"), (1, 0, 2)).reshape(rows, plen)
    to_owner = call(
        lambda *r: stats_kernel((ny, nx, zh, zl), *r),
        "ssvv",
        sds((zl, zh, MSG, 128), BF16),
        [pltpu.VMEM((zh * zl * SHARD, 128), F32)],
        shards, ids, got, usage, us=10,
    )
    nearer = call(partial_kernel, "v", sds((zh, MSG, 128), BF16), [], exchange(to_owner, "zl"))
    final = call(
        total_kernel, "v", sds((ny * nx * nc, MSG, 128), BF16), [], exchange(nearer, "zh")
    )
    new_dictionary = call(
        lambda *r: renew_kernel((ny, nx), *r),
        "vv",
        sds(dictionary.shape, BF16),
        [pltpu.VMEM(dictionary.shape, F32)],
        exchange(final, ("y", "x", "c")), dictionary,
    )
    return (new_dictionary, new_codes, resid)


def solution(mesh):
    fine = Mesh(mesh.devices.reshape(DP_SPLIT + GROUP_SPLIT), ("y", "x", "c", "zh", "zl"))
    row = P(("y", "x", "c", "zh", "zl"), None)
    shard = P(("zh", "zl"), None)
    return jax.shard_map(
        functools.partial(body, DP_SPLIT[0], DP_SPLIT[1], *GROUP_SPLIT),
        mesh=fine,
        in_specs=(row, row, row, row, shard),
        out_specs=(shard, row, row),
        check_vma=False,
    )
```

time: 512 us -> 212 us (0.41)
  blocking collectives: 260 us -> 93.2 us
  waiting for transfers between devices: 178 us -> 28.9 us
  Pallas kernels: 0 us -> 37.7 us
  matrix products: 34.3 us -> 0 us
  starting transfers between devices: 8.85 us -> 38.2 us
  between operations: 14.2 us -> 0.73 us
  other arithmetic: 6.92 us -> 1.28 us
    all_gather x1 -> x0, waiting for transfers between devices: 108 us -> none  [body(): whole = lax.all_gather(dictionary, 'group', axis=0, tiled=True)]
    all_to_all x1 -> x7, blocking collectives: 191 us -> 93.2 us  [exchange(): return lax.all_to_all(x, axes, split_axis=0, concat_axis=0, tiled=True)]
    psum x1 -> x0, blocking collectives: 69.3 us -> none  [body(): full_stats, full_usage = lax.psum((stats, usage), 'dp')]
    psum x1 -> x0, waiting for transfers between devices: 67.7 us -> none  [body(): full_stats, full_usage = lax.psum((stats, usage), 'dp')]
    pallas_call x0 -> x8, Pallas kernels: none -> 37.7 us  [call(): pl.pallas_call(kernel, out_shape=outs, in_specs=[pl.BlockSpec(memory_spac...]
    dot_general x8 -> x0, matrix products: 34.3 us -> none  [the longest x3 17 us: resid_of(): rebuilt = jnp.dot(matrix, whole, preferred_element_type=jnp.float32)]
    all_to_all x1 -> x4, waiting for transfers between devices: 1.58 us -> 27.2 us  [exchange(): return lax.all_to_all(x, axes, split_axis=0, concat_axis=0, tiled=True)]
    all_to_all x1 -> x4, starting transfers between devices: 8.77 us -> 31 us  [exchange(): return lax.all_to_all(x, axes, split_axis=0, concat_axis=0, tiled=True)]
  transfers between devices with their start and end apart: 3 -> 5, of which waited for: 3 -> 5; matrix products, arithmetic and copies ran while one was open for 3% -> 4% of each run, Pallas kernels for 0% -> 2%
where the time goes in v2:
time: 212 us; the launch traced here: 210 us
  blocking collectives  93.2 us (44%)
  starting transfers between devices  38.2 us (18%)
  Pallas kernels  37.7 us (18%)
  waiting for transfers between devices  28.9 us (14%)
  local copies, waits for them, and re-layouts  10.5 us (5%)
    all_to_all x7, blocking collectives, exchange(): return lax.all_to_all(x, axes, split_axis=0, concat_axis=0, tiled=True)  93.2 us
    pallas_call x8, Pallas kernels, call(): pl.pallas_call(kernel, out_shape=outs, in_specs=[pl.BlockSpec(memory_spac...  37.7 us
    all_to_all x4, starting transfers between devices, exchange(): return lax.all_to_all(x, axes, split_axis=0, concat_axis=0, tiled=True)  31 us
    all_to_all x4, waiting for transfers between devices, exchange(): return lax.all_to_all(x, axes, split_axis=0, concat_axis=0, tiled=True)  27.2 us
    ppermute x1, starting transfers between devices, body(): other = lax.ppermute(mine, 'c', [(0, 1), (1, 0)])  7.17 us
    unnamed x14, local copies, waits for them, and re-layouts  5.69 us
  transfers between devices with their start and end apart: 5, of which 5 were waited for; matrix products, arithmetic and copies ran while one was open for 4% of the time, Pallas kernels for 2%

profile of v2, /device:TPU:1, one launch (start us, length us, event | category | flops | bytes accessed | tf_op | source)
XLA Modules:
  0.0 210.5 jit_solution(717040206692087111)
XLA Ops:
  2.0 15.6 %all-to-all-start = ((bf16[4,16,512]{2,1,0:T(8,128)(2,1)}), bf16[4,16,512]{2,1,0:T(8,128)(2,1)S(1)}, u32[]{:S(2)}, u32[]{:S(2)}) async-start(bf16[4,16,512]{2,1,0:T(8,128)(2,1)} %broadcast_in_dim.8), calls=%async_computation | async-start | bytes 131072 | tf_op jit(solution)/shard_map/all_to_all | solution.py:305
  21.9 2.1 shard_map.76
  24.0 6.2 %all-to-all-done = bf16[4,16,512]{2,1,0:T(8,128)(2,1)S(1)} async-done(((bf16[4,16,512]{2,1,0:T(8,128)(2,1)}), bf16[4,16,512]{2,1,0:T(8,128)(2,1)S(1)}, u32[]{:S(2)}, u32[]{:S(2)}) %all-to-all-start) | async-done | bytes 65568 | tf_op jit(solution)/shard_map/all_to_all | solution.py:305
  30.1 12.2 %all_to_all.55.r_2_ = bf16[4,144,512]{2,1,0:T(8,128)(2,1)S(1)} all-to-all(bf16[4,144,512]{2,1,0:T(8,128)(2,1)} %shard_map.76), channel_id=1, replica_groups=mesh['y'=4,'x'=4,'c'=2,'zh'=4,'zl'=4] {'x'}, dimensions={0} | all-to-all | bytes 1179648 | tf_op jit(solution)/shard_map/all_to_all | solution.py:305
  43.1 3.4 %all-to-all-start.1 = ((bf16[4,4,16,512]{3,2,1,0:T(8,128)(2,1)}), bf16[4,4,16,512]{3,2,1,0:T(8,128)(2,1)S(1)}, u32[]{:S(2)}, u32[]{:S(2)}) async-start(bf16[4,4,16,512]{3,2,1,0:T(8,128)(2,1)} %broadcast_in_dim.9), calls=%async_computation.1 | async-start | bytes 524288 | tf_op jit(solution)/shard_map/all_to_all | solution.py:305
  46.7 5.5 %all-to-all-done.1 = bf16[4,4,16,512]{3,2,1,0:T(8,128)(2,1)S(1)} async-done(((bf16[4,4,16,512]{3,2,1,0:T(8,128)(2,1)}), bf16[4,4,16,512]{3,2,1,0:T(8,128)(2,1)S(1)}, u32[]{:S(2)}, u32[]{:S(2)}) %all-to-all-start.1) | async-done | bytes 262176 | tf_op jit(solution)/shard_map/all_to_all | solution.py:305
  52.3 15.5 %all_to_all.56.r_3_ = bf16[4,17,16,512]{3,2,1,0:T(8,128)(2,1)S(1)} all-to-all(bf16[4,17,16,512]{3,2,1,0:T(8,128)(2,1)S(1)} %broadcast_in_dim.11), channel_id=1, replica_groups=mesh['y'=4,'x'=4,'c'=2,'zh'=4,'zl'=4] {'y'}, dimensions={0} | all-to-all | bytes 2228224 | tf_op jit(solution)/shard_map/all_to_all | solution.py:305
  67.8 7.2 %collective-permute-start = (bf16[4,17,16,512]{3,2,1,0:T(8,128)(2,1)S(1)}, bf16[4,17,16,512]{3,2,1,0:T(8,128)(2,1)S(1)}, u32[]{:S(2)}, u32[]{:S(2)}) collective-permute-start(bf16[4,17,16,512]{3,2,1,0:T(8,128)(2,1)S(1)} %all_to_all.56.r_3_), channel_id=1, source_target_pairs={{0,16},{16,0},{1,17},{17,1},{2,18},{18,2},{3,19},{19,3},{4,20},{20... | collective-permute-start | bytes 3342344 | tf_op jit(solution)/shard_map/ppermute | solution.py:336
  75.6 1.7 collective-permute-done.r_4_
  78.3 6.8 %shard_map.77 = f32[4,8,512]{2,1,0:T(8,128)} custom-call(s32[256]{0:T(256)} %reshape.29.r_0_, s32[3]{0:T(128)} %pad_add_fusion.r_1_, bf16[4,144,512]{2,1,0:T(8,128)(2,1)} %copy-done.2, bf16[4,17,16,512]{3,2,1,0:T(8,128)(2,1)} %copy-done, bf16[4,17,16,512]{3,2,1,0:T(8,128)(2,1)} %copy-done.3), custom_call_target="tpu_custom_call" | custom-call | flops 1000000000 | bytes 3000000 | tf_op jit(solution)/shard_map/pallas_call | solution.py:291
  85.1 8.4 %all_to_all.57.r_5_ = f32[4,8,512]{2,1,0:T(8,128)} all-to-all(f32[4,8,512]{2,1,0:T(8,128)} %shard_map.77), channel_id=1, replica_groups=mesh['y'=4,'x'=4,'c'=2,'zh'=4,'zl'=4] {'x'}, dimensions={0} | all-to-all | bytes 131072 | tf_op jit(solution)/shard_map/all_to_all | solution.py:305
  93.6 6.6 %shard_map.78 = (f32[4,8,512]{2,1,0:T(8,128)}, f32[8,512]{1,0:T(8,128)}) custom-call(s32[256]{0:T(256)} %reshape.29.r_0_, s32[3]{0:T(128)} %pad_add_fusion.r_1_, bf16[4,144,512]{2,1,0:T(8,128)(2,1)} %copy-done.2, bf16[4,17,16,512]{3,2,1,0:T(8,128)(2,1)} %copy-done, bf16[4,17,16,512]{3,2,1,0:T(8,128)(2,1)} %copy-done.3, f32[4,8,512]{2,1,0:T(8,128)} %all_to_all.57.r_5_), custom_call_target="tpu_custom_call" | custom-call | flops 1000000000 | bytes 3000000 | tf_op jit(solution)/shard_map/pallas_call | solution.py:291
  100.2 8.4 %all_to_all.58.r_5_ = f32[4,8,512]{2,1,0:T(8,128)} all-to-all(f32[4,8,512]{2,1,0:T(8,128)} %get-tuple-element.9), channel_id=1, replica_groups=mesh['y'=4,'x'=4,'c'=2,'zh'=4,'zl'=4] {'x'}, dimensions={0} | all-to-all | bytes 131072 | tf_op jit(solution)/shard_map/all_to_all | solution.py:305
  108.6 6.4 %shard_map.79 = (bf16[4,128,512]{2,1,0:T(8,128)(2,1)}, bf16[8,4,80,128]{3,2,1,0:T(8,128)(2,1)}, f32[16,128]{1,0:T(8,128)}, f32[4,8,128]{2,1,0:T(8,128)}) custom-call(s32[256]{0:T(256)} %reshape.29.r_0_, s32[3]{0:T(128)} %pad_add_fusion.r_1_, bf16[4,144,512]{2,1,0:T(8,128)(2,1)} %copy-done.2, bf16[4,17,16,512]{3,2,1,0:T(8,128)(2,1)} %copy-done, ...), custom_call_target="tpu_custom_call" | custom-call | flops 1000000000 | bytes 3000000 | tf_op jit(solution)/shard_map/pallas_call | solution.py:291
  115.0 17.8 %all_to_all.59 = bf16[8,4,80,128]{3,2,1,0:T(8,128)(2,1)} all-to-all(bf16[8,4,80,128]{3,2,1,0:T(8,128)(2,1)} %get-tuple-element.11), channel_id=1, replica_groups=mesh['y'=4,'x'=4,'c'=2,'zh'=4,'zl'=4] {'y','c'}, dimensions={0} | all-to-all | bytes 1310720 | tf_op jit(solution)/shard_map/all_to_all | solution.py:305
  132.8 9.8 %shard_map.80 = bf16[4,4,80,128]{3,2,1,0:T(8,128)(2,1)} custom-call(s32[256]{0:T(256)} %reshape.29.r_0_, s32[3]{0:T(128)} %pad_add_fusion.r_1_, bf16[32,80,128]{2,1,0:T(8,128)(2,1)} %bitcast.22, f32[16,128]{1,0:T(8,128)} %get-tuple-element.12.r_3_), custom_call_target="tpu_custom_call" | custom-call | flops 10000000000 | bytes 30000000 | tf_op jit(solution)/shard_map/pallas_call | solution.py:291
  142.6 13.2 %all_to_all.60.parts_ref = bf16[4,4,80,128]{3,2,1,0:T(8,128)(2,1)} all-to-all(bf16[4,4,80,128]{3,2,1,0:T(8,128)(2,1)} %shard_map.80), channel_id=1, replica_groups=mesh['y'=4,'x'=4,'c'=2,'zh'=4,'zl'=4] {'zl'}, dimensions={0} | all-to-all | bytes 655360 | tf_op jit(solution)/shard_map/all_to_all | solution.py:305
  157.5 17.6 %all_to_all.61.parts_ref = bf16[4,80,128]{2,1,0:T(8,128)(2,1)} all-to-all(bf16[4,80,128]{2,1,0:T(8,128)(2,1)} %shard_map.81), channel_id=1, replica_groups=mesh['y'=4,'x'=4,'c'=2,'zh'=4,'zl'=4] {'zh'}, dimensions={0} | all-to-all | bytes 163840 | tf_op jit(solution)/shard_map/all_to_all | solution.py:305
  175.1 3.5 %all-to-all-start.10 = ((bf16[4,128,512]{2,1,0:T(8,128)(2,1)}), bf16[4,128,512]{2,1,0:T(8,128)(2,1)S(1)}, u32[]{:S(2)}, u32[]{:S(2)}) async-start(bf16[4,128,512]{2,1,0:T(8,128)(2,1)} %get-tuple-element.14), calls=%async_computation.10 | async-start | bytes 1048576 | tf_op jit(solution)/shard_map/all_to_all | solution.py:305
  178.6 1.8 shard_map.82
  180.4 5.1 %all-to-all-done.10 = bf16[4,128,512]{2,1,0:T(8,128)(2,1)S(1)} async-done(((bf16[4,128,512]{2,1,0:T(8,128)(2,1)}), bf16[4,128,512]{2,1,0:T(8,128)(2,1)S(1)}, u32[]{:S(2)}, u32[]{:S(2)}) %all-to-all-start.10) | async-done | bytes 524320 | tf_op jit(solution)/shard_map/all_to_all | solution.py:305
  185.5 8.5 %all-to-all-start.9 = ((bf16[32,80,128]{2,1,0:T(8,128)(2,1)}), bf16[32,80,128]{2,1,0:T(8,128)(2,1)S(1)}, u32[]{:S(2)}, u32[]{:S(2)}) async-start(bf16[32,80,128]{2,1,0:T(8,128)(2,1)} %shard_map.82), calls=%async_computation.9 | async-start | bytes 1310720 | tf_op jit(solution)/shard_map/all_to_all | solution.py:305
  196.6 10.5 %all-to-all-done.9.r_0_ = bf16[32,80,128]{2,1,0:T(8,128)(2,1)S(1)} async-done(((bf16[32,80,128]{2,1,0:T(8,128)(2,1)}), bf16[32,80,128]{2,1,0:T(8,128)(2,1)S(1)}, u32[]{:S(2)}, u32[]{:S(2)}) %all-to-all-start.9) | async-done | bytes 655392 | tf_op jit(solution)/shard_map/all_to_all | solution.py:305
  207.9 2.6 %shard_map.83 = bf16[128,2048]{1,0:T(8,128)(2,1)} custom-call(bf16[32,80,128]{2,1,0:T(8,128)(2,1)} %copy-done.1, bf16[128,2048]{1,0:T(8,128)(2,1)} %r_1_.1), custom_call_target="tpu_custom_call" | custom-call | flops 1000000000 | bytes 3000000 | tf_op jit(solution)/shard_map/pallas_call | solution.py:291
  (32 shorter events, 13.4 us)
Async XLA Ops:
  2.0 28.1 %all-to-all-start = ((bf16[4,16,512]{2,1,0:T(8,128)(2,1)}), bf16[4,16,512]{2,1,0:T(8,128)(2,1)S(1)}, u32[]{:S(2)}, u32[]{:S(2)}) async-start(bf16[4,16,512]{2,1,0:T(8,128)(2,1)} %broadcast_in_dim.8), calls=%async_computation | async-start | bytes 131072 | tf_op jit(solution)/shard_map/all_to_all | solution.py:305
  42.4 9.9 %copy-start.2 = (bf16[4,144,512]{2,1,0:T(8,128)(2,1)}, bf16[4,144,512]{2,1,0:T(8,128)(2,1)S(1)}, u32[]{:S(2)}) copy-start(bf16[4,144,512]{2,1,0:T(8,128)(2,1)S(1)} %all_to_all.55.r_2_) | copy-start | bytes 1769476
  43.1 9.0 %all-to-all-start.1 = ((bf16[4,4,16,512]{3,2,1,0:T(8,128)(2,1)}), bf16[4,4,16,512]{3,2,1,0:T(8,128)(2,1)S(1)}, u32[]{:S(2)}, u32[]{:S(2)}) async-start(bf16[4,4,16,512]{3,2,1,0:T(8,128)(2,1)} %broadcast_in_dim.9), calls=%async_computation.1 | async-start | bytes 524288 | tf_op jit(solution)/shard_map/all_to_all | solution.py:305
  67.8 10.3 %copy-start = (bf16[4,17,16,512]{3,2,1,0:T(8,128)(2,1)}, bf16[4,17,16,512]{3,2,1,0:T(8,128)(2,1)S(1)}, u32[]{:S(2)}) copy-start(bf16[4,17,16,512]{3,2,1,0:T(8,128)(2,1)S(1)} %all_to_all.56.r_3_) | copy-start | bytes 3342340
  67.8 9.5 %collective-permute-start = (bf16[4,17,16,512]{3,2,1,0:T(8,128)(2,1)S(1)}, bf16[4,17,16,512]{3,2,1,0:T(8,128)(2,1)S(1)}, u32[]{:S(2)}, u32[]{:S(2)}) collective-permute-start(bf16[4,17,16,512]{3,2,1,0:T(8,128)(2,1)S(1)} %all_to_all.56.r_3_), channel_id=1, source_target_pairs={{0,16},{16,0},{1,17},{17,1},{2,18},{18,2},{3,19},{19,3},{4,20},{20... | collective-permute-start | bytes 3342344 | tf_op jit(solution)/shard_map/ppermute | solution.py:336
  77.3 1.0 copy-start.3
  175.1 10.4 %all-to-all-start.10 = ((bf16[4,128,512]{2,1,0:T(8,128)(2,1)}), bf16[4,128,512]{2,1,0:T(8,128)(2,1)S(1)}, u32[]{:S(2)}, u32[]{:S(2)}) async-start(bf16[4,128,512]{2,1,0:T(8,128)(2,1)} %get-tuple-element.14), calls=%async_computation.10 | async-start | bytes 1048576 | tf_op jit(solution)/shard_map/all_to_all | solution.py:305
  185.5 21.5 %all-to-all-start.9 = ((bf16[32,80,128]{2,1,0:T(8,128)(2,1)}), bf16[32,80,128]{2,1,0:T(8,128)(2,1)S(1)}, u32[]{:S(2)}, u32[]{:S(2)}) async-start(bf16[32,80,128]{2,1,0:T(8,128)(2,1)} %shard_map.82), calls=%async_computation.9 | async-start | bytes 1310720 | tf_op jit(solution)/shard_map/all_to_all | solution.py:305
  207.0 0.8 copy-start.1

commit v3 on v2

--- a/solution.py
+++ b/solution.py
@@ -225,8 +225,8 @@
             s = hi * zl + lo
             full = acc_ref[s * 128 : (s + 1) * 128, :]
             full = full + pltpu.roll(full, 64, 1)
-            out_ref[lo, hi, :MAIN, :] = jnp.where(low, full[:MAIN], full[MAIN:]).astype(BF16)
-            out_ref[lo, hi, MAIN:, :] = two_parts(usage_ref[s : s + 1, :], row)
+            out_ref[s, :MAIN, :] = jnp.where(low, full[:MAIN], full[MAIN:]).astype(BF16)
+            out_ref[s, MAIN:, :] = two_parts(usage_ref[s : s + 1, :], row)
 
 
 def two_parts(used, row):
@@ -239,14 +239,6 @@
     for z in range(1, parts_ref.shape[0]):
         total = total + parts_ref[(z,) + at].astype(F32)
     return total
-
-
-def partial_kernel(parts_ref, out_ref):
-    row = lax.broadcasted_iota(jnp.int32, (16, 128), 0)
-    for hi in range(out_ref.shape[0]):
-        total = summed(parts_ref, (hi,))
-        out_ref[hi, :MAIN, :] = total[:MAIN].astype(BF16)
-        out_ref[hi, MAIN:, :] = two_parts(total[MAIN : MAIN + 1] + total[MAIN + 1 : MAIN + 2], row)
 
 
 def total_kernel(parts_ref, out_ref):
@@ -366,17 +358,22 @@
     )
     new_codes = jnp.transpose(lax.dynamic_index_in_dim(codes_2, x, 0, keepdims=False))
     got = exchange(msg, ("y", "c")).reshape(ny * nc * nx, MSG, 128)
-    resid = jnp.transpose(exchange(home, "x"), (1, 0, 2)).reshape(rows, plen)
+    at_home = exchange(home, "x")
     to_owner = call(
         lambda *r: stats_kernel((ny, nx, zh, zl), *r),
         "ssvv",
-        sds((zl, zh, MSG, 128), BF16),
+        sds((zh * zl, MSG, 128), BF16),
         [pltpu.VMEM((zh * zl * SHARD, 128), F32)],
         shards, ids, got, usage, us=10,
     )
-    nearer = call(partial_kernel, "v", sds((zh, MSG, 128), BF16), [], exchange(to_owner, "zl"))
+    to_owner, at_home = lax.optimization_barrier((to_owner, at_home))
+    resid = jnp.transpose(at_home, (1, 0, 2)).reshape(rows, plen)
     final = call(
-        total_kernel, "v", sds((ny * nx * nc, MSG, 128), BF16), [], exchange(nearer, "zh")
+        total_kernel,
+        "v",
+        sds((ny * nx * nc, MSG, 128), BF16),
+        [],
+        exchange(to_owner, ("zh", "zl")),
     )
     new_dictionary = call(
         lambda *r: renew_kernel((ny, nx), *r),

time: 212 us -> 199 us (0.939)
  blocking collectives: 93.2 us -> 83.1 us
  waiting for transfers between devices: 28.9 us -> 23.7 us
  starting transfers between devices: 38.2 us -> 41.9 us
    all_to_all x7 -> x6, blocking collectives: 93.2 us -> 83.1 us  [exchange(): return lax.all_to_all(x, axes, split_axis=0, concat_axis=0, tiled=True)]
    all_to_all x4, waiting for transfers between devices: 27.2 us -> 22 us  [exchange(): return lax.all_to_all(x, axes, split_axis=0, concat_axis=0, tiled=True)]
    all_to_all x4, starting transfers between devices: 31 us -> 34.7 us  [exchange(): return lax.all_to_all(x, axes, split_axis=0, concat_axis=0, tiled=True)]
    pallas_call x8 -> x7, Pallas kernels: 37.7 us -> 36.1 us  [call(): pl.pallas_call(kernel, out_shape=outs, in_specs=[pl.BlockSpec(memory_spac...]
  transfers between devices with their start and end apart: 5 -> 5, of which waited for: 5 -> 4; matrix products, arithmetic and copies ran while one was open for 4% -> 4% of each run, Pallas kernels for 2% -> 6%
where the time goes in v3:
time: 199 us; the launch traced here: 197 us
  blocking collectives  83.1 us (42%)
  starting transfers between devices  41.9 us (21%)
  Pallas kernels  36.1 us (18%)
  waiting for transfers between devices  23.7 us (12%)
  local copies, waits for them, and re-layouts  10.5 us (5%)
    all_to_all x6, blocking collectives, exchange(): return lax.all_to_all(x, axes, split_axis=0, concat_axis=0, tiled=True)  83.1 us
    pallas_call x7, Pallas kernels, call(): pl.pallas_call(kernel, out_shape=outs, in_specs=[pl.BlockSpec(memory_spac...  36.1 us
    all_to_all x4, starting transfers between devices, exchange(): return lax.all_to_all(x, axes, split_axis=0, concat_axis=0, tiled=True)  34.7 us
    all_to_all x4, waiting for transfers between devices, exchange(): return lax.all_to_all(x, axes, split_axis=0, concat_axis=0, tiled=True)  22 us
    ppermute x1, starting transfers between devices, body(): other = lax.ppermute(mine, 'c', [(0, 1), (1, 0)])  7.17 us
    unnamed x14, local copies, waits for them, and re-layouts  5.69 us
  transfers between devices with their start and end apart: 5, of which 4 were waited for; matrix products, arithmetic and copies ran while one was open for 4% of the time, Pallas kernels for 6%

profile of v3, /device:TPU:1, one launch (start us, length us, event | category | flops | bytes accessed | tf_op | source)
XLA Modules:
  0.0 197.3 jit_solution(15452879899874175957)
XLA Ops:
  2.0 15.6 %all-to-all-start = ((bf16[4,16,512]{2,1,0:T(8,128)(2,1)}), bf16[4,16,512]{2,1,0:T(8,128)(2,1)S(1)}, u32[]{:S(2)}, u32[]{:S(2)}) async-start(bf16[4,16,512]{2,1,0:T(8,128)(2,1)} %broadcast_in_dim.8), calls=%async_computation | async-start | bytes 131072 | tf_op jit(solution)/shard_map/all_to_all | solution.py:297
  18.5 1.4 copy.12.codes_ref
  19.9 1.4 copy.13.sup_ref
  21.9 2.1 %shard_map.76 = bf16[4,144,512]{2,1,0:T(8,128)(2,1)} custom-call(bf16[128,2048]{1,0:T(8,128)(2,1)} %x_ref.1, f32[128,8]{1,0:T(8,128)} %copy.12.codes_ref, s32[128,8]{1,0:T(8,128)} %copy.13.sup_ref, f32[16,128]{1,0:T(8,128)} %pad_convert_fusion.names_ref), custom_call_target="tpu_custom_call" | custom-call | flops 1000000000 | bytes 3000000 | tf_op jit(solution)/shard_map/pallas_call | solution.py:283
  24.0 6.2 %all-to-all-done = bf16[4,16,512]{2,1,0:T(8,128)(2,1)S(1)} async-done(((bf16[4,16,512]{2,1,0:T(8,128)(2,1)}), bf16[4,16,512]{2,1,0:T(8,128)(2,1)S(1)}, u32[]{:S(2)}, u32[]{:S(2)}) %all-to-all-start) | async-done | bytes 65568 | tf_op jit(solution)/shard_map/all_to_all | solution.py:297
  30.1 12.2 %all_to_all.50.r_2_ = bf16[4,144,512]{2,1,0:T(8,128)(2,1)S(1)} all-to-all(bf16[4,144,512]{2,1,0:T(8,128)(2,1)} %shard_map.76), channel_id=1, replica_groups=mesh['y'=4,'x'=4,'c'=2,'zh'=4,'zl'=4] {'x'}, dimensions={0} | all-to-all | bytes 1179648 | tf_op jit(solution)/shard_map/all_to_all | solution.py:297
  43.1 3.4 %all-to-all-start.1 = ((bf16[4,4,16,512]{3,2,1,0:T(8,128)(2,1)}), bf16[4,4,16,512]{3,2,1,0:T(8,128)(2,1)S(1)}, u32[]{:S(2)}, u32[]{:S(2)}) async-start(bf16[4,4,16,512]{3,2,1,0:T(8,128)(2,1)} %broadcast_in_dim.9), calls=%async_computation.1 | async-start | bytes 524288 | tf_op jit(solution)/shard_map/all_to_all | solution.py:297
  46.7 5.5 %all-to-all-done.1 = bf16[4,4,16,512]{3,2,1,0:T(8,128)(2,1)S(1)} async-done(((bf16[4,4,16,512]{3,2,1,0:T(8,128)(2,1)}), bf16[4,4,16,512]{3,2,1,0:T(8,128)(2,1)S(1)}, u32[]{:S(2)}, u32[]{:S(2)}) %all-to-all-start.1) | async-done | bytes 262176 | tf_op jit(solution)/shard_map/all_to_all | solution.py:297
  52.3 15.5 %all_to_all.51.r_3_ = bf16[4,17,16,512]{3,2,1,0:T(8,128)(2,1)S(1)} all-to-all(bf16[4,17,16,512]{3,2,1,0:T(8,128)(2,1)S(1)} %broadcast_in_dim.11), channel_id=1, replica_groups=mesh['y'=4,'x'=4,'c'=2,'zh'=4,'zl'=4] {'y'}, dimensions={0} | all-to-all | bytes 2228224 | tf_op jit(solution)/shard_map/all_to_all | solution.py:297
  67.8 7.2 %collective-permute-start = (bf16[4,17,16,512]{3,2,1,0:T(8,128)(2,1)S(1)}, bf16[4,17,16,512]{3,2,1,0:T(8,128)(2,1)S(1)}, u32[]{:S(2)}, u32[]{:S(2)}) collective-permute-start(bf16[4,17,16,512]{3,2,1,0:T(8,128)(2,1)S(1)} %all_to_all.51.r_3_), channel_id=1, source_target_pairs={{0,16},{16,0},{1,17},{17,1},{2,18},{18,2},{3,19},{19,3},{4,20},{20... | collective-permute-start | bytes 3342344 | tf_op jit(solution)/shard_map/ppermute | solution.py:328
  75.6 1.7 collective-permute-done.r_4_
  78.3 6.8 %shard_map.77 = f32[4,8,512]{2,1,0:T(8,128)} custom-call(s32[256]{0:T(256)} %reshape.29.r_0_, s32[3]{0:T(128)} %pad_add_fusion.r_1_, bf16[4,144,512]{2,1,0:T(8,128)(2,1)} %copy-done.2, bf16[4,17,16,512]{3,2,1,0:T(8,128)(2,1)} %copy-done, bf16[4,17,16,512]{3,2,1,0:T(8,128)(2,1)} %copy-done.3), custom_call_target="tpu_custom_call" | custom-call | flops 1000000000 | bytes 3000000 | tf_op jit(solution)/shard_map/pallas_call | solution.py:283
  85.1 8.4 %all_to_all.52.r_5_ = f32[4,8,512]{2,1,0:T(8,128)} all-to-all(f32[4,8,512]{2,1,0:T(8,128)} %shard_map.77), channel_id=1, replica_groups=mesh['y'=4,'x'=4,'c'=2,'zh'=4,'zl'=4] {'x'}, dimensions={0} | all-to-all | bytes 131072 | tf_op jit(solution)/shard_map/all_to_all | solution.py:297
  93.6 6.6 %shard_map.78 = (f32[4,8,512]{2,1,0:T(8,128)}, f32[8,512]{1,0:T(8,128)}) custom-call(s32[256]{0:T(256)} %reshape.29.r_0_, s32[3]{0:T(128)} %pad_add_fusion.r_1_, bf16[4,144,512]{2,1,0:T(8,128)(2,1)} %copy-done.2, bf16[4,17,16,512]{3,2,1,0:T(8,128)(2,1)} %copy-done, bf16[4,17,16,512]{3,2,1,0:T(8,128)(2,1)} %copy-done.3, f32[4,8,512]{2,1,0:T(8,128)} %all_to_all.52.r_5_), custom_call_target="tpu_custom_call" | custom-call | flops 1000000000 | bytes 3000000 | tf_op jit(solution)/shard_map/pallas_call | solution.py:283
  100.2 8.4 %all_to_all.53.r_5_ = f32[4,8,512]{2,1,0:T(8,128)} all-to-all(f32[4,8,512]{2,1,0:T(8,128)} %get-tuple-element.11), channel_id=1, replica_groups=mesh['y'=4,'x'=4,'c'=2,'zh'=4,'zl'=4] {'x'}, dimensions={0} | all-to-all | bytes 131072 | tf_op jit(solution)/shard_map/all_to_all | solution.py:297
  108.6 6.4 %shard_map.79 = (bf16[4,128,512]{2,1,0:T(8,128)(2,1)}, bf16[8,4,80,128]{3,2,1,0:T(8,128)(2,1)}, f32[16,128]{1,0:T(8,128)}, f32[4,8,128]{2,1,0:T(8,128)}) custom-call(s32[256]{0:T(256)} %reshape.29.r_0_, s32[3]{0:T(128)} %pad_add_fusion.r_1_, bf16[4,144,512]{2,1,0:T(8,128)(2,1)} %copy-done.2, bf16[4,17,16,512]{3,2,1,0:T(8,128)(2,1)} %copy-done, ...), custom_call_target="tpu_custom_call" | custom-call | flops 1000000000 | bytes 3000000 | tf_op jit(solution)/shard_map/pallas_call | solution.py:283
  115.0 17.8 %all_to_all.54 = bf16[8,4,80,128]{3,2,1,0:T(8,128)(2,1)} all-to-all(bf16[8,4,80,128]{3,2,1,0:T(8,128)(2,1)} %get-tuple-element.13), channel_id=1, replica_groups=mesh['y'=4,'x'=4,'c'=2,'zh'=4,'zl'=4] {'y','c'}, dimensions={0} | all-to-all | bytes 1310720 | tf_op jit(solution)/shard_map/all_to_all | solution.py:297
  132.8 3.5 %all-to-all-start.7 = ((bf16[4,128,512]{2,1,0:T(8,128)(2,1)}), bf16[4,128,512]{2,1,0:T(8,128)(2,1)S(1)}, u32[]{:S(2)}, u32[]{:S(2)}) async-start(bf16[4,128,512]{2,1,0:T(8,128)(2,1)} %get-tuple-element.15), calls=%async_computation.7 | async-start | bytes 1048576 | tf_op jit(solution)/shard_map/all_to_all | solution.py:297
  136.3 9.8 %shard_map.80 = bf16[16,80,128]{2,1,0:T(8,128)(2,1)} custom-call(s32[256]{0:T(256)} %reshape.29.r_0_, s32[3]{0:T(128)} %pad_add_fusion.r_1_, bf16[32,80,128]{2,1,0:T(8,128)(2,1)} %bitcast.22, f32[16,128]{1,0:T(8,128)} %get-tuple-element.14.r_3_), custom_call_target="tpu_custom_call" | custom-call | flops 10000000000 | bytes 30000000 | tf_op jit(solution)/shard_map/pallas_call | solution.py:283
  146.1 20.8 %all_to_all.55.parts_ref = bf16[16,80,128]{2,1,0:T(8,128)(2,1)} all-to-all(bf16[16,80,128]{2,1,0:T(8,128)(2,1)} %shard_map.80), channel_id=1, replica_groups=mesh['y'=4,'x'=4,'c'=2,'zh'=4,'zl'=4] {'zh','zl'}, dimensions={0} | all-to-all | bytes 655360 | tf_op jit(solution)/shard_map/all_to_all | solution.py:297
  166.9 1.9 shard_map.81
  168.7 12.2 %all-to-all-start.9 = ((bf16[32,80,128]{2,1,0:T(8,128)(2,1)}), bf16[32,80,128]{2,1,0:T(8,128)(2,1)S(1)}, u32[]{:S(2)}, u32[]{:S(2)}) async-start(bf16[32,80,128]{2,1,0:T(8,128)(2,1)} %shard_map.81), calls=%async_computation.9 | async-start | bytes 1310720 | tf_op jit(solution)/shard_map/all_to_all | solution.py:297
  183.5 10.3 %all-to-all-done.9.r_0_ = bf16[32,80,128]{2,1,0:T(8,128)(2,1)S(1)} async-done(((bf16[32,80,128]{2,1,0:T(8,128)(2,1)}), bf16[32,80,128]{2,1,0:T(8,128)(2,1)S(1)}, u32[]{:S(2)}, u32[]{:S(2)}) %all-to-all-start.9) | async-done | bytes 655392 | tf_op jit(solution)/shard_map/all_to_all | solution.py:297
  194.7 2.6 %shard_map.82 = bf16[128,2048]{1,0:T(8,128)(2,1)} custom-call(bf16[32,80,128]{2,1,0:T(8,128)(2,1)} %copy-done.1, bf16[128,2048]{1,0:T(8,128)(2,1)} %r_1_.1), custom_call_target="tpu_custom_call" | custom-call | flops 1000000000 | bytes 3000000 | tf_op jit(solution)/shard_map/pallas_call | solution.py:283
  (30 shorter events, 8.9 us)
Async XLA Ops:
  2.0 28.1 %all-to-all-start = ((bf16[4,16,512]{2,1,0:T(8,128)(2,1)}), bf16[4,16,512]{2,1,0:T(8,128)(2,1)S(1)}, u32[]{:S(2)}, u32[]{:S(2)}) async-start(bf16[4,16,512]{2,1,0:T(8,128)(2,1)} %broadcast_in_dim.8), calls=%async_computation | async-start | bytes 131072 | tf_op jit(solution)/shard_map/all_to_all | solution.py:297
  42.4 9.9 %copy-start.2 = (bf16[4,144,512]{2,1,0:T(8,128)(2,1)}, bf16[4,144,512]{2,1,0:T(8,128)(2,1)S(1)}, u32[]{:S(2)}) copy-start(bf16[4,144,512]{2,1,0:T(8,128)(2,1)S(1)} %all_to_all.50.r_2_) | copy-start | bytes 1769476
  43.1 9.0 %all-to-all-start.1 = ((bf16[4,4,16,512]{3,2,1,0:T(8,128)(2,1)}), bf16[4,4,16,512]{3,2,1,0:T(8,128)(2,1)S(1)}, u32[]{:S(2)}, u32[]{:S(2)}) async-start(bf16[4,4,16,512]{3,2,1,0:T(8,128)(2,1)} %broadcast_in_dim.9), calls=%async_computation.1 | async-start | bytes 524288 | tf_op jit(solution)/shard_map/all_to_all | solution.py:297
  67.8 10.3 %copy-start = (bf16[4,17,16,512]{3,2,1,0:T(8,128)(2,1)}, bf16[4,17,16,512]{3,2,1,0:T(8,128)(2,1)S(1)}, u32[]{:S(2)}) copy-start(bf16[4,17,16,512]{3,2,1,0:T(8,128)(2,1)S(1)} %all_to_all.51.r_3_) | copy-start | bytes 3342340
  67.8 9.5 %collective-permute-start = (bf16[4,17,16,512]{3,2,1,0:T(8,128)(2,1)S(1)}, bf16[4,17,16,512]{3,2,1,0:T(8,128)(2,1)S(1)}, u32[]{:S(2)}, u32[]{:S(2)}) collective-permute-start(bf16[4,17,16,512]{3,2,1,0:T(8,128)(2,1)S(1)} %all_to_all.51.r_3_), channel_id=1, source_target_pairs={{0,16},{16,0},{1,17},{17,1},{2,18},{18,2},{3,19},{19,3},{4,20},{20... | collective-permute-start | bytes 3342344 | tf_op jit(solution)/shard_map/ppermute | solution.py:328
  77.3 1.0 copy-start.3
  132.8 13.3 %all-to-all-start.7 = ((bf16[4,128,512]{2,1,0:T(8,128)(2,1)}), bf16[4,128,512]{2,1,0:T(8,128)(2,1)S(1)}, u32[]{:S(2)}, u32[]{:S(2)}) async-start(bf16[4,128,512]{2,1,0:T(8,128)(2,1)} %get-tuple-element.15), calls=%async_computation.7 | async-start | bytes 1048576 | tf_op jit(solution)/shard_map/all_to_all | solution.py:297
  168.7 25.1 %all-to-all-start.9 = ((bf16[32,80,128]{2,1,0:T(8,128)(2,1)}), bf16[32,80,128]{2,1,0:T(8,128)(2,1)S(1)}, u32[]{:S(2)}, u32[]{:S(2)}) async-start(bf16[32,80,128]{2,1,0:T(8,128)(2,1)} %shard_map.81), calls=%async_computation.9 | async-start | bytes 1310720 | tf_op jit(solution)/shard_map/all_to_all | solution.py:297
  193.9 0.8 copy-start.1

commit v4 on v3

--- a/solution.py
+++ b/solution.py
@@ -19,33 +19,36 @@
 MSG = 80
 
 
-def pack_kernel(x_ref, codes_ref, sup_ref, names_ref, out_ref):
+def pack_kernel(names_ref, ids_ref, x_ref, codes_ref, sup_ref, *outs):
     rows = x_ref.shape[0]
-    count, _height, width = out_ref.shape
+    width = outs[0].shape[1]
+    count = len(outs)
+    codes = codes_ref[...]
+    first = codes.astype(BF16).astype(F32)
+    rest = codes - first
+    second = rest.astype(BF16).astype(F32)
+    third = rest - second
+    top = jnp.concatenate([first, second], axis=0).astype(BF16)
+    low = jnp.concatenate([third, sup_ref[...].astype(F32)], axis=0).astype(BF16)
+    lane = lax.broadcasted_iota(jnp.int32, (16, 128), 1)
+    names = jnp.zeros((16, 128), jnp.int32)
+    for b in range(names_ref.shape[1]):
+        for h in range(2):
+            names = jnp.where(lane == 2 * b + h, names_ref[h, b], names)
+    names = names.astype(F32).astype(BF16)
     for j in range(count):
-        out_ref[j, :rows, :] = x_ref[:, j * width : (j + 1) * width]
-    side = jnp.concatenate(
-        [codes_ref[...], sup_ref[...].astype(F32), jnp.zeros((rows, 128 - 2 * SLOTS), F32)], axis=1
-    )
-    side = jnp.transpose(side)
-    codes, sup = side[:SLOTS], side[SLOTS : 2 * SLOTS]
-    first = codes.astype(BF16)
-    rest = codes - first.astype(F32)
-    second = rest.astype(BF16)
-    third = (rest - second.astype(F32)).astype(BF16)
-    top = jnp.concatenate([first.astype(F32), second.astype(F32)], axis=0).astype(BF16)
-    low = jnp.concatenate([third.astype(F32), sup], axis=0).astype(BF16)
-    for j in range(count):
-        out_ref[j, rows : rows + 16, :128] = top
-        out_ref[j, rows : rows + 16, 128:256] = low
-        out_ref[j, rows : rows + 16, 256:384] = names_ref[...].astype(BF16)
+        start = pl.multiple_of(((ids_ref[1] + j) & (count - 1)) * width, 128)
+        outs[j][:rows, :] = x_ref[:, pl.ds(start, width)]
+        outs[j][rows : rows + 16, :128] = top
+        outs[j][rows : rows + 16, 128:256] = low
+        outs[j][rows : rows + 16, 256:384] = names
         for t in range(384, width, 128):
-            out_ref[j, rows : rows + 16, t : t + 128] = jnp.zeros((16, 128), BF16)
-
-
-def read_side(x_ref, src, rows):
-    top = x_ref[src, rows : rows + 16, :128].astype(F32)
-    low = x_ref[src, rows : rows + 16, 128:256].astype(F32)
+            outs[j][rows : rows + 16, t : t + 128] = jnp.zeros((16, 128), BF16)
+
+
+def read_side(x_ref, rows):
+    top = x_ref[rows : rows + 16, :128].astype(F32)
+    low = x_ref[rows : rows + 16, 128:256].astype(F32)
     return top[:SLOTS] + top[SLOTS:] + low[:SLOTS], low[SLOTS:]
 
 
@@ -88,9 +91,10 @@
     return (shard & (zl - 1)) * zh + (shard >> shift)
 
 
-def refine_kernel(step, sizes, shards_ref, ids_ref, x_ref, mine_ref, other_ref, *refs):
-    ny, zh, zl, plen = sizes
-    count, height, width = x_ref.shape
+def refine_kernel(step, sizes, shards_ref, ids_ref, *refs):
+    ny, nx, zh, zl, plen = sizes
+    x_refs, (mine_ref, other_ref), refs = refs[:nx], refs[nx : nx + 2], refs[nx + 2 :]
+    height, width = x_refs[0].shape
     rows = height - 16
     piece = mine_ref.shape[2]
     blocks = rows // 32
@@ -104,28 +108,31 @@
         parts_ref, grad_out, codes_out = refs
     else:
         parts_ref, codes_ref, home_out, msg_out, usage_out, codes_out = refs
-        usage_out[...] = jnp.zeros_like(usage_out)
-    if step > 0:
-        moved = parts_ref[0]
-        for j in range(1, count):
-            moved = moved + parts_ref[j]
-        moved = 1.5 * (moved / plen)
     low = lax.broadcasted_iota(jnp.int32, (MAIN, 128), 1) < 64
-    for s in range(count):
-        codes_t, sup_t = read_side(x_ref, s, rows)
+    for s in range(nx):
+        source = (ids_ref[1] - s) & (nx - 1)
+        at = pl.ds(pl.multiple_of(source * 128, 128), 128)
+        mine = slice(s * 128, (s + 1) * 128)
+        codes_t, sup_t = read_side(x_refs[s], rows)
+        if step > 0:
+            moved = parts_ref[0, :, at]
+            for j in range(1, nx):
+                moved = moved + parts_ref[j, :, at]
+            moved = 1.5 * (moved / plen)
         if step == 1:
-            codes_t = codes_t + moved[:, s * 128 : (s + 1) * 128]
-            codes_out[:, s * 128 : (s + 1) * 128] = codes_t
+            codes_t = codes_t + moved
+            codes_out[:, mine] = codes_t
         if step == 2:
-            codes_t = codes_ref[:, s * 128 : (s + 1) * 128] + moved[:, s * 128 : (s + 1) * 128]
-            codes_out[s] = codes_t
+            codes_t = codes_ref[:, mine] + moved
+            if s == 0:
+                codes_out[...] = codes_t
         side = to_rows(codes_t, sup_t)
         hits = masks_of(side, lanes)
         matrix = code_matrix(side, hits)
         scores = []
         outs = [[] for _ in range(width // chunk)]
         for b in range(blocks):
-            base = (ids_ref[0] * count + s) * 2 * blocks + 2 * b
+            base = (ids_ref[0] * nx + s) * 2 * blocks + 2 * b
             at_a = shard_row(shards_ref[base], zh, zl)
             at_b = shard_row(shards_ref[base + 1], zh, zl)
             part = matrix[b * 32 : (b + 1) * 32]
@@ -134,14 +141,14 @@
                 c0 = j * chunk
                 atoms = jnp.concatenate(
                     [
-                        ref[:, at, :, c0 : c0 + chunk].reshape(ny * piece, chunk)
-                        for at in (at_a, at_b)
+                        ref[:, z, :, c0 : c0 + chunk].reshape(ny * piece, chunk)
+                        for z in (at_a, at_b)
                         for ref in (mine_ref, other_ref)
                     ],
                     axis=0,
                 )
                 rebuilt = jnp.dot(part, atoms, preferred_element_type=F32)
-                x = x_ref[s, b * 32 : (b + 1) * 32, c0 : c0 + chunk].astype(F32)
+                x = x_refs[s][b * 32 : (b + 1) * 32, c0 : c0 + chunk].astype(F32)
                 resid = (x - rebuilt).astype(BF16)
                 if step < 2:
                     score = lax.dot_general(resid, atoms, NT, preferred_element_type=F32)
@@ -152,33 +159,31 @@
         if step < 2:
             grad = pick(jnp.concatenate(scores, axis=0), hits, slot_lane)
             grad_t = jnp.transpose(grad)[:SLOTS]
-            for j in range(count):
-                grad_out[j, :, s * 128 : (s + 1) * 128] = grad_t
+            for j in range(nx):
+                grad_out[j, :, at] = grad_t
             continue
-        merged = pick(matrix.astype(F32), hits, slot_lane)
-        merged_t = jnp.transpose(merged)[:SLOTS]
+        merged_t = jnp.transpose(pick(matrix.astype(F32), hits, slot_lane))[:SLOTS]
         side_t = jnp.concatenate([merged_t, sup_t], axis=0).astype(BF16)
         for j in range(width // chunk):
             full = jnp.concatenate(outs[j], axis=0)
-            home_out[s, :, j * chunk : (j + 1) * chunk] = full
+            home_out[source, :, j * chunk : (j + 1) * chunk] = full
             for t in range(chunk // 128):
                 u = (j * chunk) // 128 + t
                 tile = full[:, t * 128 : (t + 1) * 128].astype(F32)
                 top, bottom = tile[:MAIN], tile[MAIN:]
                 even = jnp.where(low, top, pltpu.roll(bottom, 64, 1))
                 odd = jnp.where(low, pltpu.roll(top, 64, 1), bottom)
-                msg_out[2 * u, s, :MAIN, :] = even.astype(BF16)
-                msg_out[2 * u + 1, s, :MAIN, :] = odd.astype(BF16)
-                msg_out[2 * u, s, MAIN:, :] = side_t
-                msg_out[2 * u + 1, s, MAIN:, :] = side_t
-
-        @pl.when(ids_ref[1] == s)
-        def _(side=side):
+                msg_out[2 * u, source, :MAIN, :] = even.astype(BF16)
+                msg_out[2 * u + 1, source, :MAIN, :] = odd.astype(BF16)
+                msg_out[2 * u, source, MAIN:, :] = side_t
+                msg_out[2 * u + 1, source, MAIN:, :] = side_t
+        if s == 0:
+            usage_out[...] = jnp.zeros_like(usage_out)
             plain = lax.broadcasted_iota(jnp.int32, (rows, 256), 1).astype(F32)
             wide = code_matrix(side, masks_of(side, plain)).astype(F32)
             wide = wide * wide
             for b in range(blocks):
-                base = (ids_ref[0] * count + s) * 2 * blocks + 2 * b
+                base = (ids_ref[0] * nx + s) * 2 * blocks + 2 * b
                 squares = jnp.sum(wide[b * 32 : (b + 1) * 32], axis=0, keepdims=True)
                 usage_out[pl.ds(shards_ref[base], 1), :] += squares[:, :128]
                 usage_out[pl.ds(shards_ref[base + 1], 1), :] += squares[:, 128:]
@@ -201,7 +206,8 @@
             )
         matrix = matrix.astype(BF16)
         source = q // nx
-        base = ((((source & 1) ^ core) * ny + (source >> 1)) * nx + q % nx) * 8
+        away = (ids_ref[1] - q) & (nx - 1)
+        base = ((((source & 1) ^ core) * ny + (source >> 1)) * nx + away) * 8
         none = jnp.zeros((32, 128), F32)
         for pair in range(2):
             x = msg_ref[q, pair * 32 : pair * 32 + 32, :].astype(F32)
@@ -310,16 +316,17 @@
     sds = jax.ShapeDtypeStruct
     y, x, c = (lax.axis_index(a) for a in ("y", "x", "c"))
     ids = jnp.stack([y, x, c]).astype(jnp.int32)
-    names = jnp.pad(block_shards.reshape(1, -1), ((0, 15), (0, 128 - 2 * blocks))).astype(F32)
     packed = call(
         pack_kernel,
-        "vvvv",
-        sds((nx, rows + 16, width), BF16),
+        "ssvvv",
+        tuple(sds((rows + 16, width), BF16) for _ in range(nx)),
         [],
-        patches, codes, support, names,
-    )
-    held = exchange(packed, "x")
-    names = held[:, rows, 256 : 256 + 2 * blocks].reshape(1, -1)
+        block_shards.T, ids, patches, codes.T, support.T,
+    )
+    held = [packed[0]]
+    for j in range(1, nx):
+        held.append(lax.ppermute(packed[j], "x", [(i, (i + j) % nx) for i in range(nx)]))
+    names = jnp.concatenate([h[rows : rows + 1, 256 : 256 + 2 * blocks] for h in held], axis=1)
     own = lax.dynamic_slice(dictionary, ((y * nc + c) * piece, x * width), (piece, width))
     by_hi = spread(own, "zh", zh)
     by_z = spread(by_hi, "zl", zl).reshape(zh * zl, piece, width)
@@ -329,34 +336,36 @@
     cut = 2 * blocks * nx
     shards = jnp.concatenate([mine[:, zh * zl, 0, :cut], other[:, zh * zl, 0, :cut]], axis=0)
     shards = shards.astype(jnp.int32).reshape(-1)
-    common = (shards, ids, held, mine, other)
+    common = (shards, ids, *held, mine, other)
+    sizes = (ny, nx, zh, zl, plen)
+    takes = "ss" + "v" * (nx + 2)
     grads = sds((nx, SLOTS, nx * rows), F32)
     first = call(
-        lambda *r: refine_kernel(0, (ny, zh, zl, plen), *r), "ssvvv", grads, [], *common
+        lambda *r: refine_kernel(0, sizes, *r), takes, grads, [], *common
     )
     second, codes_1 = call(
-        lambda *r: refine_kernel(1, (ny, zh, zl, plen), *r),
-        "ssvvvv",
+        lambda *r: refine_kernel(1, sizes, *r),
+        takes + "v",
         (grads, sds((SLOTS, nx * rows), F32)),
         [],
         *common,
         exchange(first, "x"),
     )
     home, msg, usage, codes_2 = call(
-        lambda *r: refine_kernel(2, (ny, zh, zl, plen), *r),
-        "ssvvvvv",
+        lambda *r: refine_kernel(2, sizes, *r),
+        takes + "vv",
         (
             sds((nx, rows, width), BF16),
             sds((ny * nc, nx, MSG, 128), BF16),
             sds((zh * zl, 128), F32),
-            sds((nx, SLOTS, rows), F32),
+            sds((SLOTS, rows), F32),
         ),
         [],
         *common,
         exchange(second, "x"),
         codes_1,
     )
-    new_codes = jnp.transpose(lax.dynamic_index_in_dim(codes_2, x, 0, keepdims=False))
+    new_codes = codes_2.T
     got = exchange(msg, ("y", "c")).reshape(ny * nc * nx, MSG, 128)
     at_home = exchange(home, "x")
     to_owner = call(

time: 199 us -> 195 us (0.980)
  blocking collectives: 83.1 us -> 98.9 us
  waiting for transfers between devices: 23.7 us -> 16.7 us
  starting transfers between devices: 41.9 us -> 35.8 us
  local copies, waits for them, and re-layouts: 10.5 us -> 5.39 us
    all_to_all x6, blocking collectives: 83.1 us -> 98.9 us  [exchange(): return lax.all_to_all(x, axes, split_axis=0, concat_axis=0, tiled=True)]
    all_to_all x4 -> x3, starting transfers between devices: 34.7 us -> 19.1 us  [exchange(): return lax.all_to_all(x, axes, split_axis=0, concat_axis=0, tiled=True)]
    ppermute x0 -> x3, starting transfers between devices: none -> 10.5 us  [body(): lax.ppermute(packed[j], 'x', [(i, (i + j) % nx) for i in range(nx)])]
    all_to_all x4 -> x3, waiting for transfers between devices: 22 us -> 11.6 us  [exchange(): return lax.all_to_all(x, axes, split_axis=0, concat_axis=0, tiled=True)]
    unnamed x14 -> x15, local copies, waits for them, and re-layouts: 5.69 us -> 2.03 us
    ppermute x0 -> x3, waiting for transfers between devices: none -> 2.78 us  [body(): lax.ppermute(packed[j], 'x', [(i, (i + j) % nx) for i in range(nx)])]
  transfers between devices with their start and end apart: 5 -> 7, of which waited for: 4 -> 4; matrix products, arithmetic and copies ran while one was open for 4% -> 1% of each run, Pallas kernels for 6% -> 6%
where the time goes in v4:
time: 195 us; the launch traced here: 194 us
  blocking collectives  98.9 us (51%)
  starting transfers between devices  35.8 us (18%)
  Pallas kernels  35.5 us (18%)
  waiting for transfers between devices  16.7 us (9%)
  local copies, waits for them, and re-layouts  5.39 us (3%)
    all_to_all x6, blocking collectives, exchange(): return lax.all_to_all(x, axes, split_axis=0, concat_axis=0, tiled=True)  98.9 us
    pallas_call x7, Pallas kernels, call(): pl.pallas_call(kernel, out_shape=outs, in_specs=[pl.BlockSpec(memory_spac...  35.5 us
    all_to_all x3, starting transfers between devices, exchange(): return lax.all_to_all(x, axes, split_axis=0, concat_axis=0, tiled=True)  19.1 us
    all_to_all x3, waiting for transfers between devices, exchange(): return lax.all_to_all(x, axes, split_axis=0, concat_axis=0, tiled=True)  11.6 us
    ppermute x3, starting transfers between devices, body(): lax.ppermute(packed[j], 'x', [(i, (i + j) % nx) for i in range(nx)])  10.5 us
    ppermute x1, starting transfers between devices, body(): other = lax.ppermute(mine, 'c', [(0, 1), (1, 0)])  6.2 us
  transfers between devices with their start and end apart: 7, of which 4 were waited for; matrix products, arithmetic and copies ran while one was open for 1% of the time, Pallas kernels for 6%

profile of v4, /device:TPU:1, one launch (start us, length us, event | category | flops | bytes accessed | tf_op | source)
XLA Modules:
  0.0 193.9 jit_solution(11279180224931215569)
XLA Ops:
  1.4 27.9 %all_to_all.45 = bf16[4,16,512]{2,1,0:T(8,128)(2,1)S(1)} all-to-all(bf16[4,16,512]{2,1,0:T(8,128)(2,1)S(1)} %broadcast_in_dim.8), channel_id=1, replica_groups=mesh['y'=4,'x'=4,'c'=2,'zh'=4,'zl'=4] {'zh'}, dimensions={0} | all-to-all | bytes 131072 | tf_op jit(solution)/shard_map/all_to_all | solution.py:303
  30.0 3.4 %all-to-all-start.1 = ((bf16[4,4,16,512]{3,2,1,0:T(8,128)(2,1)}), bf16[4,4,16,512]{3,2,1,0:T(8,128)(2,1)S(1)}, u32[]{:S(2)}, u32[]{:S(2)}) async-start(bf16[4,4,16,512]{3,2,1,0:T(8,128)(2,1)} %broadcast_in_dim.9), calls=%async_computation.1 | async-start | bytes 524288 | tf_op jit(solution)/shard_map/all_to_all | solution.py:303
  34.1 1.9 shard_map.76
  36.0 3.1 %collective-permute-start = (bf16[144,512]{1,0:T(8,128)(2,1)}, bf16[144,512]{1,0:T(8,128)(2,1)S(1)}, u32[]{:S(2)}, u32[]{:S(2)}) collective-permute-start(bf16[144,512]{1,0:T(8,128)(2,1)} %get-tuple-element.16), channel_id=1, source_target_pairs={{0,32},{32,64},{64,96},{96,0},{1,33},{33,65},{65,97},{97,1},{2,34}... | collective-permute-start | bytes 442376 | tf_op jit(solution)/shard_map/ppermute | solution.py:328
  39.2 4.4 %collective-permute-start.1 = (bf16[144,512]{1,0:T(8,128)(2,1)}, bf16[144,512]{1,0:T(8,128)(2,1)S(1)}, u32[]{:S(2)}, u32[]{:S(2)}) collective-permute-start(bf16[144,512]{1,0:T(8,128)(2,1)} %get-tuple-element.17), channel_id=1, source_target_pairs={{0,64},{32,96},{64,0},{96,32},{1,65},{33,97},{65,1},{97,33},{2,66}... | collective-permute-start | bytes 442376 | tf_op jit(solution)/shard_map/ppermute | solution.py:328
  43.5 3.1 %collective-permute-start.2 = (bf16[144,512]{1,0:T(8,128)(2,1)}, bf16[144,512]{1,0:T(8,128)(2,1)S(1)}, u32[]{:S(2)}, u32[]{:S(2)}) collective-permute-start(bf16[144,512]{1,0:T(8,128)(2,1)} %get-tuple-element.18), channel_id=1, source_target_pairs={{0,96},{32,0},{64,32},{96,64},{1,97},{33,1},{65,33},{97,65},{2,98}... | collective-permute-start | bytes 442376 | tf_op jit(solution)/shard_map/ppermute | solution.py:328
  47.3 1.3 collective-permute-done.1.r_4_
  48.6 1.4 collective-permute-done.2.r_5_
  50.3 16.4 %all_to_all.46.r_6_ = bf16[4,17,16,512]{3,2,1,0:T(8,128)(2,1)S(1)} all-to-all(bf16[4,17,16,512]{3,2,1,0:T(8,128)(2,1)S(1)} %broadcast_in_dim.11), channel_id=1, replica_groups=mesh['y'=4,'x'=4,'c'=2,'zh'=4,'zl'=4] {'y'}, dimensions={0} | all-to-all | bytes 2228224 | tf_op jit(solution)/shard_map/all_to_all | solution.py:303
  66.8 6.2 %collective-permute-start.3 = (bf16[4,17,16,512]{3,2,1,0:T(8,128)(2,1)S(1)}, bf16[4,17,16,512]{3,2,1,0:T(8,128)(2,1)S(1)}, u32[]{:S(2)}, u32[]{:S(2)}) collective-permute-start(bf16[4,17,16,512]{3,2,1,0:T(8,128)(2,1)S(1)} %all_to_all.46.r_6_), channel_id=1, source_target_pairs={{0,16},{16,0},{1,17},{17,1},{2,18},{18,2},{3,19},{19,3},{4,20},{20... | collective-permute-start | bytes 3342344 | tf_op jit(solution)/shard_map/ppermute | solution.py:335
  73.0 2.3 %collective-permute-done.3.r_7_ = bf16[4,17,16,512]{3,2,1,0:T(8,128)(2,1)S(1)} collective-permute-done((bf16[4,17,16,512]{3,2,1,0:T(8,128)(2,1)S(1)}, bf16[4,17,16,512]{3,2,1,0:T(8,128)(2,1)S(1)}, u32[]{:S(2)}, u32[]{:S(2)}) %collective-permute-start.3) | collective-permute-done | bytes 1114144 | tf_op jit(solution)/shard_map/ppermute | solution.py:335
  76.3 6.9 %shard_map.77 = f32[4,8,512]{2,1,0:T(8,128)} custom-call(s32[256]{0:T(256)} %reshape.25.r_0_, s32[3]{0:T(128)} %pad_add_fusion.ids_ref.r_1_, bf16[144,512]{1,0:T(8,128)(2,1)} %get-tuple-element.15.r_2_, bf16[144,512]{1,0:T(8,128)(2,1)} %copy-done.3, bf16[144,512]{1,0:T(8,128)(2,1)} %copy-done.4, bf16[144,512]{1,0:T(8,128)(2,1)} %copy-done.5, ...), custom_call_target="tpu_custom_call" | custom-call | flops 1000000000 | bytes 3000000 | tf_op jit(solution)/shard_map/pallas_call | solution.py:289
  83.3 8.4 %all_to_all.47.r_8_ = f32[4,8,512]{2,1,0:T(8,128)} all-to-all(f32[4,8,512]{2,1,0:T(8,128)} %shard_map.77), channel_id=1, replica_groups=mesh['y'=4,'x'=4,'c'=2,'zh'=4,'zl'=4] {'x'}, dimensions={0} | all-to-all | bytes 131072 | tf_op jit(solution)/shard_map/all_to_all | solution.py:303
  91.7 6.6 %shard_map.78 = (f32[4,8,512]{2,1,0:T(8,128)}, f32[8,512]{1,0:T(8,128)}) custom-call(s32[256]{0:T(256)} %reshape.25.r_0_, s32[3]{0:T(128)} %pad_add_fusion.ids_ref.r_1_, bf16[144,512]{1,0:T(8,128)(2,1)} %get-tuple-element.15.r_2_, bf16[144,512]{1,0:T(8,128)(2,1)} %copy-done.3, bf16[144,512]{1,0:T(8,128)(2,1)} %copy-done.4, bf16[144,512]{1,0:T(8,128)(2,1)} %copy-done.5, ...), custom_call_target="tpu_custom_call" | custom-call | flops 1000000000 | bytes 3000000 | tf_op jit(solution)/shard_map/pallas_call | solution.py:289
  98.3 8.4 %all_to_all.48.r_8_ = f32[4,8,512]{2,1,0:T(8,128)} all-to-all(f32[4,8,512]{2,1,0:T(8,128)} %get-tuple-element.19), channel_id=1, replica_groups=mesh['y'=4,'x'=4,'c'=2,'zh'=4,'zl'=4] {'x'}, dimensions={0} | all-to-all | bytes 131072 | tf_op jit(solution)/shard_map/all_to_all | solution.py:303
  106.7 5.7 %shard_map.79 = (bf16[4,128,512]{2,1,0:T(8,128)(2,1)}, bf16[8,4,80,128]{3,2,1,0:T(8,128)(2,1)}, f32[16,128]{1,0:T(8,128)}, f32[8,128]{1,0:T(8,128)}) custom-call(s32[256]{0:T(256)} %reshape.25.r_0_, s32[3]{0:T(128)} %pad_add_fusion.ids_ref.r_1_, bf16[144,512]{1,0:T(8,128)(2,1)} %get-tuple-element.15.r_2_, bf16[144,512]{1,0:T(8,128)(2,1)} %copy-done.3, ...), custom_call_target="tpu_custom_call" | custom-call | flops 1000000000 | bytes 3000000 | tf_op jit(solution)/shard_map/pallas_call | solution.py:289
  112.5 17.8 %all_to_all.49 = bf16[8,4,80,128]{3,2,1,0:T(8,128)(2,1)} all-to-all(bf16[8,4,80,128]{3,2,1,0:T(8,128)(2,1)} %get-tuple-element.21), channel_id=1, replica_groups=mesh['y'=4,'x'=4,'c'=2,'zh'=4,'zl'=4] {'y','c'}, dimensions={0} | all-to-all | bytes 1310720 | tf_op jit(solution)/shard_map/all_to_all | solution.py:303
  130.3 3.5 %all-to-all-start.6 = ((bf16[4,128,512]{2,1,0:T(8,128)(2,1)}), bf16[4,128,512]{2,1,0:T(8,128)(2,1)S(1)}, u32[]{:S(2)}, u32[]{:S(2)}) async-start(bf16[4,128,512]{2,1,0:T(8,128)(2,1)} %get-tuple-element.23), calls=%async_computation.6 | async-start | bytes 1048576 | tf_op jit(solution)/shard_map/all_to_all | solution.py:303
  133.8 9.8 %shard_map.80 = bf16[16,80,128]{2,1,0:T(8,128)(2,1)} custom-call(s32[256]{0:T(256)} %reshape.25.r_0_, s32[3]{0:T(128)} %pad_add_fusion.ids_ref.r_1_, bf16[32,80,128]{2,1,0:T(8,128)(2,1)} %bitcast.22, f32[16,128]{1,0:T(8,128)} %get-tuple-element.22.r_3_), custom_call_target="tpu_custom_call" | custom-call | flops 10000000000 | bytes 30000000 | tf_op jit(solution)/shard_map/pallas_call | solution.py:289
  143.6 19.8 %all_to_all.50.parts_ref = bf16[16,80,128]{2,1,0:T(8,128)(2,1)} all-to-all(bf16[16,80,128]{2,1,0:T(8,128)(2,1)} %shard_map.80), channel_id=1, replica_groups=mesh['y'=4,'x'=4,'c'=2,'zh'=4,'zl'=4] {'zh','zl'}, dimensions={0} | all-to-all | bytes 655360 | tf_op jit(solution)/shard_map/all_to_all | solution.py:303
  163.4 1.9 shard_map.81
  165.3 12.2 %all-to-all-start.8 = ((bf16[32,80,128]{2,1,0:T(8,128)(2,1)}), bf16[32,80,128]{2,1,0:T(8,128)(2,1)S(1)}, u32[]{:S(2)}, u32[]{:S(2)}) async-start(bf16[32,80,128]{2,1,0:T(8,128)(2,1)} %shard_map.81), calls=%async_computation.8 | async-start | bytes 1310720 | tf_op jit(solution)/shard_map/all_to_all | solution.py:303
  178.8 11.6 %all-to-all-done.8.r_0_ = bf16[32,80,128]{2,1,0:T(8,128)(2,1)S(1)} async-done(((bf16[32,80,128]{2,1,0:T(8,128)(2,1)}), bf16[32,80,128]{2,1,0:T(8,128)(2,1)S(1)}, u32[]{:S(2)}, u32[]{:S(2)}) %all-to-all-start.8) | async-done | bytes 655392 | tf_op jit(solution)/shard_map/all_to_all | solution.py:303
  191.3 2.6 %shard_map.82 = bf16[128,2048]{1,0:T(8,128)(2,1)} custom-call(bf16[32,80,128]{2,1,0:T(8,128)(2,1)} %copy-done.1, bf16[128,2048]{1,0:T(8,128)(2,1)} %r_1_.1), custom_call_target="tpu_custom_call" | custom-call | flops 1000000000 | bytes 3000000 | tf_op jit(solution)/shard_map/pallas_call | solution.py:289
  (34 shorter events, 6.2 us)
Async XLA Ops:
  30.0 20.1 %all-to-all-start.1 = ((bf16[4,4,16,512]{3,2,1,0:T(8,128)(2,1)}), bf16[4,4,16,512]{3,2,1,0:T(8,128)(2,1)S(1)}, u32[]{:S(2)}, u32[]{:S(2)}) async-start(bf16[4,4,16,512]{3,2,1,0:T(8,128)(2,1)} %broadcast_in_dim.9), calls=%async_computation.1 | async-start | bytes 524288 | tf_op jit(solution)/shard_map/all_to_all | solution.py:303
  36.0 11.2 %collective-permute-start = (bf16[144,512]{1,0:T(8,128)(2,1)}, bf16[144,512]{1,0:T(8,128)(2,1)S(1)}, u32[]{:S(2)}, u32[]{:S(2)}) collective-permute-start(bf16[144,512]{1,0:T(8,128)(2,1)} %get-tuple-element.16), channel_id=1, source_target_pairs={{0,32},{32,64},{64,96},{96,0},{1,33},{33,65},{65,97},{97,1},{2,34}... | collective-permute-start | bytes 442376 | tf_op jit(solution)/shard_map/ppermute | solution.py:328
  39.2 9.5 %collective-permute-start.1 = (bf16[144,512]{1,0:T(8,128)(2,1)}, bf16[144,512]{1,0:T(8,128)(2,1)S(1)}, u32[]{:S(2)}, u32[]{:S(2)}) collective-permute-start(bf16[144,512]{1,0:T(8,128)(2,1)} %get-tuple-element.17), channel_id=1, source_target_pairs={{0,64},{32,96},{64,0},{96,32},{1,65},{33,97},{65,1},{97,33},{2,66}... | collective-permute-start | bytes 442376 | tf_op jit(solution)/shard_map/ppermute | solution.py:328
  43.5 6.5 %collective-permute-start.2 = (bf16[144,512]{1,0:T(8,128)(2,1)}, bf16[144,512]{1,0:T(8,128)(2,1)S(1)}, u32[]{:S(2)}, u32[]{:S(2)}) collective-permute-start(bf16[144,512]{1,0:T(8,128)(2,1)} %get-tuple-element.18), channel_id=1, source_target_pairs={{0,96},{32,0},{64,32},{96,64},{1,97},{33,1},{65,33},{97,65},{2,98}... | collective-permute-start | bytes 442376 | tf_op jit(solution)/shard_map/ppermute | solution.py:328
  47.3 19.5 %copy-start.3 = (bf16[144,512]{1,0:T(8,128)(2,1)}, bf16[144,512]{1,0:T(8,128)(2,1)S(1)}, u32[]{:S(2)}) copy-start(bf16[144,512]{1,0:T(8,128)(2,1)S(1)} %collective-permute-done.r_3_) | copy-start | bytes 442372
  48.6 18.1 %copy-start.4 = (bf16[144,512]{1,0:T(8,128)(2,1)}, bf16[144,512]{1,0:T(8,128)(2,1)S(1)}, u32[]{:S(2)}) copy-start(bf16[144,512]{1,0:T(8,128)(2,1)S(1)} %collective-permute-done.1.r_4_) | copy-start | bytes 442372
  50.1 16.7 %copy-start.5 = (bf16[144,512]{1,0:T(8,128)(2,1)}, bf16[144,512]{1,0:T(8,128)(2,1)S(1)}, u32[]{:S(2)}) copy-start(bf16[144,512]{1,0:T(8,128)(2,1)S(1)} %collective-permute-done.2.r_5_) | copy-start | bytes 442372
  66.8 9.4 %copy-start = (bf16[4,17,16,512]{3,2,1,0:T(8,128)(2,1)}, bf16[4,17,16,512]{3,2,1,0:T(8,128)(2,1)S(1)}, u32[]{:S(2)}) copy-start(bf16[4,17,16,512]{3,2,1,0:T(8,128)(2,1)S(1)} %all_to_all.46.r_6_) | copy-start | bytes 3342340
  66.8 8.6 %collective-permute-start.3 = (bf16[4,17,16,512]{3,2,1,0:T(8,128)(2,1)S(1)}, bf16[4,17,16,512]{3,2,1,0:T(8,128)(2,1)S(1)}, u32[]{:S(2)}, u32[]{:S(2)}) collective-permute-start(bf16[4,17,16,512]{3,2,1,0:T(8,128)(2,1)S(1)} %all_to_all.46.r_6_), channel_id=1, source_target_pairs={{0,16},{16,0},{1,17},{17,1},{2,18},{18,2},{3,19},{19,3},{4,20},{20... | collective-permute-start | bytes 3342344 | tf_op jit(solution)/shard_map/ppermute | solution.py:335
  75.4 1.0 copy-start.2
  130.3 13.3 %all-to-all-start.6 = ((bf16[4,128,512]{2,1,0:T(8,128)(2,1)}), bf16[4,128,512]{2,1,0:T(8,128)(2,1)S(1)}, u32[]{:S(2)}, u32[]{:S(2)}) async-start(bf16[4,128,512]{2,1,0:T(8,128)(2,1)} %get-tuple-element.23), calls=%async_computation.6 | async-start | bytes 1048576 | tf_op jit(solution)/shard_map/all_to_all | solution.py:303
  165.3 25.1 %all-to-all-start.8 = ((bf16[32,80,128]{2,1,0:T(8,128)(2,1)}), bf16[32,80,128]{2,1,0:T(8,128)(2,1)S(1)}, u32[]{:S(2)}, u32[]{:S(2)}) async-start(bf16[32,80,128]{2,1,0:T(8,128)(2,1)} %shard_map.81), calls=%async_computation.8 | async-start | bytes 1310720 | tf_op jit(solution)/shard_map/all_to_all | solution.py:303
  190.4 0.8 copy-start.1

commit v5 on v4

--- a/solution.py
+++ b/solution.py
@@ -12,7 +12,6 @@
 NT = (((1,), (1,)), ((), ()))
 VMEM_LIMIT = 56 * 1024 * 1024
 DP_SPLIT = (4, 4, 2)
-GROUP_SPLIT = (4, 4)
 SHARD = 128
 SLOTS = 8
 MAIN = 64
@@ -52,47 +51,35 @@
     return top[:SLOTS] + top[SLOTS:] + low[:SLOTS], low[SLOTS:]
 
 
-def to_rows(codes_t, sup_t):
-    side = jnp.concatenate([codes_t, sup_t, jnp.zeros((128 - 2 * SLOTS, 128), F32)], axis=0)
-    return jnp.transpose(side)
-
-
-def atom_lanes(rows, core, piece):
-    lane = lax.broadcasted_iota(jnp.int32, (rows, 256), 1)
+def atom_rows(core, piece):
+    row = lax.broadcasted_iota(jnp.int32, (256, 128), 0)
     shift = piece.bit_length() - 1
-    spot = lane & 127
+    spot = row & 127
     other = spot >> 6
     half = spot & 63
     place = ((half >> shift) * 2 + (core ^ other)) * piece + (half & (piece - 1))
-    return ((lane & 128) + place).astype(F32)
-
-
-def masks_of(side, lanes):
-    return [side[:, SLOTS + k : SLOTS + k + 1] == lanes for k in range(SLOTS)]
-
-
-def code_matrix(values, hits):
-    summed = jnp.where(hits[0], values[:, 0:1], 0.0)
+    return ((row & 128) + place).astype(F32)
+
+
+def code_matrix(codes_t, sup_t, atoms):
+    total = jnp.where(sup_t[0:1] == atoms, codes_t[0:1], 0.0)
     for k in range(1, SLOTS):
-        summed = summed + jnp.where(hits[k], values[:, k : k + 1], 0.0)
-    return summed.astype(BF16)
-
-
-def pick(matrix, hits, slot_lane):
-    out = jnp.zeros(slot_lane.shape, F32)
-    for k in range(SLOTS):
-        col = jnp.sum(jnp.where(hits[k], matrix, 0.0), axis=1, keepdims=True)
-        out = jnp.where(slot_lane == k, col, out)
-    return out
-
-
-def shard_row(shard, zh, zl):
-    shift = zl.bit_length() - 1
-    return (shard & (zl - 1)) * zh + (shard >> shift)
+        total = total + jnp.where(sup_t[k : k + 1] == atoms, codes_t[k : k + 1], 0.0)
+    return total
+
+
+def pick(matrix, sup_t, atoms):
+    return jnp.concatenate(
+        [
+            jnp.sum(jnp.where(sup_t[k : k + 1] == atoms, matrix, 0.0), axis=0, keepdims=True)
+            for k in range(SLOTS)
+        ],
+        axis=0,
+    )
 
 
 def refine_kernel(step, sizes, shards_ref, ids_ref, *refs):
-    ny, nx, zh, zl, plen = sizes
+    ny, nx, plen = sizes
     x_refs, (mine_ref, other_ref), refs = refs[:nx], refs[nx : nx + 2], refs[nx + 2 :]
     height, width = x_refs[0].shape
     rows = height - 16
@@ -100,8 +87,7 @@
     blocks = rows // 32
     chunk = min(256, width)
     core = ids_ref[2]
-    lanes = atom_lanes(rows, core, piece)
-    slot_lane = lax.broadcasted_iota(jnp.int32, (rows, 128), 1)
+    order = atom_rows(core, piece)
     if step == 0:
         (grad_out,) = refs
     elif step == 1:
@@ -126,15 +112,14 @@
             codes_t = codes_ref[:, mine] + moved
             if s == 0:
                 codes_out[...] = codes_t
-        side = to_rows(codes_t, sup_t)
-        hits = masks_of(side, lanes)
-        matrix = code_matrix(side, hits)
+        upright = code_matrix(codes_t, sup_t, order)
+        matrix = jnp.transpose(upright).astype(BF16)
         scores = []
         outs = [[] for _ in range(width // chunk)]
         for b in range(blocks):
             base = (ids_ref[0] * nx + s) * 2 * blocks + 2 * b
-            at_a = shard_row(shards_ref[base], zh, zl)
-            at_b = shard_row(shards_ref[base + 1], zh, zl)
+            at_a = shards_ref[base]
+            at_b = shards_ref[base + 1]
             part = matrix[b * 32 : (b + 1) * 32]
             total = None
             for j in range(width // chunk):
@@ -157,12 +142,11 @@
                     outs[j].append(resid)
             scores.append(total)
         if step < 2:
-            grad = pick(jnp.concatenate(scores, axis=0), hits, slot_lane)
-            grad_t = jnp.transpose(grad)[:SLOTS]
+            grad_t = pick(jnp.transpose(jnp.concatenate(scores, axis=0)), sup_t, order)
             for j in range(nx):
                 grad_out[j, :, at] = grad_t
             continue
-        merged_t = jnp.transpose(pick(matrix.astype(F32), hits, slot_lane))[:SLOTS]
+        merged_t = pick(upright.astype(BF16).astype(F32), sup_t, order)
         side_t = jnp.concatenate([merged_t, sup_t], axis=0).astype(BF16)
         for j in range(width // chunk):
             full = jnp.concatenate(outs[j], axis=0)
@@ -179,9 +163,9 @@
                 msg_out[2 * u + 1, source, MAIN:, :] = side_t
         if s == 0:
             usage_out[...] = jnp.zeros_like(usage_out)
-            plain = lax.broadcasted_iota(jnp.int32, (rows, 256), 1).astype(F32)
-            wide = code_matrix(side, masks_of(side, plain)).astype(F32)
-            wide = wide * wide
+            plain = lax.broadcasted_iota(jnp.int32, (256, 128), 0).astype(F32)
+            wide = code_matrix(codes_t, sup_t, plain).astype(BF16).astype(F32)
+            wide = jnp.transpose(wide * wide)
             for b in range(blocks):
                 base = (ids_ref[0] * nx + s) * 2 * blocks + 2 * b
                 squares = jnp.sum(wide[b * 32 : (b + 1) * 32], axis=0, keepdims=True)
@@ -190,7 +174,7 @@
 
 
 def stats_kernel(sizes, shards_ref, ids_ref, msg_ref, usage_ref, out_ref, acc_ref):
-    ny, nx, zh, zl = sizes
+    ny, nx = sizes
     acc_ref[...] = jnp.zeros_like(acc_ref)
     atom = lax.broadcasted_iota(jnp.int32, (256, 128), 0).astype(F32)
     low = lax.broadcasted_iota(jnp.int32, (32, 128), 1) < 64
@@ -223,16 +207,14 @@
                 acc_ref[pl.ds(at1, 128), :] += jnp.where(low_all, 0.0, values)
         return carry
 
-    lax.fori_loop(0, msg_ref.shape[0], one, 0)
+    lax.fori_loop(0, msg_ref.shape[0], one, 0, unroll=4)
     low = lax.broadcasted_iota(jnp.int32, (MAIN, 128), 1) < 64
     row = lax.broadcasted_iota(jnp.int32, (16, 128), 0)
-    for lo in range(zl):
-        for hi in range(zh):
-            s = hi * zl + lo
-            full = acc_ref[s * 128 : (s + 1) * 128, :]
-            full = full + pltpu.roll(full, 64, 1)
-            out_ref[s, :MAIN, :] = jnp.where(low, full[:MAIN], full[MAIN:]).astype(BF16)
-            out_ref[s, MAIN:, :] = two_parts(usage_ref[s : s + 1, :], row)
+    for s in range(out_ref.shape[0]):
+        full = acc_ref[s * 128 : (s + 1) * 128, :]
+        full = full + pltpu.roll(full, 64, 1)
+        out_ref[s, :MAIN, :] = jnp.where(low, full[:MAIN], full[MAIN:]).astype(BF16)
+        out_ref[s, MAIN:, :] = two_parts(usage_ref[s : s + 1, :], row)
 
 
 def two_parts(used, row):
@@ -307,7 +289,7 @@
     return exchange(jnp.broadcast_to(x[None], (count, *x.shape)), axes)
 
 
-def body(ny, nx, zh, zl, patches, codes, support, block_shards, dictionary):
+def body(ny, nx, nz, patches, codes, support, block_shards, dictionary):
     rows, plen = patches.shape
     blocks = block_shards.shape[0]
     width = plen // nx
@@ -328,16 +310,15 @@
         held.append(lax.ppermute(packed[j], "x", [(i, (i + j) % nx) for i in range(nx)]))
     names = jnp.concatenate([h[rows : rows + 1, 256 : 256 + 2 * blocks] for h in held], axis=1)
     own = lax.dynamic_slice(dictionary, ((y * nc + c) * piece, x * width), (piece, width))
-    by_hi = spread(own, "zh", zh)
-    by_z = spread(by_hi, "zl", zl).reshape(zh * zl, piece, width)
+    by_z = spread(own, "z", nz).reshape(nz, piece, width)
     extra = jnp.pad(names, ((0, piece - 1), (0, width - names.shape[1])))
     mine = spread(jnp.concatenate([by_z, extra[None]], axis=0), "y", ny)
     other = lax.ppermute(mine, "c", [(0, 1), (1, 0)])
     cut = 2 * blocks * nx
-    shards = jnp.concatenate([mine[:, zh * zl, 0, :cut], other[:, zh * zl, 0, :cut]], axis=0)
+    shards = jnp.concatenate([mine[:, nz, 0, :cut], other[:, nz, 0, :cut]], axis=0)
     shards = shards.astype(jnp.int32).reshape(-1)
     common = (shards, ids, *held, mine, other)
-    sizes = (ny, nx, zh, zl, plen)
+    sizes = (ny, nx, plen)
     takes = "ss" + "v" * (nx + 2)
     grads = sds((nx, SLOTS, nx * rows), F32)
     first = call(
@@ -357,7 +338,7 @@
         (
             sds((nx, rows, width), BF16),
             sds((ny * nc, nx, MSG, 128), BF16),
-            sds((zh * zl, 128), F32),
+            sds((nz, 128), F32),
             sds((SLOTS, rows), F32),
         ),
         [],
@@ -369,10 +350,10 @@
     got = exchange(msg, ("y", "c")).reshape(ny * nc * nx, MSG, 128)
     at_home = exchange(home, "x")
     to_owner = call(
-        lambda *r: stats_kernel((ny, nx, zh, zl), *r),
+        lambda *r: stats_kernel((ny, nx), *r),
         "ssvv",
-        sds((zh * zl, MSG, 128), BF16),
-        [pltpu.VMEM((zh * zl * SHARD, 128), F32)],
+        sds((nz, MSG, 128), BF16),
+        [pltpu.VMEM((nz * SHARD, 128), F32)],
         shards, ids, got, usage, us=10,
     )
     to_owner, at_home = lax.optimization_barrier((to_owner, at_home))
@@ -382,7 +363,7 @@
         "v",
         sds((ny * nx * nc, MSG, 128), BF16),
         [],
-        exchange(to_owner, ("zh", "zl")),
+        exchange(to_owner, "z"),
     )
     new_dictionary = call(
         lambda *r: renew_kernel((ny, nx), *r),
@@ -395,11 +376,11 @@
 
 
 def solution(mesh):
-    fine = Mesh(mesh.devices.reshape(DP_SPLIT + GROUP_SPLIT), ("y", "x", "c", "zh", "zl"))
-    row = P(("y", "x", "c", "zh", "zl"), None)
-    shard = P(("zh", "zl"), None)
+    fine = Mesh(mesh.devices.reshape(DP_SPLIT + (-1,)), ("y", "x", "c", "z"))
+    row = P(("y", "x", "c", "z"), None)
+    shard = P("z", None)
     return jax.shard_map(
-        functools.partial(body, DP_SPLIT[0], DP_SPLIT[1], *GROUP_SPLIT),
+        functools.partial(body, DP_SPLIT[0], DP_SPLIT[1], mesh.shape["group"]),
         mesh=fine,
         in_specs=(row, row, row, row, shard),
         out_specs=(shard, row, row),

time: 195 us -> 179 us (0.918)
  blocking collectives: 98.9 us -> 76.3 us
  starting transfers between devices: 35.8 us -> 47.6 us
  Pallas kernels: 35.5 us -> 28.1 us
  waiting for transfers between devices: 16.7 us -> 18.8 us
    all_to_all x6 -> x5, blocking collectives: 98.9 us -> 76.3 us  [exchange(): return lax.all_to_all(x, axes, split_axis=0, concat_axis=0, tiled=True)]
    all_to_all x3, starting transfers between devices: 19.1 us -> 30.9 us  [exchange(): return lax.all_to_all(x, axes, split_axis=0, concat_axis=0, tiled=True)]
    pallas_call x7, Pallas kernels: 35.5 us -> 28.1 us  [call(): pl.pallas_call(kernel, out_shape=outs, in_specs=[pl.BlockSpec(memory_spac...]
    all_to_all x3, waiting for transfers between devices: 11.6 us -> 13.8 us  [exchange(): return lax.all_to_all(x, axes, split_axis=0, concat_axis=0, tiled=True)]
  transfers between devices with their start and end apart: 7 -> 7, of which waited for: 4 -> 5; matrix products, arithmetic and copies ran while one was open for 1% -> 2% of each run, Pallas kernels for 6% -> 5%
where the time goes in v5:
time: 179 us; the launch traced here: 178 us
  blocking collectives  76.3 us (43%)
  starting transfers between devices  47.6 us (27%)
  Pallas kernels  28.1 us (16%)
  waiting for transfers between devices  18.8 us (11%)
  local copies, waits for them, and re-layouts  5.38 us (3%)
    all_to_all x5, blocking collectives, exchange(): return lax.all_to_all(x, axes, split_axis=0, concat_axis=0, tiled=True)  76.3 us
    all_to_all x3, starting transfers between devices, exchange(): return lax.all_to_all(x, axes, split_axis=0, concat_axis=0, tiled=True)  30.9 us
    pallas_call x7, Pallas kernels, call(): pl.pallas_call(kernel, out_shape=outs, in_specs=[pl.BlockSpec(memory_spac...  28.1 us
    all_to_all x3, waiting for transfers between devices, exchange(): return lax.all_to_all(x, axes, split_axis=0, concat_axis=0, tiled=True)  13.8 us
    ppermute x3, starting transfers between devices, body(): lax.ppermute(packed[j], 'x', [(i, (i + j) % nx) for i in range(nx)])  10.5 us
    ppermute x1, starting transfers between devices, body(): other = lax.ppermute(mine, 'c', [(0, 1), (1, 0)])  6.16 us
  transfers between devices with their start and end apart: 7, of which 5 were waited for; matrix products, arithmetic and copies ran while one was open for 2% of the time, Pallas kernels for 5%

profile of v5, /device:TPU:1, one launch (start us, length us, event | category | flops | bytes accessed | tf_op | source)
XLA Modules:
  0.0 177.6 jit_solution(633453871035623983)
XLA Ops:
  2.1 15.7 %all-to-all-start = ((bf16[16,16,512]{2,1,0:T(8,128)(2,1)}), bf16[16,16,512]{2,1,0:T(8,128)(2,1)S(1)}, u32[]{:S(2)}, u32[]{:S(2)}) async-start(bf16[16,16,512]{2,1,0:T(8,128)(2,1)} %broadcast_in_dim.6), calls=%async_computation | async-start | bytes 524288 | tf_op jit(solution)/shard_map/all_to_all | solution.py:285
  18.5 1.9 %shard_map.76 = (bf16[144,512]{1,0:T(8,128)(2,1)}, bf16[144,512]{1,0:T(8,128)(2,1)}, bf16[144,512]{1,0:T(8,128)(2,1)}, bf16[144,512]{1,0:T(8,128)(2,1)}) custom-call(s32[2,4]{1,0:T(2,128)} %bitcast.25, s32[3]{0:T(128)} %pad_add_fusion.ids_ref.r_1_, bf16[128,2048]{1,0:T(8,128)(2,1)} %x_ref.1, f32[8,128]{1,0:T(8,128)} %bitcast.23, s32[8,128]{1,0:T(8,128)} %bitcast.24), custom_call_target="tpu_custom_call" | custom-call | flops 1000000000 | bytes 3000000 | tf_op jit(solution)/shard_map/pallas_call | solution.py:271
  20.5 3.1 %collective-permute-start = (bf16[144,512]{1,0:T(8,128)(2,1)}, bf16[144,512]{1,0:T(8,128)(2,1)S(1)}, u32[]{:S(2)}, u32[]{:S(2)}) collective-permute-start(bf16[144,512]{1,0:T(8,128)(2,1)} %get-tuple-element.16), channel_id=1, source_target_pairs={{0,32},{32,64},{64,96},{96,0},{1,33},{33,65},{65,97},{97,1},{2,34}... | collective-permute-start | bytes 442376 | tf_op jit(solution)/shard_map/ppermute | solution.py:310
  23.6 4.4 %collective-permute-start.1 = (bf16[144,512]{1,0:T(8,128)(2,1)}, bf16[144,512]{1,0:T(8,128)(2,1)S(1)}, u32[]{:S(2)}, u32[]{:S(2)}) collective-permute-start(bf16[144,512]{1,0:T(8,128)(2,1)} %get-tuple-element.17), channel_id=1, source_target_pairs={{0,64},{32,96},{64,0},{96,32},{1,65},{33,97},{65,1},{97,33},{2,66}... | collective-permute-start | bytes 442376 | tf_op jit(solution)/shard_map/ppermute | solution.py:310
  27.9 3.1 %collective-permute-start.2 = (bf16[144,512]{1,0:T(8,128)(2,1)}, bf16[144,512]{1,0:T(8,128)(2,1)S(1)}, u32[]{:S(2)}, u32[]{:S(2)}) collective-permute-start(bf16[144,512]{1,0:T(8,128)(2,1)} %get-tuple-element.18), channel_id=1, source_target_pairs={{0,96},{32,0},{64,32},{96,64},{1,97},{33,1},{65,33},{97,65},{2,98}... | collective-permute-start | bytes 442376 | tf_op jit(solution)/shard_map/ppermute | solution.py:310
  31.7 1.0 collective-permute-done.1.r_4_
  32.7 1.6 collective-permute-done.2.r_5_
  34.6 16.5 %all_to_all.40.r_6_ = bf16[4,17,16,512]{3,2,1,0:T(8,128)(2,1)S(1)} all-to-all(bf16[4,17,16,512]{3,2,1,0:T(8,128)(2,1)S(1)} %broadcast_in_dim.8), channel_id=1, replica_groups=mesh['y'=4,'x'=4,'c'=2,'z'=16] {'y'}, dimensions={0} | all-to-all | bytes 2228224 | tf_op jit(solution)/shard_map/all_to_all | solution.py:285
  51.1 6.2 %collective-permute-start.3 = (bf16[4,17,16,512]{3,2,1,0:T(8,128)(2,1)S(1)}, bf16[4,17,16,512]{3,2,1,0:T(8,128)(2,1)S(1)}, u32[]{:S(2)}, u32[]{:S(2)}) collective-permute-start(bf16[4,17,16,512]{3,2,1,0:T(8,128)(2,1)S(1)} %all_to_all.40.r_6_), channel_id=1, source_target_pairs={{0,16},{16,0},{1,17},{17,1},{2,18},{18,2},{3,19},{19,3},{4,20},{20... | collective-permute-start | bytes 3342344 | tf_op jit(solution)/shard_map/ppermute | solution.py:316
  57.3 2.3 %collective-permute-done.3.r_7_ = bf16[4,17,16,512]{3,2,1,0:T(8,128)(2,1)S(1)} collective-permute-done((bf16[4,17,16,512]{3,2,1,0:T(8,128)(2,1)S(1)}, bf16[4,17,16,512]{3,2,1,0:T(8,128)(2,1)S(1)}, u32[]{:S(2)}, u32[]{:S(2)}) %collective-permute-start.3) | collective-permute-done | bytes 1114144 | tf_op jit(solution)/shard_map/ppermute | solution.py:316
  60.6 5.3 %shard_map.77 = f32[4,8,512]{2,1,0:T(8,128)} custom-call(s32[256]{0:T(256)} %reshape.20.r_0_, s32[3]{0:T(128)} %pad_add_fusion.ids_ref.r_1_, bf16[144,512]{1,0:T(8,128)(2,1)} %get-tuple-element.15.r_2_, bf16[144,512]{1,0:T(8,128)(2,1)} %copy-done.3, bf16[144,512]{1,0:T(8,128)(2,1)} %copy-done.4, bf16[144,512]{1,0:T(8,128)(2,1)} %copy-done.5, ...), custom_call_target="tpu_custom_call" | custom-call | flops 1000000000 | bytes 3000000 | tf_op jit(solution)/shard_map/pallas_call | solution.py:271
  65.9 8.4 %all_to_all.41.r_8_ = f32[4,8,512]{2,1,0:T(8,128)} all-to-all(f32[4,8,512]{2,1,0:T(8,128)} %shard_map.77), channel_id=1, replica_groups=mesh['y'=4,'x'=4,'c'=2,'z'=16] {'x'}, dimensions={0} | all-to-all | bytes 131072 | tf_op jit(solution)/shard_map/all_to_all | solution.py:285
  74.4 5.3 %shard_map.78 = (f32[4,8,512]{2,1,0:T(8,128)}, f32[8,512]{1,0:T(8,128)}) custom-call(s32[256]{0:T(256)} %reshape.20.r_0_, s32[3]{0:T(128)} %pad_add_fusion.ids_ref.r_1_, bf16[144,512]{1,0:T(8,128)(2,1)} %get-tuple-element.15.r_2_, bf16[144,512]{1,0:T(8,128)(2,1)} %copy-done.3, bf16[144,512]{1,0:T(8,128)(2,1)} %copy-done.4, bf16[144,512]{1,0:T(8,128)(2,1)} %copy-done.5, ...), custom_call_target="tpu_custom_call" | custom-call | flops 1000000000 | bytes 3000000 | tf_op jit(solution)/shard_map/pallas_call | solution.py:271
  79.6 8.4 %all_to_all.42.r_8_ = f32[4,8,512]{2,1,0:T(8,128)} all-to-all(f32[4,8,512]{2,1,0:T(8,128)} %get-tuple-element.19), channel_id=1, replica_groups=mesh['y'=4,'x'=4,'c'=2,'z'=16] {'x'}, dimensions={0} | all-to-all | bytes 131072 | tf_op jit(solution)/shard_map/all_to_all | solution.py:285
  88.1 4.5 %shard_map.79 = (bf16[4,128,512]{2,1,0:T(8,128)(2,1)}, bf16[8,4,80,128]{3,2,1,0:T(8,128)(2,1)}, f32[16,128]{1,0:T(8,128)}, f32[8,128]{1,0:T(8,128)}) custom-call(s32[256]{0:T(256)} %reshape.20.r_0_, s32[3]{0:T(128)} %pad_add_fusion.ids_ref.r_1_, bf16[144,512]{1,0:T(8,128)(2,1)} %get-tuple-element.15.r_2_, bf16[144,512]{1,0:T(8,128)(2,1)} %copy-done.3, ...), custom_call_target="tpu_custom_call" | custom-call | flops 1000000000 | bytes 3000000 | tf_op jit(solution)/shard_map/pallas_call | solution.py:271
  92.6 18.0 %all_to_all.43 = bf16[8,4,80,128]{3,2,1,0:T(8,128)(2,1)} all-to-all(bf16[8,4,80,128]{3,2,1,0:T(8,128)(2,1)} %get-tuple-element.21), channel_id=1, replica_groups=mesh['y'=4,'x'=4,'c'=2,'z'=16] {'y','c'}, dimensions={0} | all-to-all | bytes 1310720 | tf_op jit(solution)/shard_map/all_to_all | solution.py:285
  110.6 3.5 %all-to-all-start.5 = ((bf16[4,128,512]{2,1,0:T(8,128)(2,1)}), bf16[4,128,512]{2,1,0:T(8,128)(2,1)S(1)}, u32[]{:S(2)}, u32[]{:S(2)}) async-start(bf16[4,128,512]{2,1,0:T(8,128)(2,1)} %get-tuple-element.23), calls=%async_computation.5 | async-start | bytes 1048576 | tf_op jit(solution)/shard_map/all_to_all | solution.py:285
  114.0 6.5 %shard_map.80 = bf16[16,80,128]{2,1,0:T(8,128)(2,1)} custom-call(s32[256]{0:T(256)} %reshape.20.r_0_, s32[3]{0:T(128)} %pad_add_fusion.ids_ref.r_1_, bf16[32,80,128]{2,1,0:T(8,128)(2,1)} %bitcast.20, f32[16,128]{1,0:T(8,128)} %get-tuple-element.22.r_3_), custom_call_target="tpu_custom_call" | custom-call | flops 10000000000 | bytes 30000000 | tf_op jit(solution)/shard_map/pallas_call | solution.py:271
  120.6 2.1 %all-to-all-done.5 = bf16[4,128,512]{2,1,0:T(8,128)(2,1)S(1)} async-done(((bf16[4,128,512]{2,1,0:T(8,128)(2,1)}), bf16[4,128,512]{2,1,0:T(8,128)(2,1)S(1)}, u32[]{:S(2)}, u32[]{:S(2)}) %all-to-all-start.5) | async-done | bytes 524320 | tf_op jit(solution)/shard_map/all_to_all | solution.py:285
  122.7 25.0 %all_to_all.44.parts_ref = bf16[16,80,128]{2,1,0:T(8,128)(2,1)} all-to-all(bf16[16,80,128]{2,1,0:T(8,128)(2,1)} %shard_map.80), channel_id=1, replica_groups=mesh['y'=4,'x'=4,'c'=2,'z'=16] {'z'}, dimensions={0} | all-to-all | bytes 655360 | tf_op jit(solution)/shard_map/all_to_all | solution.py:285
  147.6 1.9 %shard_map.81 = bf16[32,80,128]{2,1,0:T(8,128)(2,1)} custom-call(bf16[16,80,128]{2,1,0:T(8,128)(2,1)} %all_to_all.44.parts_ref), custom_call_target="tpu_custom_call" | custom-call | flops 1000000000 | bytes 3000000 | tf_op jit(solution)/shard_map/pallas_call | solution.py:271
  149.5 11.7 %all-to-all-start.7 = ((bf16[32,80,128]{2,1,0:T(8,128)(2,1)}), bf16[32,80,128]{2,1,0:T(8,128)(2,1)S(1)}, u32[]{:S(2)}, u32[]{:S(2)}) async-start(bf16[32,80,128]{2,1,0:T(8,128)(2,1)} %shard_map.81), calls=%async_computation.7 | async-start | bytes 1310720 | tf_op jit(solution)/shard_map/all_to_all | solution.py:285
  162.5 11.7 %all-to-all-done.7.r_0_ = bf16[32,80,128]{2,1,0:T(8,128)(2,1)S(1)} async-done(((bf16[32,80,128]{2,1,0:T(8,128)(2,1)}), bf16[32,80,128]{2,1,0:T(8,128)(2,1)S(1)}, u32[]{:S(2)}, u32[]{:S(2)}) %all-to-all-start.7) | async-done | bytes 655392 | tf_op jit(solution)/shard_map/all_to_all | solution.py:285
  175.0 2.6 %shard_map.82 = bf16[128,2048]{1,0:T(8,128)(2,1)} custom-call(bf16[32,80,128]{2,1,0:T(8,128)(2,1)} %copy-done.1, bf16[128,2048]{1,0:T(8,128)(2,1)} %r_1_.1), custom_call_target="tpu_custom_call" | custom-call | flops 1000000000 | bytes 3000000 | tf_op jit(solution)/shard_map/pallas_call | solution.py:271
  (32 shorter events, 6.2 us)
Async XLA Ops:
  2.1 32.3 %all-to-all-start = ((bf16[16,16,512]{2,1,0:T(8,128)(2,1)}), bf16[16,16,512]{2,1,0:T(8,128)(2,1)S(1)}, u32[]{:S(2)}, u32[]{:S(2)}) async-start(bf16[16,16,512]{2,1,0:T(8,128)(2,1)} %broadcast_in_dim.6), calls=%async_computation | async-start | bytes 524288 | tf_op jit(solution)/shard_map/all_to_all | solution.py:285
  20.5 11.2 %collective-permute-start = (bf16[144,512]{1,0:T(8,128)(2,1)}, bf16[144,512]{1,0:T(8,128)(2,1)S(1)}, u32[]{:S(2)}, u32[]{:S(2)}) collective-permute-start(bf16[144,512]{1,0:T(8,128)(2,1)} %get-tuple-element.16), channel_id=1, source_target_pairs={{0,32},{32,64},{64,96},{96,0},{1,33},{33,65},{65,97},{97,1},{2,34}... | collective-permute-start | bytes 442376 | tf_op jit(solution)/shard_map/ppermute | solution.py:310
  23.6 9.2 %collective-permute-start.1 = (bf16[144,512]{1,0:T(8,128)(2,1)}, bf16[144,512]{1,0:T(8,128)(2,1)S(1)}, u32[]{:S(2)}, u32[]{:S(2)}) collective-permute-start(bf16[144,512]{1,0:T(8,128)(2,1)} %get-tuple-element.17), channel_id=1, source_target_pairs={{0,64},{32,96},{64,0},{96,32},{1,65},{33,97},{65,1},{97,33},{2,66}... | collective-permute-start | bytes 442376 | tf_op jit(solution)/shard_map/ppermute | solution.py:310
  27.9 6.4 %collective-permute-start.2 = (bf16[144,512]{1,0:T(8,128)(2,1)}, bf16[144,512]{1,0:T(8,128)(2,1)S(1)}, u32[]{:S(2)}, u32[]{:S(2)}) collective-permute-start(bf16[144,512]{1,0:T(8,128)(2,1)} %get-tuple-element.18), channel_id=1, source_target_pairs={{0,96},{32,0},{64,32},{96,64},{1,97},{33,1},{65,33},{97,65},{2,98}... | collective-permute-start | bytes 442376 | tf_op jit(solution)/shard_map/ppermute | solution.py:310
  31.7 19.4 %copy-start.3 = (bf16[144,512]{1,0:T(8,128)(2,1)}, bf16[144,512]{1,0:T(8,128)(2,1)S(1)}, u32[]{:S(2)}) copy-start(bf16[144,512]{1,0:T(8,128)(2,1)S(1)} %collective-permute-done.r_3_) | copy-start | bytes 442372
  32.7 18.3 %copy-start.4 = (bf16[144,512]{1,0:T(8,128)(2,1)}, bf16[144,512]{1,0:T(8,128)(2,1)S(1)}, u32[]{:S(2)}) copy-start(bf16[144,512]{1,0:T(8,128)(2,1)S(1)} %collective-permute-done.1.r_4_) | copy-start | bytes 442372
  34.3 16.8 %copy-start.5 = (bf16[144,512]{1,0:T(8,128)(2,1)}, bf16[144,512]{1,0:T(8,128)(2,1)S(1)}, u32[]{:S(2)}) copy-start(bf16[144,512]{1,0:T(8,128)(2,1)S(1)} %collective-permute-done.2.r_5_) | copy-start | bytes 442372
  51.1 9.4 %copy-start = (bf16[4,17,16,512]{3,2,1,0:T(8,128)(2,1)}, bf16[4,17,16,512]{3,2,1,0:T(8,128)(2,1)S(1)}, u32[]{:S(2)}) copy-start(bf16[4,17,16,512]{3,2,1,0:T(8,128)(2,1)S(1)} %all_to_all.40.r_6_) | copy-start | bytes 3342340
  51.1 8.5 %collective-permute-start.3 = (bf16[4,17,16,512]{3,2,1,0:T(8,128)(2,1)S(1)}, bf16[4,17,16,512]{3,2,1,0:T(8,128)(2,1)S(1)}, u32[]{:S(2)}, u32[]{:S(2)}) collective-permute-start(bf16[4,17,16,512]{3,2,1,0:T(8,128)(2,1)S(1)} %all_to_all.40.r_6_), channel_id=1, source_target_pairs={{0,16},{16,0},{1,17},{17,1},{2,18},{18,2},{3,19},{19,3},{4,20},{20... | collective-permute-start | bytes 3342344 | tf_op jit(solution)/shard_map/ppermute | solution.py:316
  59.6 1.0 copy-start.2
  110.6 12.1 %all-to-all-start.5 = ((bf16[4,128,512]{2,1,0:T(8,128)(2,1)}), bf16[4,128,512]{2,1,0:T(8,128)(2,1)S(1)}, u32[]{:S(2)}, u32[]{:S(2)}) async-start(bf16[4,128,512]{2,1,0:T(8,128)(2,1)} %get-tuple-element.23), calls=%async_computation.5 | async-start | bytes 1048576 | tf_op jit(solution)/shard_map/all_to_all | solution.py:285
  149.5 24.7 %all-to-all-start.7 = ((bf16[32,80,128]{2,1,0:T(8,128)(2,1)}), bf16[32,80,128]{2,1,0:T(8,128)(2,1)S(1)}, u32[]{:S(2)}, u32[]{:S(2)}) async-start(bf16[32,80,128]{2,1,0:T(8,128)(2,1)} %shard_map.81), calls=%async_computation.7 | async-start | bytes 1310720 | tf_op jit(solution)/shard_map/all_to_all | solution.py:285
  174.2 0.8 copy-start.1

commit v6 on v5

--- a/solution.py
+++ b/solution.py
@@ -10,7 +10,7 @@
 F32 = jnp.float32
 BF16 = jnp.bfloat16
 NT = (((1,), (1,)), ((), ()))
-VMEM_LIMIT = 56 * 1024 * 1024
+VMEM_LIMIT = 16 * 1024 * 1024
 DP_SPLIT = (4, 4, 2)
 SHARD = 128
 SLOTS = 8
@@ -117,7 +117,7 @@
         scores = []
         outs = [[] for _ in range(width // chunk)]
         for b in range(blocks):
-            base = (ids_ref[0] * nx + s) * 2 * blocks + 2 * b
+            base = s * 2 * blocks + 2 * b
             at_a = shards_ref[base]
             at_b = shards_ref[base + 1]
             part = matrix[b * 32 : (b + 1) * 32]
@@ -167,19 +167,17 @@
             wide = code_matrix(codes_t, sup_t, plain).astype(BF16).astype(F32)
             wide = jnp.transpose(wide * wide)
             for b in range(blocks):
-                base = (ids_ref[0] * nx + s) * 2 * blocks + 2 * b
+                base = s * 2 * blocks + 2 * b
                 squares = jnp.sum(wide[b * 32 : (b + 1) * 32], axis=0, keepdims=True)
                 usage_out[pl.ds(shards_ref[base], 1), :] += squares[:, :128]
                 usage_out[pl.ds(shards_ref[base + 1], 1), :] += squares[:, 128:]
 
 
-def stats_kernel(sizes, shards_ref, ids_ref, msg_ref, usage_ref, out_ref, acc_ref):
-    ny, nx = sizes
+def stats_kernel(nx, shards_ref, ids_ref, msg_ref, usage_ref, out_ref, acc_ref):
     acc_ref[...] = jnp.zeros_like(acc_ref)
     atom = lax.broadcasted_iota(jnp.int32, (256, 128), 0).astype(F32)
     low = lax.broadcasted_iota(jnp.int32, (32, 128), 1) < 64
     low_all = lax.broadcasted_iota(jnp.int32, (128, 128), 1) < 64
-    core = ids_ref[2]
 
     def one(q, carry):
         weights = msg_ref[q, MAIN : MAIN + 16, :].astype(F32)
@@ -189,9 +187,7 @@
                 weights[SLOTS + k : SLOTS + k + 1, :] == atom, weights[k : k + 1, :], matrix
             )
         matrix = matrix.astype(BF16)
-        source = q // nx
-        away = (ids_ref[1] - q) & (nx - 1)
-        base = ((((source & 1) ^ core) * ny + (source >> 1)) * nx + away) * 8
+        base = (q - q % nx + ((ids_ref[1] - q) & (nx - 1))) * 8
         none = jnp.zeros((32, 128), F32)
         for pair in range(2):
             x = msg_ref[q, pair * 32 : pair * 32 + 32, :].astype(F32)
@@ -305,25 +301,28 @@
         [],
         block_shards.T, ids, patches, codes.T, support.T,
     )
-    held = [packed[0]]
-    for j in range(1, nx):
-        held.append(lax.ppermute(packed[j], "x", [(i, (i + j) % nx) for i in range(nx)]))
-    names = jnp.concatenate([h[rows : rows + 1, 256 : 256 + 2 * blocks] for h in held], axis=1)
     own = lax.dynamic_slice(dictionary, ((y * nc + c) * piece, x * width), (piece, width))
     by_z = spread(own, "z", nz).reshape(nz, piece, width)
-    extra = jnp.pad(names, ((0, piece - 1), (0, width - names.shape[1])))
-    mine = spread(jnp.concatenate([by_z, extra[None]], axis=0), "y", ny)
+    def ahead(sent, j):
+        return lax.ppermute(sent, "x", [(i, (i + j) % nx) for i in range(nx)])
+
+    by_z, near, *later = lax.optimization_barrier((by_z, ahead(packed[1], 1), *packed[2:]))
+    mine = spread(by_z, "y", ny)
+    held = [packed[0], near, *(ahead(sent, j + 2) for j, sent in enumerate(later))]
+    mine, *held = lax.optimization_barrier((mine, *held))
     other = lax.ppermute(mine, "c", [(0, 1), (1, 0)])
-    cut = 2 * blocks * nx
-    shards = jnp.concatenate([mine[:, nz, 0, :cut], other[:, nz, 0, :cut]], axis=0)
-    shards = shards.astype(jnp.int32).reshape(-1)
-    common = (shards, ids, *held, mine, other)
+    names = jnp.concatenate([h[rows : rows + 1, 256 : 256 + 2 * blocks] for h in held], axis=1)
+    near_shards = names.astype(jnp.int32).reshape(-1)
+    plane = spread(names, ("y", "c"), ny * nc)
+    common = (near_shards, ids, *held, mine, other)
     sizes = (ny, nx, plen)
     takes = "ss" + "v" * (nx + 2)
     grads = sds((nx, SLOTS, nx * rows), F32)
     first = call(
         lambda *r: refine_kernel(0, sizes, *r), takes, grads, [], *common
     )
+    first, plane = lax.optimization_barrier((first, plane))
+    shards = plane.astype(jnp.int32).reshape(-1)
     second, codes_1 = call(
         lambda *r: refine_kernel(1, sizes, *r),
         takes + "v",
@@ -350,7 +349,7 @@
     got = exchange(msg, ("y", "c")).reshape(ny * nc * nx, MSG, 128)
     at_home = exchange(home, "x")
     to_owner = call(
-        lambda *r: stats_kernel((ny, nx), *r),
+        lambda *r: stats_kernel(nx, *r),
         "ssvv",
         sds((nz, MSG, 128), BF16),
         [pltpu.VMEM((nz * SHARD, 128), F32)],

time: 179 us -> 166 us (0.927)
  blocking collectives: 76.3 us -> 35.5 us
  waiting for transfers between devices: 18.8 us -> 38.9 us
  starting transfers between devices: 47.6 us -> 66.7 us
  Pallas kernels: 28.1 us -> 18.1 us
    all_to_all x5 -> x3, blocking collectives: 76.3 us -> 35.5 us  [exchange(): return lax.all_to_all(x, axes, split_axis=0, concat_axis=0, tiled=True)]
    all_to_all x3 -> x6, waiting for transfers between devices: 13.8 us -> 31.1 us  [exchange(): return lax.all_to_all(x, axes, split_axis=0, concat_axis=0, tiled=True)]
    all_to_all x3 -> x6, starting transfers between devices: 30.9 us -> 46.7 us  [exchange(): return lax.all_to_all(x, axes, split_axis=0, concat_axis=0, tiled=True)]
    pallas_call x7, Pallas kernels: 28.1 us -> 18.1 us  [call(): pl.pallas_call(kernel, out_shape=outs, in_specs=[pl.BlockSpec(memory_spac...]
    ppermute x3, waiting for transfers between devices: 2.63 us -> 7.77 us  [ahead(): return lax.ppermute(sent, 'x', [(i, (i + j) % nx) for i in range(nx)])]
    ppermute x1, starting transfers between devices: 6.16 us -> 9.49 us  [body(): other = lax.ppermute(mine, 'c', [(0, 1), (1, 0)])]
    ppermute x1, waiting for transfers between devices: 2.33 us -> 0.01 us  [body(): other = lax.ppermute(mine, 'c', [(0, 1), (1, 0)])]
  transfers between devices with their start and end apart: 7 -> 10, of which waited for: 5 -> 7; matrix products, arithmetic and copies ran while one was open for 2% -> 1% of each run, Pallas kernels for 5% -> 6%
where the time goes in v6:
time: 166 us
  starting transfers between devices  66.7 us (40%)
  waiting for transfers between devices  38.9 us (23%)
  blocking collectives  35.5 us (21%)
  Pallas kernels  18.1 us (11%)
  local copies, waits for them, and re-layouts  5.24 us (3%)
    all_to_all x6, starting transfers between devices, exchange(): return lax.all_to_all(x, axes, split_axis=0, concat_axis=0, tiled=True)  46.7 us
    all_to_all x3, blocking collectives, exchange(): return lax.all_to_all(x, axes, split_axis=0, concat_axis=0, tiled=True)  35.5 us
    all_to_all x6, waiting for transfers between devices, exchange(): return lax.all_to_all(x, axes, split_axis=0, concat_axis=0, tiled=True)  31.1 us
    pallas_call x7, Pallas kernels, call(): pl.pallas_call(kernel, out_shape=outs, in_specs=[pl.BlockSpec(memory_spac...  18.1 us
    ppermute x3, starting transfers between devices, ahead(): return lax.ppermute(sent, 'x', [(i, (i + j) % nx) for i in range(nx)])  10.5 us
    ppermute x1, starting transfers between devices, body(): other = lax.ppermute(mine, 'c', [(0, 1), (1, 0)])  9.49 us
    ppermute x3, waiting for transfers between devices, ahead(): return lax.ppermute(sent, 'x', [(i, (i + j) % nx) for i in range(nx)])  7.77 us
  transfers between devices with their start and end apart: 10, of which 7 were waited for; matrix products, arithmetic and copies ran while one was open for 1% of the time, Pallas kernels for 6%

profile of v6, /device:TPU:1, one launch (start us, length us, event | category | flops | bytes accessed | tf_op | source)
XLA Modules:
  0.0 165.6 jit_solution(18070439655700283292)
XLA Ops:
  2.1 15.7 %all-to-all-start = ((bf16[16,16,512]{2,1,0:T(8,128)(2,1)}), bf16[16,16,512]{2,1,0:T(8,128)(2,1)S(1)}, u32[]{:S(2)}, u32[]{:S(2)}) async-start(bf16[16,16,512]{2,1,0:T(8,128)(2,1)} %broadcast_in_dim.8), calls=%async_computation | async-start | bytes 524288 | tf_op jit(solution)/shard_map/all_to_all | solution.py:281
  19.2 3.1 %collective-permute-start = (bf16[144,512]{1,0:T(8,128)(2,1)S(1)}, bf16[144,512]{1,0:T(8,128)(2,1)S(1)}, u32[]{:S(2)}, u32[]{:S(2)}) collective-permute-start(bf16[144,512]{1,0:T(8,128)(2,1)S(1)} %get-tuple-element.26), channel_id=1, source_target_pairs={{0,32},{32,64},{64,96},{96,0},{1,33},{33,65},{65,97},{97,1},{2,34}... | collective-permute-start | bytes 442376 | tf_op jit(solution)/shard_map/ppermute | solution.py:307
  22.4 4.4 %collective-permute-done.r_3_ = bf16[144,512]{1,0:T(8,128)(2,1)S(1)} collective-permute-done((bf16[144,512]{1,0:T(8,128)(2,1)S(1)}, bf16[144,512]{1,0:T(8,128)(2,1)S(1)}, u32[]{:S(2)}, u32[]{:S(2)}) %collective-permute-start) | collective-permute-done | bytes 147488 | tf_op jit(solution)/shard_map/ppermute | solution.py:307
  26.7 4.2 %all-to-all-done = bf16[16,16,512]{2,1,0:T(8,128)(2,1)S(1)} async-done(((bf16[16,16,512]{2,1,0:T(8,128)(2,1)}), bf16[16,16,512]{2,1,0:T(8,128)(2,1)S(1)}, u32[]{:S(2)}, u32[]{:S(2)}) %all-to-all-start) | async-done | bytes 262176 | tf_op jit(solution)/shard_map/all_to_all | solution.py:281
  32.1 4.2 %all-to-all-start.1 = ((bf16[4,16,16,512]{3,2,1,0:T(8,128)(2,1)}), bf16[4,16,16,512]{3,2,1,0:T(8,128)(2,1)S(1)}, u32[]{:S(2)}, u32[]{:S(2)}) async-start(bf16[4,16,16,512]{3,2,1,0:T(8,128)(2,1)} %broadcast_in_dim.9), calls=%async_computation.1 | async-start | bytes 2097152 | tf_op jit(solution)/shard_map/all_to_all | solution.py:281
  36.3 4.6 %collective-permute-start.1 = (bf16[144,512]{1,0:T(8,128)(2,1)S(1)}, bf16[144,512]{1,0:T(8,128)(2,1)S(1)}, u32[]{:S(2)}, u32[]{:S(2)}) collective-permute-start(bf16[144,512]{1,0:T(8,128)(2,1)S(1)} %get-tuple-element.32), channel_id=1, source_target_pairs={{0,64},{32,96},{64,0},{96,32},{1,65},{33,97},{65,1},{97,33},{2,66}... | collective-permute-start | bytes 442376 | tf_op jit(solution)/shard_map/ppermute | solution.py:307
  40.9 2.8 %collective-permute-start.2 = (bf16[144,512]{1,0:T(8,128)(2,1)S(1)}, bf16[144,512]{1,0:T(8,128)(2,1)S(1)}, u32[]{:S(2)}, u32[]{:S(2)}) collective-permute-start(bf16[144,512]{1,0:T(8,128)(2,1)S(1)} %get-tuple-element.33), channel_id=1, source_target_pairs={{0,96},{32,0},{64,32},{96,64},{1,97},{33,1},{65,33},{97,65},{2,98}... | collective-permute-start | bytes 442376 | tf_op jit(solution)/shard_map/ppermute | solution.py:307
  43.7 3.4 %collective-permute-done.2.r_5_ = bf16[144,512]{1,0:T(8,128)(2,1)S(1)} collective-permute-done((bf16[144,512]{1,0:T(8,128)(2,1)S(1)}, bf16[144,512]{1,0:T(8,128)(2,1)S(1)}, u32[]{:S(2)}, u32[]{:S(2)}) %collective-permute-start.2) | collective-permute-done | bytes 147488 | tf_op jit(solution)/shard_map/ppermute | solution.py:307
  47.1 9.5 %collective-permute-start.3 = (bf16[4,16,16,512]{3,2,1,0:T(8,128)(2,1)S(1)}, bf16[4,16,16,512]{3,2,1,0:T(8,128)(2,1)S(1)}, u32[]{:S(2)}, u32[]{:S(2)}) collective-permute-start(bf16[4,16,16,512]{3,2,1,0:T(8,128)(2,1)S(1)} %all-to-all-done.1.r_6_), channel_id=1, source_target_pairs={{0,16},{16,0},{1,17},{17,1},{2,18},{18,2},{3,19},{19,3},{4,20},{20... | collective-permute-start | bytes 3145736 | tf_op jit(solution)/shard_map/ppermute | solution.py:313
  57.3 4.9 %all-to-all-start.2 = ((bf16[8,1,32]{2,1,0:T(2,128)(2,1)}), bf16[8,1,32]{2,1,0:T(2,128)(2,1)S(1)}, u32[]{:S(2)}, u32[]{:S(2)}) async-start(bf16[8,1,32]{2,1,0:T(2,128)(2,1)} %broadcast_in_dim.11), calls=%async_computation.2 | async-start | bytes 8192 | tf_op jit(solution)/shard_map/all_to_all | solution.py:281
  62.3 3.4 %shard_map.77 = f32[4,8,512]{2,1,0:T(8,128)S(1)} custom-call(s32[32]{0:T(128)S(1)} %maximum_convert_fusion.r_0_, s32[3]{0:T(128)S(1)} %pad_add_fusion.ids_ref.r_1_, bf16[144,512]{1,0:T(8,128)(2,1)S(1)} %get-tuple-element.34.r_2_, bf16[144,512]{1,0:T(8,128)(2,1)S(1)} %collective-permute-done.r_3_, bf16[144,512]{1,0:T(8,128)(2,1)S(1)} %collective-permute-done.1.r_4_, ...), custom_call_target="tpu_custom_call" | custom-call | flops 1000000000 | bytes 3000000 | tf_op jit(solution)/shard_map/pallas_call | solution.py:267
  66.8 7.6 %all_to_all.45.r_8_ = f32[4,8,512]{2,1,0:T(8,128)S(1)} all-to-all(f32[4,8,512]{2,1,0:T(8,128)S(1)} %shard_map.77), channel_id=1, replica_groups=mesh['y'=4,'x'=4,'c'=2,'z'=16] {'x'}, dimensions={0} | all-to-all | bytes 131072 | tf_op jit(solution)/shard_map/all_to_all | solution.py:281
  74.4 3.4 %shard_map.78 = (f32[4,8,512]{2,1,0:T(8,128)S(1)}, f32[8,512]{1,0:T(8,128)S(1)}) custom-call(s32[32]{0:T(128)S(1)} %maximum_convert_fusion.r_0_, s32[3]{0:T(128)S(1)} %pad_add_fusion.ids_ref.r_1_, bf16[144,512]{1,0:T(8,128)(2,1)S(1)} %get-tuple-element.34.r_2_, bf16[144,512]{1,0:T(8,128)(2,1)S(1)} %collective-permute-done.r_3_, ...), custom_call_target="tpu_custom_call" | custom-call | flops 1000000000 | bytes 3000000 | tf_op jit(solution)/shard_map/pallas_call | solution.py:267
  77.7 6.8 %all_to_all.46.r_8_ = f32[4,8,512]{2,1,0:T(8,128)S(1)} all-to-all(f32[4,8,512]{2,1,0:T(8,128)S(1)} %get-tuple-element.41), channel_id=1, replica_groups=mesh['y'=4,'x'=4,'c'=2,'z'=16] {'x'}, dimensions={0} | all-to-all | bytes 131072 | tf_op jit(solution)/shard_map/all_to_all | solution.py:281
  84.6 3.2 %shard_map.79 = (bf16[4,128,512]{2,1,0:T(8,128)(2,1)}, bf16[8,4,80,128]{3,2,1,0:T(8,128)(2,1)}, f32[16,128]{1,0:T(8,128)S(1)}, f32[8,128]{1,0:T(8,128)}) custom-call(s32[32]{0:T(128)S(1)} %maximum_convert_fusion.r_0_, s32[3]{0:T(128)S(1)} %pad_add_fusion.ids_ref.r_1_, bf16[144,512]{1,0:T(8,128)(2,1)S(1)} %get-tuple-element.34.r_2_, ...), custom_call_target="tpu_custom_call" | custom-call | flops 1000000000 | bytes 3000000 | tf_op jit(solution)/shard_map/pallas_call | solution.py:267
  87.8 6.7 %all-to-all-start.5 = ((bf16[8,4,80,128]{3,2,1,0:T(8,128)(2,1)}), bf16[8,4,80,128]{3,2,1,0:T(8,128)(2,1)S(1)}, u32[]{:S(2)}, u32[]{:S(2)}) async-start(bf16[8,4,80,128]{3,2,1,0:T(8,128)(2,1)} %get-tuple-element.43), calls=%async_computation.5 | async-start | bytes 1310720 | tf_op jit(solution)/shard_map/all_to_all | solution.py:281
  94.6 10.8 %all-to-all-done.5 = bf16[8,4,80,128]{3,2,1,0:T(8,128)(2,1)S(1)} async-done(((bf16[8,4,80,128]{3,2,1,0:T(8,128)(2,1)}), bf16[8,4,80,128]{3,2,1,0:T(8,128)(2,1)S(1)}, u32[]{:S(2)}, u32[]{:S(2)}) %all-to-all-start.5) | async-done | bytes 655392 | tf_op jit(solution)/shard_map/all_to_all | solution.py:281
  105.4 3.5 %all-to-all-start.6 = ((bf16[4,128,512]{2,1,0:T(8,128)(2,1)}), bf16[4,128,512]{2,1,0:T(8,128)(2,1)S(1)}, u32[]{:S(2)}, u32[]{:S(2)}) async-start(bf16[4,128,512]{2,1,0:T(8,128)(2,1)} %get-tuple-element.45), calls=%async_computation.6 | async-start | bytes 1048576 | tf_op jit(solution)/shard_map/all_to_all | solution.py:281
  108.9 5.3 %shard_map.80 = bf16[16,80,128]{2,1,0:T(8,128)(2,1)S(1)} custom-call(s32[256]{0:T(256)S(1)} %reshape.49.r_0_, s32[3]{0:T(128)S(1)} %pad_add_fusion.ids_ref.r_1_, bf16[32,80,128]{2,1,0:T(8,128)(2,1)S(1)} %bitcast.20, f32[16,128]{1,0:T(8,128)S(1)} %get-tuple-element.44.r_3_), custom_call_target="tpu_custom_call" | custom-call | flops 10000000000 | bytes 30000000 | tf_op jit(solution)/shard_map/pallas_call | solution.py:267
  114.2 3.3 %all-to-all-done.6 = bf16[4,128,512]{2,1,0:T(8,128)(2,1)S(1)} async-done(((bf16[4,128,512]{2,1,0:T(8,128)(2,1)}), bf16[4,128,512]{2,1,0:T(8,128)(2,1)S(1)}, u32[]{:S(2)}, u32[]{:S(2)}) %all-to-all-start.6) | async-done | bytes 524320 | tf_op jit(solution)/shard_map/all_to_all | solution.py:281
  117.5 21.1 %all_to_all.47.parts_ref = bf16[16,80,128]{2,1,0:T(8,128)(2,1)S(1)} all-to-all(bf16[16,80,128]{2,1,0:T(8,128)(2,1)S(1)} %shard_map.80), channel_id=1, replica_groups=mesh['y'=4,'x'=4,'c'=2,'z'=16] {'z'}, dimensions={0} | all-to-all | bytes 655360 | tf_op jit(solution)/shard_map/all_to_all | solution.py:281
  139.5 11.6 %all-to-all-start.8 = ((bf16[32,80,128]{2,1,0:T(8,128)(2,1)}), bf16[32,80,128]{2,1,0:T(8,128)(2,1)S(1)}, u32[]{:S(2)}, u32[]{:S(2)}) async-start(bf16[32,80,128]{2,1,0:T(8,128)(2,1)} %shard_map.81), calls=%async_computation.8 | async-start | bytes 1310720 | tf_op jit(solution)/shard_map/all_to_all | solution.py:281
  152.5 11.7 %all-to-all-done.8.r_0_ = bf16[32,80,128]{2,1,0:T(8,128)(2,1)S(1)} async-done(((bf16[32,80,128]{2,1,0:T(8,128)(2,1)}), bf16[32,80,128]{2,1,0:T(8,128)(2,1)S(1)}, u32[]{:S(2)}, u32[]{:S(2)}) %all-to-all-start.8) | async-done | bytes 655392 | tf_op jit(solution)/shard_map/all_to_all | solution.py:281
  164.2 1.4 shard_map.82
  (30 shorter events, 8.1 us)
Async XLA Ops:
  0.6 0.7 dynamic-slice-start
  0.7 17.3 %copy-start.1 = (bf16[128,2048]{1,0:T(8,128)(2,1)S(1)}, bf16[128,2048]{1,0:T(8,128)(2,1)}, u32[]{:S(2)}) copy-start(bf16[128,2048]{1,0:T(8,128)(2,1)} %x_ref.1) | copy-start | bytes 1572868
  2.1 28.9 %all-to-all-start = ((bf16[16,16,512]{2,1,0:T(8,128)(2,1)}), bf16[16,16,512]{2,1,0:T(8,128)(2,1)S(1)}, u32[]{:S(2)}, u32[]{:S(2)}) async-start(bf16[16,16,512]{2,1,0:T(8,128)(2,1)} %broadcast_in_dim.8), calls=%async_computation | async-start | bytes 524288 | tf_op jit(solution)/shard_map/all_to_all | solution.py:281
  17.8 0.7 copy-start.3
  17.9 0.7 copy-start.2
  18.0 0.7 copy-start.4
  19.2 7.5 %collective-permute-start = (bf16[144,512]{1,0:T(8,128)(2,1)S(1)}, bf16[144,512]{1,0:T(8,128)(2,1)S(1)}, u32[]{:S(2)}, u32[]{:S(2)}) collective-permute-start(bf16[144,512]{1,0:T(8,128)(2,1)S(1)} %get-tuple-element.26), channel_id=1, source_target_pairs={{0,32},{32,64},{64,96},{96,0},{1,33},{33,65},{65,97},{97,1},{2,34}... | collective-permute-start | bytes 442376 | tf_op jit(solution)/shard_map/ppermute | solution.py:307
  32.1 15.0 %all-to-all-start.1 = ((bf16[4,16,16,512]{3,2,1,0:T(8,128)(2,1)}), bf16[4,16,16,512]{3,2,1,0:T(8,128)(2,1)S(1)}, u32[]{:S(2)}, u32[]{:S(2)}) async-start(bf16[4,16,16,512]{3,2,1,0:T(8,128)(2,1)} %broadcast_in_dim.9), calls=%async_computation.1 | async-start | bytes 2097152 | tf_op jit(solution)/shard_map/all_to_all | solution.py:281
  36.3 7.4 %collective-permute-start.1 = (bf16[144,512]{1,0:T(8,128)(2,1)S(1)}, bf16[144,512]{1,0:T(8,128)(2,1)S(1)}, u32[]{:S(2)}, u32[]{:S(2)}) collective-permute-start(bf16[144,512]{1,0:T(8,128)(2,1)S(1)} %get-tuple-element.32), channel_id=1, source_target_pairs={{0,64},{32,96},{64,0},{96,32},{1,65},{33,97},{65,1},{97,33},{2,66}... | collective-permute-start | bytes 442376 | tf_op jit(solution)/shard_map/ppermute | solution.py:307
  40.9 6.2 %collective-permute-start.2 = (bf16[144,512]{1,0:T(8,128)(2,1)S(1)}, bf16[144,512]{1,0:T(8,128)(2,1)S(1)}, u32[]{:S(2)}, u32[]{:S(2)}) collective-permute-start(bf16[144,512]{1,0:T(8,128)(2,1)S(1)} %get-tuple-element.33), channel_id=1, source_target_pairs={{0,96},{32,0},{64,32},{96,64},{1,97},{33,1},{65,33},{97,65},{2,98}... | collective-permute-start | bytes 442376 | tf_op jit(solution)/shard_map/ppermute | solution.py:307
  47.1 15.2 %collective-permute-start.3 = (bf16[4,16,16,512]{3,2,1,0:T(8,128)(2,1)S(1)}, bf16[4,16,16,512]{3,2,1,0:T(8,128)(2,1)S(1)}, u32[]{:S(2)}, u32[]{:S(2)}) collective-permute-start(bf16[4,16,16,512]{3,2,1,0:T(8,128)(2,1)S(1)} %all-to-all-done.1.r_6_), channel_id=1, source_target_pairs={{0,16},{16,0},{1,17},{17,1},{2,18},{18,2},{3,19},{19,3},{4,20},{20... | collective-permute-start | bytes 3145736 | tf_op jit(solution)/shard_map/ppermute | solution.py:313
  57.3 9.4 %all-to-all-start.2 = ((bf16[8,1,32]{2,1,0:T(2,128)(2,1)}), bf16[8,1,32]{2,1,0:T(2,128)(2,1)S(1)}, u32[]{:S(2)}, u32[]{:S(2)}) async-start(bf16[8,1,32]{2,1,0:T(2,128)(2,1)} %broadcast_in_dim.11), calls=%async_computation.2 | async-start | bytes 8192 | tf_op jit(solution)/shard_map/all_to_all | solution.py:281
  87.8 17.6 %all-to-all-start.5 = ((bf16[8,4,80,128]{3,2,1,0:T(8,128)(2,1)}), bf16[8,4,80,128]{3,2,1,0:T(8,128)(2,1)S(1)}, u32[]{:S(2)}, u32[]{:S(2)}) async-start(bf16[8,4,80,128]{3,2,1,0:T(8,128)(2,1)} %get-tuple-element.43), calls=%async_computation.5 | async-start | bytes 1310720 | tf_op jit(solution)/shard_map/all_to_all | solution.py:281
  105.4 12.1 %all-to-all-start.6 = ((bf16[4,128,512]{2,1,0:T(8,128)(2,1)}), bf16[4,128,512]{2,1,0:T(8,128)(2,1)S(1)}, u32[]{:S(2)}, u32[]{:S(2)}) async-start(bf16[4,128,512]{2,1,0:T(8,128)(2,1)} %get-tuple-element.45), calls=%async_computation.6 | async-start | bytes 1048576 | tf_op jit(solution)/shard_map/all_to_all | solution.py:281
  139.5 24.7 %all-to-all-start.8 = ((bf16[32,80,128]{2,1,0:T(8,128)(2,1)}), bf16[32,80,128]{2,1,0:T(8,128)(2,1)S(1)}, u32[]{:S(2)}, u32[]{:S(2)}) async-start(bf16[32,80,128]{2,1,0:T(8,128)(2,1)} %shard_map.81), calls=%async_computation.8 | async-start | bytes 1310720 | tf_op jit(solution)/shard_map/all_to_all | solution.py:281
  151.5 12.7 %copy-start = (bf16[128,2048]{1,0:T(8,128)(2,1)S(1)}, bf16[128,2048]{1,0:T(8,128)(2,1)}, u32[]{:S(2)}) copy-start(bf16[128,2048]{1,0:T(8,128)(2,1)} %r_1_.1) | copy-start | bytes 1572868

commit v7 on v6

--- a/solution.py
+++ b/solution.py
@@ -93,7 +93,7 @@
     elif step == 1:
         parts_ref, grad_out, codes_out = refs
     else:
-        parts_ref, codes_ref, home_out, msg_out, usage_out, codes_out = refs
+        parts_ref, codes_ref, *home_outs, msg_out, usage_out, codes_out = refs
     low = lax.broadcasted_iota(jnp.int32, (MAIN, 128), 1) < 64
     for s in range(nx):
         source = (ids_ref[1] - s) & (nx - 1)
@@ -150,7 +150,7 @@
         side_t = jnp.concatenate([merged_t, sup_t], axis=0).astype(BF16)
         for j in range(width // chunk):
             full = jnp.concatenate(outs[j], axis=0)
-            home_out[source, :, j * chunk : (j + 1) * chunk] = full
+            home_outs[s][:, j * chunk : (j + 1) * chunk] = full
             for t in range(chunk // 128):
                 u = (j * chunk) // 128 + t
                 tile = full[:, t * 128 : (t + 1) * 128].astype(F32)
@@ -233,6 +233,14 @@
     for q in range(out_ref.shape[0]):
         out_ref[q, :MAIN, :] = main
         out_ref[q, MAIN:, :] = side
+
+
+def home_kernel(ids_ref, *refs):
+    *parts, out_ref = refs
+    width = parts[0].shape[1]
+    for j, part in enumerate(parts):
+        start = pl.multiple_of(((ids_ref[1] + j) & (len(parts) - 1)) * width, 128)
+        out_ref[:, pl.ds(start, width)] = part[...]
 
 
 def renew_kernel(sizes, parts_ref, dict_ref, out_ref, moved_ref):
@@ -306,9 +314,13 @@
     def ahead(sent, j):
         return lax.ppermute(sent, "x", [(i, (i + j) % nx) for i in range(nx)])
 
-    by_z, near, *later = lax.optimization_barrier((by_z, ahead(packed[1], 1), *packed[2:]))
+    held = [packed[0]] + [None if j == nx // 2 else ahead(packed[j], j) for j in range(1, nx)]
+    by_z, far, *near = lax.optimization_barrier(
+        (by_z, packed[nx // 2], *(h for h in held[1:] if h is not None))
+    )
     mine = spread(by_z, "y", ny)
-    held = [packed[0], near, *(ahead(sent, j + 2) for j, sent in enumerate(later))]
+    near.insert(nx // 2 - 1, ahead(far, nx // 2))
+    held = [packed[0], *near]
     mine, *held = lax.optimization_barrier((mine, *held))
     other = lax.ppermute(mine, "c", [(0, 1), (1, 0)])
     names = jnp.concatenate([h[rows : rows + 1, 256 : 256 + 2 * blocks] for h in held], axis=1)
@@ -331,11 +343,11 @@
         *common,
         exchange(first, "x"),
     )
-    home, msg, usage, codes_2 = call(
+    *home, msg, usage, codes_2 = call(
         lambda *r: refine_kernel(2, sizes, *r),
         takes + "vv",
         (
-            sds((nx, rows, width), BF16),
+            *(sds((rows, width), BF16) for _ in range(nx)),
             sds((ny * nc, nx, MSG, 128), BF16),
             sds((nz, 128), F32),
             sds((SLOTS, rows), F32),
@@ -347,7 +359,6 @@
     )
     new_codes = codes_2.T
     got = exchange(msg, ("y", "c")).reshape(ny * nc * nx, MSG, 128)
-    at_home = exchange(home, "x")
     to_owner = call(
         lambda *r: stats_kernel(nx, *r),
         "ssvv",
@@ -355,15 +366,14 @@
         [pltpu.VMEM((nz * SHARD, 128), F32)],
         shards, ids, got, usage, us=10,
     )
-    to_owner, at_home = lax.optimization_barrier((to_owner, at_home))
-    resid = jnp.transpose(at_home, (1, 0, 2)).reshape(rows, plen)
-    final = call(
-        total_kernel,
-        "v",
-        sds((ny * nx * nc, MSG, 128), BF16),
-        [],
-        exchange(to_owner, "z"),
-    )
+    to_owner, *home = lax.optimization_barrier((to_owner, *home))
+    at_owner = exchange(to_owner, "z")
+    home = [home[0]] + [
+        lax.ppermute(home[j], "x", [(i, (i - j) % nx) for i in range(nx)]) for j in range(1, nx)
+    ]
+    at_owner, *home = lax.optimization_barrier((at_owner, *home))
+    final = call(total_kernel, "v", sds((ny * nx * nc, MSG, 128), BF16), [], at_owner)
+    resid = call(home_kernel, "s" + "v" * nx, sds((rows, plen), BF16), [], ids, *home)
     new_dictionary = call(
         lambda *r: renew_kernel((ny, nx), *r),
         "vv",

time: 166 us -> 160 us (0.964)
  blocking collectives: 35.5 us -> 15.1 us
  starting transfers between devices: 66.7 us -> 78.3 us
  Pallas kernels: 18.1 us -> 20.2 us
  waiting for transfers between devices: 38.9 us -> 40.7 us
    all_to_all x3 -> x2, blocking collectives: 35.5 us -> 15.1 us  [exchange(): return lax.all_to_all(x, axes, split_axis=0, concat_axis=0, tiled=True)]
    ppermute x0 -> x3, starting transfers between devices: none -> 7.81 us  [body(): lax.ppermute(home[j], 'x', [(i, (i - j) % nx) for i in range(nx)])]
    ppermute x0 -> x3, waiting for transfers between devices: none -> 5.77 us  [body(): lax.ppermute(home[j], 'x', [(i, (i - j) % nx) for i in range(nx)])]
    all_to_all x6, starting transfers between devices: 46.7 us -> 49.9 us  [exchange(): return lax.all_to_all(x, axes, split_axis=0, concat_axis=0, tiled=True)]
    ppermute x3, waiting for transfers between devices: 7.77 us -> 5.53 us  [ahead(): return lax.ppermute(sent, 'x', [(i, (i + j) % nx) for i in range(nx)])]
    pallas_call x7 -> x8, Pallas kernels: 18.1 us -> 20.2 us  [call(): pl.pallas_call(kernel, out_shape=outs, in_specs=[pl.BlockSpec(memory_spac...]
    all_to_all x6, waiting for transfers between devices: 31.1 us -> 29.4 us  [exchange(): return lax.all_to_all(x, axes, split_axis=0, concat_axis=0, tiled=True)]
  transfers between devices with their start and end apart: 10 -> 13, of which waited for: 7 -> 11; matrix products, arithmetic and copies ran while one was open for 1% -> 1% of each run, Pallas kernels for 6% -> 3%
where the time goes in v7:
time: 160 us; the launch traced here: 159 us
  starting transfers between devices  78.3 us (49%)
  waiting for transfers between devices  40.7 us (25%)
  Pallas kernels  20.2 us (13%)
  blocking collectives  15.1 us (9%)
  local copies, waits for them, and re-layouts  3.96 us (2%)
    all_to_all x6, starting transfers between devices, exchange(): return lax.all_to_all(x, axes, split_axis=0, concat_axis=0, tiled=True)  49.9 us
    all_to_all x6, waiting for transfers between devices, exchange(): return lax.all_to_all(x, axes, split_axis=0, concat_axis=0, tiled=True)  29.4 us
    pallas_call x8, Pallas kernels, call(): pl.pallas_call(kernel, out_shape=outs, in_specs=[pl.BlockSpec(memory_spac...  20.2 us
    all_to_all x2, blocking collectives, exchange(): return lax.all_to_all(x, axes, split_axis=0, concat_axis=0, tiled=True)  15.1 us
    ppermute x3, starting transfers between devices, ahead(): return lax.ppermute(sent, 'x', [(i, (i + j) % nx) for i in range(nx)])  11.1 us
    ppermute x1, starting transfers between devices, body(): other = lax.ppermute(mine, 'c', [(0, 1), (1, 0)])  9.51 us
    ppermute x3, starting transfers between devices, body(): lax.ppermute(home[j], 'x', [(i, (i - j) % nx) for i in range(nx)])  7.81 us
    ppermute x3, waiting for transfers between devices, body(): lax.ppermute(home[j], 'x', [(i, (i - j) % nx) for i in range(nx)])  5.77 us
  transfers between devices with their start and end apart: 13, of which 11 were waited for; matrix products, arithmetic and copies ran while one was open for 1% of the time, Pallas kernels for 3%

profile of v7, /device:TPU:1, one launch (start us, length us, event | category | flops | bytes accessed | tf_op | source)
XLA Modules:
  0.0 159.4 jit_solution(528116636726975768)
XLA Ops:
  2.1 15.7 %all-to-all-start = ((bf16[16,16,512]{2,1,0:T(8,128)(2,1)}), bf16[16,16,512]{2,1,0:T(8,128)(2,1)S(1)}, u32[]{:S(2)}, u32[]{:S(2)}) async-start(bf16[16,16,512]{2,1,0:T(8,128)(2,1)} %broadcast_in_dim.8), calls=%async_computation | async-start | bytes 524288 | tf_op jit(solution)/shard_map/all_to_all | solution.py:289
  19.2 3.1 %collective-permute-start = (bf16[144,512]{1,0:T(8,128)(2,1)S(1)}, bf16[144,512]{1,0:T(8,128)(2,1)S(1)}, u32[]{:S(2)}, u32[]{:S(2)}) collective-permute-start(bf16[144,512]{1,0:T(8,128)(2,1)S(1)} %get-tuple-element.38), channel_id=1, source_target_pairs={{0,32},{32,64},{64,96},{96,0},{1,33},{33,65},{65,97},{97,1},{2,34}... | collective-permute-start | bytes 442376 | tf_op jit(solution)/shard_map/ppermute | solution.py:315
  22.4 3.4 %collective-permute-start.1 = (bf16[144,512]{1,0:T(8,128)(2,1)S(1)}, bf16[144,512]{1,0:T(8,128)(2,1)S(1)}, u32[]{:S(2)}, u32[]{:S(2)}) collective-permute-start(bf16[144,512]{1,0:T(8,128)(2,1)S(1)} %get-tuple-element.39), channel_id=1, source_target_pairs={{0,96},{32,0},{64,32},{96,64},{1,97},{33,1},{65,33},{97,65},{2,98}... | collective-permute-start | bytes 442376 | tf_op jit(solution)/shard_map/ppermute | solution.py:315
  28.5 2.4 %all-to-all-done = bf16[16,16,512]{2,1,0:T(8,128)(2,1)S(1)} async-done(((bf16[16,16,512]{2,1,0:T(8,128)(2,1)}), bf16[16,16,512]{2,1,0:T(8,128)(2,1)S(1)}, u32[]{:S(2)}, u32[]{:S(2)}) %all-to-all-start) | async-done | bytes 262176 | tf_op jit(solution)/shard_map/all_to_all | solution.py:289
  32.1 4.2 %all-to-all-start.1 = ((bf16[4,16,16,512]{3,2,1,0:T(8,128)(2,1)}), bf16[4,16,16,512]{3,2,1,0:T(8,128)(2,1)S(1)}, u32[]{:S(2)}, u32[]{:S(2)}) async-start(bf16[4,16,16,512]{3,2,1,0:T(8,128)(2,1)} %broadcast_in_dim.9), calls=%async_computation.1 | async-start | bytes 2097152 | tf_op jit(solution)/shard_map/all_to_all | solution.py:289
  36.3 4.6 %collective-permute-start.2 = (bf16[144,512]{1,0:T(8,128)(2,1)S(1)}, bf16[144,512]{1,0:T(8,128)(2,1)S(1)}, u32[]{:S(2)}, u32[]{:S(2)}) collective-permute-start(bf16[144,512]{1,0:T(8,128)(2,1)S(1)} %get-tuple-element.43), channel_id=1, source_target_pairs={{0,64},{32,96},{64,0},{96,32},{1,65},{33,97},{65,1},{97,33},{2,66}... | collective-permute-start | bytes 442376 | tf_op jit(solution)/shard_map/ppermute | solution.py:315
  41.0 2.7 %collective-permute-done.2.r_4_ = bf16[144,512]{1,0:T(8,128)(2,1)S(1)} collective-permute-done((bf16[144,512]{1,0:T(8,128)(2,1)S(1)}, bf16[144,512]{1,0:T(8,128)(2,1)S(1)}, u32[]{:S(2)}, u32[]{:S(2)}) %collective-permute-start.2) | collective-permute-done | bytes 147488 | tf_op jit(solution)/shard_map/ppermute | solution.py:315
  43.7 2.4 %all-to-all-done.1.r_6_ = bf16[4,16,16,512]{3,2,1,0:T(8,128)(2,1)S(1)} async-done(((bf16[4,16,16,512]{3,2,1,0:T(8,128)(2,1)}), bf16[4,16,16,512]{3,2,1,0:T(8,128)(2,1)S(1)}, u32[]{:S(2)}, u32[]{:S(2)}) %all-to-all-start.1) | async-done | bytes 1048608 | tf_op jit(solution)/shard_map/all_to_all | solution.py:289
  46.1 9.5 %collective-permute-start.3 = (bf16[4,16,16,512]{3,2,1,0:T(8,128)(2,1)S(1)}, bf16[4,16,16,512]{3,2,1,0:T(8,128)(2,1)S(1)}, u32[]{:S(2)}, u32[]{:S(2)}) collective-permute-start(bf16[4,16,16,512]{3,2,1,0:T(8,128)(2,1)S(1)} %all-to-all-done.1.r_6_), channel_id=1, source_target_pairs={{0,16},{16,0},{1,17},{17,1},{2,18},{18,2},{3,19},{19,3},{4,20},{20... | collective-permute-start | bytes 3145736 | tf_op jit(solution)/shard_map/ppermute | solution.py:325
  56.3 3.3 %all-to-all-start.2 = ((bf16[8,1,32]{2,1,0:T(2,128)(2,1)}), bf16[8,1,32]{2,1,0:T(2,128)(2,1)S(1)}, u32[]{:S(2)}, u32[]{:S(2)}) async-start(bf16[8,1,32]{2,1,0:T(2,128)(2,1)} %broadcast_in_dim.11), calls=%async_computation.2 | async-start | bytes 8192 | tf_op jit(solution)/shard_map/all_to_all | solution.py:289
  59.6 3.4 %shard_map.77 = f32[4,8,512]{2,1,0:T(8,128)S(1)} custom-call(s32[32]{0:T(128)S(1)} %maximum_convert_fusion.r_0_, s32[3]{0:T(128)S(1)} %pad_add_fusion.ids_ref.r_1_, bf16[144,512]{1,0:T(8,128)(2,1)S(1)} %get-tuple-element.45.r_2_, bf16[144,512]{1,0:T(8,128)(2,1)S(1)} %collective-permute-done.r_3_, bf16[144,512]{1,0:T(8,128)(2,1)S(1)} %collective-permute-done.2.r_4_, ...), custom_call_target="tpu_custom_call" | custom-call | flops 1000000000 | bytes 3000000 | tf_op jit(solution)/shard_map/pallas_call | solution.py:275
  64.0 8.3 %all_to_all.40.r_8_ = f32[4,8,512]{2,1,0:T(8,128)S(1)} all-to-all(f32[4,8,512]{2,1,0:T(8,128)S(1)} %shard_map.77), channel_id=1, replica_groups=mesh['y'=4,'x'=4,'c'=2,'z'=16] {'x'}, dimensions={0} | all-to-all | bytes 131072 | tf_op jit(solution)/shard_map/all_to_all | solution.py:289
  72.3 3.4 %shard_map.78 = (f32[4,8,512]{2,1,0:T(8,128)S(1)}, f32[8,512]{1,0:T(8,128)S(1)}) custom-call(s32[32]{0:T(128)S(1)} %maximum_convert_fusion.r_0_, s32[3]{0:T(128)S(1)} %pad_add_fusion.ids_ref.r_1_, bf16[144,512]{1,0:T(8,128)(2,1)S(1)} %get-tuple-element.45.r_2_, bf16[144,512]{1,0:T(8,128)(2,1)S(1)} %collective-permute-done.r_3_, ...), custom_call_target="tpu_custom_call" | custom-call | flops 1000000000 | bytes 3000000 | tf_op jit(solution)/shard_map/pallas_call | solution.py:275
  75.7 6.8 %all_to_all.41.r_8_ = f32[4,8,512]{2,1,0:T(8,128)S(1)} all-to-all(f32[4,8,512]{2,1,0:T(8,128)S(1)} %get-tuple-element.52), channel_id=1, replica_groups=mesh['y'=4,'x'=4,'c'=2,'z'=16] {'x'}, dimensions={0} | all-to-all | bytes 131072 | tf_op jit(solution)/shard_map/all_to_all | solution.py:289
  82.5 3.1 %shard_map.79 = (bf16[128,512]{1,0:T(8,128)(2,1)S(1)}, bf16[128,512]{1,0:T(8,128)(2,1)S(1)}, bf16[128,512]{1,0:T(8,128)(2,1)S(1)}, bf16[128,512]{1,0:T(8,128)(2,...) custom-call(s32[32]{0:T(128)S(1)} %maximum_convert_fusion.r_0_, ...), custom_call_target="tpu_custom_call" | custom-call | flops 1000000000 | bytes 3000000 | tf_op jit(solution)/shard_map/pallas_call | solution.py:275
  85.7 6.7 %all-to-all-start.5 = ((bf16[8,4,80,128]{3,2,1,0:T(8,128)(2,1)}), bf16[8,4,80,128]{3,2,1,0:T(8,128)(2,1)S(1)}, u32[]{:S(2)}, u32[]{:S(2)}) async-start(bf16[8,4,80,128]{3,2,1,0:T(8,128)(2,1)} %get-tuple-element.54), calls=%async_computation.5 | async-start | bytes 1310720 | tf_op jit(solution)/shard_map/all_to_all | solution.py:289
  92.5 10.8 %all-to-all-done.5 = bf16[8,4,80,128]{3,2,1,0:T(8,128)(2,1)S(1)} async-done(((bf16[8,4,80,128]{3,2,1,0:T(8,128)(2,1)}), bf16[8,4,80,128]{3,2,1,0:T(8,128)(2,1)S(1)}, u32[]{:S(2)}, u32[]{:S(2)}) %all-to-all-start.5) | async-done | bytes 655392 | tf_op jit(solution)/shard_map/all_to_all | solution.py:289
  103.3 6.0 %shard_map.80 = bf16[16,80,128]{2,1,0:T(8,128)(2,1)} custom-call(s32[256]{0:T(256)S(1)} %reshape.45.r_0_, s32[3]{0:T(128)S(1)} %pad_add_fusion.ids_ref.r_1_, bf16[32,80,128]{2,1,0:T(8,128)(2,1)S(1)} %bitcast.18, f32[16,128]{1,0:T(8,128)S(1)} %get-tuple-element.55.r_3_), custom_call_target="tpu_custom_call" | custom-call | flops 10000000000 | bytes 30000000 | tf_op jit(solution)/shard_map/pallas_call | solution.py:275
  109.3 9.6 %all-to-all-start.6 = ((bf16[16,80,128]{2,1,0:T(8,128)(2,1)}), bf16[16,80,128]{2,1,0:T(8,128)(2,1)S(1)}, u32[]{:S(2)}, u32[]{:S(2)}) async-start(bf16[16,80,128]{2,1,0:T(8,128)(2,1)} %shard_map.80), calls=%async_computation.6 | async-start | bytes 655360 | tf_op jit(solution)/shard_map/all_to_all | solution.py:289
  119.0 2.8 %collective-permute-start.4 = (bf16[128,512]{1,0:T(8,128)(2,1)S(1)}, bf16[128,512]{1,0:T(8,128)(2,1)S(1)}, u32[]{:S(2)}, u32[]{:S(2)}) collective-permute-start(bf16[128,512]{1,0:T(8,128)(2,1)S(1)} %get-tuple-element.62), channel_id=1, source_target_pairs={{0,96},{32,0},{64,32},{96,64},{1,97},{33,1},{65,33},{97,65},{2,98}... | collective-permute-start | bytes 393224 | tf_op jit(solution)/shard_map/ppermute | solution.py:372
  121.8 3.1 %collective-permute-start.5 = (bf16[128,512]{1,0:T(8,128)(2,1)S(1)}, bf16[128,512]{1,0:T(8,128)(2,1)S(1)}, u32[]{:S(2)}, u32[]{:S(2)}) collective-permute-start(bf16[128,512]{1,0:T(8,128)(2,1)S(1)} %get-tuple-element.63), channel_id=1, source_target_pairs={{0,64},{32,96},{64,0},{96,32},{1,65},{33,97},{65,1},{97,33},{2,66}... | collective-permute-start | bytes 393224 | tf_op jit(solution)/shard_map/ppermute | solution.py:372
  129.0 3.6 %collective-permute-done.6.refs_3_ = bf16[128,512]{1,0:T(8,128)(2,1)S(1)} collective-permute-done((bf16[128,512]{1,0:T(8,128)(2,1)S(1)}, bf16[128,512]{1,0:T(8,128)(2,1)S(1)}, u32[]{:S(2)}, u32[]{:S(2)}) %collective-permute-start.6) | collective-permute-done | bytes 131104 | tf_op jit(solution)/shard_map/ppermute | solution.py:372
  134.7 10.3 %all-to-all-start.7 = ((bf16[32,80,128]{2,1,0:T(8,128)(2,1)}), bf16[32,80,128]{2,1,0:T(8,128)(2,1)S(1)}, u32[]{:S(2)}, u32[]{:S(2)}) async-start(bf16[32,80,128]{2,1,0:T(8,128)(2,1)} %shard_map.81), calls=%async_computation.7 | async-start | bytes 1310720 | tf_op jit(solution)/shard_map/all_to_all | solution.py:289
  146.4 11.6 %all-to-all-done.7.r_0_ = bf16[32,80,128]{2,1,0:T(8,128)(2,1)S(1)} async-done(((bf16[32,80,128]{2,1,0:T(8,128)(2,1)}), bf16[32,80,128]{2,1,0:T(8,128)(2,1)S(1)}, u32[]{:S(2)}, u32[]{:S(2)}) %all-to-all-start.7) | async-done | bytes 655392 | tf_op jit(solution)/shard_map/all_to_all | solution.py:289
  (34 shorter events, 17.5 us)
Async XLA Ops:
  0.6 0.7 dynamic-slice-start
  0.7 17.3 %copy-start.1 = (bf16[128,2048]{1,0:T(8,128)(2,1)S(1)}, bf16[128,2048]{1,0:T(8,128)(2,1)}, u32[]{:S(2)}) copy-start(bf16[128,2048]{1,0:T(8,128)(2,1)} %x_ref.1) | copy-start | bytes 1572868
  2.1 28.9 %all-to-all-start = ((bf16[16,16,512]{2,1,0:T(8,128)(2,1)}), bf16[16,16,512]{2,1,0:T(8,128)(2,1)S(1)}, u32[]{:S(2)}, u32[]{:S(2)}) async-start(bf16[16,16,512]{2,1,0:T(8,128)(2,1)} %broadcast_in_dim.8), calls=%async_computation | async-start | bytes 524288 | tf_op jit(solution)/shard_map/all_to_all | solution.py:289
  17.8 0.7 copy-start.3
  17.9 0.7 copy-start.2
  18.0 0.7 copy-start.4
  19.2 7.5 %collective-permute-start = (bf16[144,512]{1,0:T(8,128)(2,1)S(1)}, bf16[144,512]{1,0:T(8,128)(2,1)S(1)}, u32[]{:S(2)}, u32[]{:S(2)}) collective-permute-start(bf16[144,512]{1,0:T(8,128)(2,1)S(1)} %get-tuple-element.38), channel_id=1, source_target_pairs={{0,32},{32,64},{64,96},{96,0},{1,33},{33,65},{65,97},{97,1},{2,34}... | collective-permute-start | bytes 442376 | tf_op jit(solution)/shard_map/ppermute | solution.py:315
  22.4 6.2 %collective-permute-start.1 = (bf16[144,512]{1,0:T(8,128)(2,1)S(1)}, bf16[144,512]{1,0:T(8,128)(2,1)S(1)}, u32[]{:S(2)}, u32[]{:S(2)}) collective-permute-start(bf16[144,512]{1,0:T(8,128)(2,1)S(1)} %get-tuple-element.39), channel_id=1, source_target_pairs={{0,96},{32,0},{64,32},{96,64},{1,97},{33,1},{65,33},{97,65},{2,98}... | collective-permute-start | bytes 442376 | tf_op jit(solution)/shard_map/ppermute | solution.py:315
  32.1 13.9 %all-to-all-start.1 = ((bf16[4,16,16,512]{3,2,1,0:T(8,128)(2,1)}), bf16[4,16,16,512]{3,2,1,0:T(8,128)(2,1)S(1)}, u32[]{:S(2)}, u32[]{:S(2)}) async-start(bf16[4,16,16,512]{3,2,1,0:T(8,128)(2,1)} %broadcast_in_dim.9), calls=%async_computation.1 | async-start | bytes 2097152 | tf_op jit(solution)/shard_map/all_to_all | solution.py:289
  36.3 7.4 %collective-permute-start.2 = (bf16[144,512]{1,0:T(8,128)(2,1)S(1)}, bf16[144,512]{1,0:T(8,128)(2,1)S(1)}, u32[]{:S(2)}, u32[]{:S(2)}) collective-permute-start(bf16[144,512]{1,0:T(8,128)(2,1)S(1)} %get-tuple-element.43), channel_id=1, source_target_pairs={{0,64},{32,96},{64,0},{96,32},{1,65},{33,97},{65,1},{97,33},{2,66}... | collective-permute-start | bytes 442376 | tf_op jit(solution)/shard_map/ppermute | solution.py:315
  46.1 13.6 %collective-permute-start.3 = (bf16[4,16,16,512]{3,2,1,0:T(8,128)(2,1)S(1)}, bf16[4,16,16,512]{3,2,1,0:T(8,128)(2,1)S(1)}, u32[]{:S(2)}, u32[]{:S(2)}) collective-permute-start(bf16[4,16,16,512]{3,2,1,0:T(8,128)(2,1)S(1)} %all-to-all-done.1.r_6_), channel_id=1, source_target_pairs={{0,16},{16,0},{1,17},{17,1},{2,18},{18,2},{3,19},{19,3},{4,20},{20... | collective-permute-start | bytes 3145736 | tf_op jit(solution)/shard_map/ppermute | solution.py:325
  56.3 7.7 %all-to-all-start.2 = ((bf16[8,1,32]{2,1,0:T(2,128)(2,1)}), bf16[8,1,32]{2,1,0:T(2,128)(2,1)S(1)}, u32[]{:S(2)}, u32[]{:S(2)}) async-start(bf16[8,1,32]{2,1,0:T(2,128)(2,1)} %broadcast_in_dim.11), calls=%async_computation.2 | async-start | bytes 8192 | tf_op jit(solution)/shard_map/all_to_all | solution.py:289
  85.7 17.6 %all-to-all-start.5 = ((bf16[8,4,80,128]{3,2,1,0:T(8,128)(2,1)}), bf16[8,4,80,128]{3,2,1,0:T(8,128)(2,1)S(1)}, u32[]{:S(2)}, u32[]{:S(2)}) async-start(bf16[8,4,80,128]{3,2,1,0:T(8,128)(2,1)} %get-tuple-element.54), calls=%async_computation.5 | async-start | bytes 1310720 | tf_op jit(solution)/shard_map/all_to_all | solution.py:289
  109.3 24.4 %all-to-all-start.6 = ((bf16[16,80,128]{2,1,0:T(8,128)(2,1)}), bf16[16,80,128]{2,1,0:T(8,128)(2,1)S(1)}, u32[]{:S(2)}, u32[]{:S(2)}) async-start(bf16[16,80,128]{2,1,0:T(8,128)(2,1)} %shard_map.80), calls=%async_computation.6 | async-start | bytes 655360 | tf_op jit(solution)/shard_map/all_to_all | solution.py:289
  119.0 7.8 %collective-permute-start.4 = (bf16[128,512]{1,0:T(8,128)(2,1)S(1)}, bf16[128,512]{1,0:T(8,128)(2,1)S(1)}, u32[]{:S(2)}, u32[]{:S(2)}) collective-permute-start(bf16[128,512]{1,0:T(8,128)(2,1)S(1)} %get-tuple-element.62), channel_id=1, source_target_pairs={{0,96},{32,0},{64,32},{96,64},{1,97},{33,1},{65,33},{97,65},{2,98}... | collective-permute-start | bytes 393224 | tf_op jit(solution)/shard_map/ppermute | solution.py:372
  121.8 7.2 %collective-permute-start.5 = (bf16[128,512]{1,0:T(8,128)(2,1)S(1)}, bf16[128,512]{1,0:T(8,128)(2,1)S(1)}, u32[]{:S(2)}, u32[]{:S(2)}) collective-permute-start(bf16[128,512]{1,0:T(8,128)(2,1)S(1)} %get-tuple-element.63), channel_id=1, source_target_pairs={{0,64},{32,96},{64,0},{96,32},{1,65},{33,97},{65,1},{97,33},{2,66}... | collective-permute-start | bytes 393224 | tf_op jit(solution)/shard_map/ppermute | solution.py:372
  124.9 7.7 %collective-permute-start.6 = (bf16[128,512]{1,0:T(8,128)(2,1)S(1)}, bf16[128,512]{1,0:T(8,128)(2,1)S(1)}, u32[]{:S(2)}, u32[]{:S(2)}) collective-permute-start(bf16[128,512]{1,0:T(8,128)(2,1)S(1)} %get-tuple-element.64), channel_id=1, source_target_pairs={{0,32},{32,64},{64,96},{96,0},{1,33},{33,65},{65,97},{97,1},{2,34}... | collective-permute-start | bytes 393224 | tf_op jit(solution)/shard_map/ppermute | solution.py:372
  134.7 23.4 %all-to-all-start.7 = ((bf16[32,80,128]{2,1,0:T(8,128)(2,1)}), bf16[32,80,128]{2,1,0:T(8,128)(2,1)S(1)}, u32[]{:S(2)}, u32[]{:S(2)}) async-start(bf16[32,80,128]{2,1,0:T(8,128)(2,1)} %shard_map.81), calls=%async_computation.7 | async-start | bytes 1310720 | tf_op jit(solution)/shard_map/all_to_all | solution.py:289
  145.0 13.0 %copy-start = (bf16[128,2048]{1,0:T(8,128)(2,1)S(1)}, bf16[128,2048]{1,0:T(8,128)(2,1)}, u32[]{:S(2)}) copy-start(bf16[128,2048]{1,0:T(8,128)(2,1)} %r_1_.1) | copy-start | bytes 1572868

commit v8 on v7

--- a/solution.py
+++ b/solution.py
@@ -90,6 +90,12 @@
     order = atom_rows(core, piece)
     if step == 0:
         (grad_out,) = refs
+        last = mine_ref.shape[1] - 1
+        names = [ref[j, last].astype(F32)[0:1] for ref in (mine_ref, other_ref) for j in range(ny)]
+        names = jnp.concatenate(names, axis=0)
+        for j in range(nx):
+            for t in range(0, nx * rows, width):
+                grad_out[j, SLOTS:, t : t + width] = names
     elif step == 1:
         parts_ref, grad_out, codes_out = refs
     else:
@@ -101,9 +107,9 @@
         mine = slice(s * 128, (s + 1) * 128)
         codes_t, sup_t = read_side(x_refs[s], rows)
         if step > 0:
-            moved = parts_ref[0, :, at]
+            moved = parts_ref[0, :SLOTS, at]
             for j in range(1, nx):
-                moved = moved + parts_ref[j, :, at]
+                moved = moved + parts_ref[j, :SLOTS, at]
             moved = 1.5 * (moved / plen)
         if step == 1:
             codes_t = codes_t + moved
@@ -144,7 +150,7 @@
         if step < 2:
             grad_t = pick(jnp.transpose(jnp.concatenate(scores, axis=0)), sup_t, order)
             for j in range(nx):
-                grad_out[j, :, at] = grad_t
+                grad_out[j, :SLOTS, at] = grad_t
             continue
         merged_t = pick(upright.astype(BF16).astype(F32), sup_t, order)
         side_t = jnp.concatenate([merged_t, sup_t], axis=0).astype(BF16)
@@ -173,21 +179,21 @@
                 usage_out[pl.ds(shards_ref[base + 1], 1), :] += squares[:, 128:]
 
 
-def stats_kernel(nx, shards_ref, ids_ref, msg_ref, usage_ref, out_ref, acc_ref):
+def stats_kernel(ny, nx, shards_ref, ids_ref, msg_ref, usage_ref, out_ref, acc_ref):
     acc_ref[...] = jnp.zeros_like(acc_ref)
-    atom = lax.broadcasted_iota(jnp.int32, (256, 128), 0).astype(F32)
+    atom = lax.broadcasted_iota(jnp.int32, (256, 128), 0).astype(F32).astype(BF16)
     low = lax.broadcasted_iota(jnp.int32, (32, 128), 1) < 64
     low_all = lax.broadcasted_iota(jnp.int32, (128, 128), 1) < 64
 
     def one(q, carry):
-        weights = msg_ref[q, MAIN : MAIN + 16, :].astype(F32)
-        matrix = jnp.zeros((256, 128), F32)
+        weights = msg_ref[q, MAIN : MAIN + 16, :]
+        matrix = jnp.zeros((256, 128), BF16)
         for k in range(SLOTS):
             matrix = jnp.where(
                 weights[SLOTS + k : SLOTS + k + 1, :] == atom, weights[k : k + 1, :], matrix
             )
-        matrix = matrix.astype(BF16)
-        base = (q - q % nx + ((ids_ref[1] - q) & (nx - 1))) * 8
+        source = q // nx
+        base = ((q % nx * 2 + ((source & 1) ^ ids_ref[2])) * ny + (source >> 1)) * 8
         none = jnp.zeros((32, 128), F32)
         for pair in range(2):
             x = msg_ref[q, pair * 32 : pair * 32 + 32, :].astype(F32)
@@ -318,30 +324,37 @@
     by_z, far, *near = lax.optimization_barrier(
         (by_z, packed[nx // 2], *(h for h in held[1:] if h is not None))
     )
-    mine = spread(by_z, "y", ny)
+    own_names = jnp.pad(
+        block_shards.reshape(1, 1, -1).astype(BF16),
+        ((0, 0), (0, piece - 1), (0, width - 2 * blocks)),
+    )
+    mine = spread(jnp.concatenate([by_z, own_names], axis=0), "y", ny)
     near.insert(nx // 2 - 1, ahead(far, nx // 2))
     held = [packed[0], *near]
     mine, *held = lax.optimization_barrier((mine, *held))
     other = lax.ppermute(mine, "c", [(0, 1), (1, 0)])
     names = jnp.concatenate([h[rows : rows + 1, 256 : 256 + 2 * blocks] for h in held], axis=1)
     near_shards = names.astype(jnp.int32).reshape(-1)
-    plane = spread(names, ("y", "c"), ny * nc)
     common = (near_shards, ids, *held, mine, other)
     sizes = (ny, nx, plen)
     takes = "ss" + "v" * (nx + 2)
     grads = sds((nx, SLOTS, nx * rows), F32)
     first = call(
-        lambda *r: refine_kernel(0, sizes, *r), takes, grads, [], *common
-    )
-    first, plane = lax.optimization_barrier((first, plane))
-    shards = plane.astype(jnp.int32).reshape(-1)
+        lambda *r: refine_kernel(0, sizes, *r),
+        takes,
+        sds((nx, SLOTS + ny * nc, nx * rows), F32),
+        [],
+        *common,
+    )
+    first = exchange(first, "x")
+    shards = first[:, SLOTS:, : 2 * blocks].astype(jnp.int32).reshape(-1)
     second, codes_1 = call(
         lambda *r: refine_kernel(1, sizes, *r),
         takes + "v",
         (grads, sds((SLOTS, nx * rows), F32)),
         [],
         *common,
-        exchange(first, "x"),
+        first,
     )
     *home, msg, usage, codes_2 = call(
         lambda *r: refine_kernel(2, sizes, *r),
@@ -360,7 +373,7 @@
     new_codes = codes_2.T
     got = exchange(msg, ("y", "c")).reshape(ny * nc * nx, MSG, 128)
     to_owner = call(
-        lambda *r: stats_kernel(nx, *r),
+        lambda *r: stats_kernel(ny, nx, *r),
         "ssvv",
         sds((nz, MSG, 128), BF16),
         [pltpu.VMEM((nz * SHARD, 128), F32)],

time: 160 us -> 158 us (0.988)
  starting transfers between devices: 78.3 us -> 75.3 us
  local copies, waits for them, and re-layouts: 3.96 us -> 6.01 us
    all_to_all x6 -> x5, waiting for transfers between devices: 29.4 us -> 26.3 us  [exchange(): return lax.all_to_all(x, axes, split_axis=0, concat_axis=0, tiled=True)]
    all_to_all x6 -> x5, starting transfers between devices: 49.9 us -> 46.9 us  [exchange(): return lax.all_to_all(x, axes, split_axis=0, concat_axis=0, tiled=True)]
    unnamed x10, local copies, waits for them, and re-layouts: 0.7 us -> 3.1 us
    ppermute x1, waiting for transfers between devices: 0.01 us -> 2.25 us  [body(): other = lax.ppermute(mine, 'c', [(0, 1), (1, 0)])]
  transfers between devices with their start and end apart: 13 -> 12, of which waited for: 11 -> 10; matrix products, arithmetic and copies ran while one was open for 1% -> 0% of each run, Pallas kernels for 3% -> 1%
where the time goes in v8:
time: 158 us; the launch traced here: 157 us
  starting transfers between devices  75.3 us (48%)
  waiting for transfers between devices  39.7 us (25%)
  Pallas kernels  19.2 us (12%)
  blocking collectives  15.5 us (10%)
  local copies, waits for them, and re-layouts  6.01 us (4%)
    all_to_all x5, starting transfers between devices, exchange(): return lax.all_to_all(x, axes, split_axis=0, concat_axis=0, tiled=True)  46.9 us
    all_to_all x5, waiting for transfers between devices, exchange(): return lax.all_to_all(x, axes, split_axis=0, concat_axis=0, tiled=True)  26.3 us
    pallas_call x8, Pallas kernels, call(): pl.pallas_call(kernel, out_shape=outs, in_specs=[pl.BlockSpec(memory_spac...  19.2 us
    all_to_all x2, blocking collectives, exchange(): return lax.all_to_all(x, axes, split_axis=0, concat_axis=0, tiled=True)  15.5 us
    ppermute x3, starting transfers between devices, ahead(): return lax.ppermute(sent, 'x', [(i, (i + j) % nx) for i in range(nx)])  11.1 us
    ppermute x1, starting transfers between devices, body(): other = lax.ppermute(mine, 'c', [(0, 1), (1, 0)])  9.51 us
    ppermute x3, starting transfers between devices, body(): lax.ppermute(home[j], 'x', [(i, (i - j) % nx) for i in range(nx)])  7.82 us
    ppermute x3, waiting for transfers between devices, body(): lax.ppermute(home[j], 'x', [(i, (i - j) % nx) for i in range(nx)])  5.76 us
  transfers between devices with their start and end apart: 12, of which 10 were waited for; matrix products, arithmetic and copies ran while one was open for 0% of the time, Pallas kernels for 1%

profile of v8, /device:TPU:1, one launch (start us, length us, event | category | flops | bytes accessed | tf_op | source)
XLA Modules:
  0.0 156.7 jit_solution(2749296312153508939)
XLA Ops:
  2.1 15.7 %all-to-all-start = ((bf16[16,16,512]{2,1,0:T(8,128)(2,1)}), bf16[16,16,512]{2,1,0:T(8,128)(2,1)S(1)}, u32[]{:S(2)}, u32[]{:S(2)}) async-start(bf16[16,16,512]{2,1,0:T(8,128)(2,1)} %broadcast_in_dim.4), calls=%async_computation | async-start | bytes 524288 | tf_op jit(solution)/shard_map/all_to_all | solution.py:295
  21.6 3.1 %collective-permute-start = (bf16[144,512]{1,0:T(8,128)(2,1)S(1)}, bf16[144,512]{1,0:T(8,128)(2,1)S(1)}, u32[]{:S(2)}, u32[]{:S(2)}) collective-permute-start(bf16[144,512]{1,0:T(8,128)(2,1)S(1)} %get-tuple-element.36), channel_id=1, source_target_pairs={{0,32},{32,64},{64,96},{96,0},{1,33},{33,65},{65,97},{97,1},{2,34}... | collective-permute-start | bytes 442376 | tf_op jit(solution)/shard_map/ppermute | solution.py:321
  24.8 3.4 %collective-permute-start.1 = (bf16[144,512]{1,0:T(8,128)(2,1)S(1)}, bf16[144,512]{1,0:T(8,128)(2,1)S(1)}, u32[]{:S(2)}, u32[]{:S(2)}) collective-permute-start(bf16[144,512]{1,0:T(8,128)(2,1)S(1)} %get-tuple-element.37), channel_id=1, source_target_pairs={{0,96},{32,0},{64,32},{96,64},{1,97},{33,1},{65,33},{97,65},{2,98}... | collective-permute-start | bytes 442376 | tf_op jit(solution)/shard_map/ppermute | solution.py:321
  32.2 4.2 %all-to-all-start.1 = ((bf16[4,17,16,512]{3,2,1,0:T(8,128)(2,1)}), bf16[4,17,16,512]{3,2,1,0:T(8,128)(2,1)S(1)}, u32[]{:S(2)}, u32[]{:S(2)}) async-start(bf16[4,17,16,512]{3,2,1,0:T(8,128)(2,1)} %broadcast_in_dim.5), calls=%async_computation.1 | async-start | bytes 2228224 | tf_op jit(solution)/shard_map/all_to_all | solution.py:295
  36.4 4.6 %collective-permute-start.2 = (bf16[144,512]{1,0:T(8,128)(2,1)S(1)}, bf16[144,512]{1,0:T(8,128)(2,1)S(1)}, u32[]{:S(2)}, u32[]{:S(2)}) collective-permute-start(bf16[144,512]{1,0:T(8,128)(2,1)S(1)} %get-tuple-element.41), channel_id=1, source_target_pairs={{0,64},{32,96},{64,0},{96,32},{1,65},{33,97},{65,1},{97,33},{2,66}... | collective-permute-start | bytes 442376 | tf_op jit(solution)/shard_map/ppermute | solution.py:321
  41.0 2.7 %collective-permute-done.2.r_4_ = bf16[144,512]{1,0:T(8,128)(2,1)S(1)} collective-permute-done((bf16[144,512]{1,0:T(8,128)(2,1)S(1)}, bf16[144,512]{1,0:T(8,128)(2,1)S(1)}, u32[]{:S(2)}, u32[]{:S(2)}) %collective-permute-start.2) | collective-permute-done | bytes 147488 | tf_op jit(solution)/shard_map/ppermute | solution.py:321
  43.7 2.7 %all-to-all-done.1.r_6_ = bf16[4,17,16,512]{3,2,1,0:T(8,128)(2,1)S(1)} async-done(((bf16[4,17,16,512]{3,2,1,0:T(8,128)(2,1)}), bf16[4,17,16,512]{3,2,1,0:T(8,128)(2,1)S(1)}, u32[]{:S(2)}, u32[]{:S(2)}) %all-to-all-start.1) | async-done | bytes 1114144 | tf_op jit(solution)/shard_map/all_to_all | solution.py:295
  46.4 9.5 %collective-permute-start.3 = (bf16[4,17,16,512]{3,2,1,0:T(8,128)(2,1)S(1)}, bf16[4,17,16,512]{3,2,1,0:T(8,128)(2,1)S(1)}, u32[]{:S(2)}, u32[]{:S(2)}) collective-permute-start(bf16[4,17,16,512]{3,2,1,0:T(8,128)(2,1)S(1)} %all-to-all-done.1.r_6_), channel_id=1, source_target_pairs={{0,16},{16,0},{1,17},{17,1},{2,18},{18,2},{3,19},{19,3},{4,20},{20... | collective-permute-start | bytes 3342344 | tf_op jit(solution)/shard_map/ppermute | solution.py:335
  56.1 2.2 %collective-permute-done.3.r_7_ = bf16[4,17,16,512]{3,2,1,0:T(8,128)(2,1)S(1)} collective-permute-done((bf16[4,17,16,512]{3,2,1,0:T(8,128)(2,1)S(1)}, bf16[4,17,16,512]{3,2,1,0:T(8,128)(2,1)S(1)}, u32[]{:S(2)}, u32[]{:S(2)}) %collective-permute-start.3) | collective-permute-done | bytes 1114144 | tf_op jit(solution)/shard_map/ppermute | solution.py:335
  58.3 3.4 %shard_map.77 = f32[4,16,512]{2,1,0:T(8,128)S(1)} custom-call(s32[32]{0:T(128)S(1)} %maximum_convert_fusion.r_0_, s32[3]{0:T(128)S(1)} %pad_add_fusion.ids_ref.r_1_, bf16[144,512]{1,0:T(8,128)(2,1)S(1)} %get-tuple-element.43.r_2_, bf16[144,512]{1,0:T(8,128)(2,1)S(1)} %collective-permute-done.r_3_, bf16[144,512]{1,0:T(8,128)(2,1)S(1)} %collective-permute-done.2.r_4_, ...), custom_call_target="tpu_custom_call" | custom-call | flops 1000000000 | bytes 3000000 | tf_op jit(solution)/shard_map/pallas_call | solution.py:281
  61.7 8.6 %all_to_all.35.r_8_ = f32[4,16,512]{2,1,0:T(8,128)S(1)} all-to-all(f32[4,16,512]{2,1,0:T(8,128)S(1)} %shard_map.77), channel_id=1, replica_groups=mesh['y'=4,'x'=4,'c'=2,'z'=16] {'x'}, dimensions={0} | all-to-all | bytes 262144 | tf_op jit(solution)/shard_map/all_to_all | solution.py:295
  70.3 3.4 %shard_map.78 = (f32[4,8,512]{2,1,0:T(8,128)S(1)}, f32[8,512]{1,0:T(8,128)S(1)}) custom-call(s32[32]{0:T(128)S(1)} %maximum_convert_fusion.r_0_, s32[3]{0:T(128)S(1)} %pad_add_fusion.ids_ref.r_1_, bf16[144,512]{1,0:T(8,128)(2,1)S(1)} %get-tuple-element.43.r_2_, bf16[144,512]{1,0:T(8,128)(2,1)S(1)} %collective-permute-done.r_3_, ...), custom_call_target="tpu_custom_call" | custom-call | flops 1000000000 | bytes 3000000 | tf_op jit(solution)/shard_map/pallas_call | solution.py:281
  73.7 6.8 %all_to_all.36.r_8_ = f32[4,8,512]{2,1,0:T(8,128)S(1)} all-to-all(f32[4,8,512]{2,1,0:T(8,128)S(1)} %get-tuple-element.48), channel_id=1, replica_groups=mesh['y'=4,'x'=4,'c'=2,'z'=16] {'x'}, dimensions={0} | all-to-all | bytes 131072 | tf_op jit(solution)/shard_map/all_to_all | solution.py:295
  80.5 3.1 %shard_map.79 = (bf16[128,512]{1,0:T(8,128)(2,1)S(1)}, bf16[128,512]{1,0:T(8,128)(2,1)S(1)}, bf16[128,512]{1,0:T(8,128)(2,1)S(1)}, bf16[128,512]{1,0:T(8,128)(2,...) custom-call(s32[32]{0:T(128)S(1)} %maximum_convert_fusion.r_0_, ...), custom_call_target="tpu_custom_call" | custom-call | flops 1000000000 | bytes 3000000 | tf_op jit(solution)/shard_map/pallas_call | solution.py:281
  83.7 6.4 %all-to-all-start.4 = ((bf16[8,4,80,128]{3,2,1,0:T(8,128)(2,1)}), bf16[8,4,80,128]{3,2,1,0:T(8,128)(2,1)S(1)}, u32[]{:S(2)}, u32[]{:S(2)}) async-start(bf16[8,4,80,128]{3,2,1,0:T(8,128)(2,1)} %get-tuple-element.50), calls=%async_computation.4 | async-start | bytes 1310720 | tf_op jit(solution)/shard_map/all_to_all | solution.py:295
  90.2 10.8 %all-to-all-done.4 = bf16[8,4,80,128]{3,2,1,0:T(8,128)(2,1)S(1)} async-done(((bf16[8,4,80,128]{3,2,1,0:T(8,128)(2,1)}), bf16[8,4,80,128]{3,2,1,0:T(8,128)(2,1)S(1)}, u32[]{:S(2)}, u32[]{:S(2)}) %all-to-all-start.4) | async-done | bytes 655392 | tf_op jit(solution)/shard_map/all_to_all | solution.py:295
  101.0 5.1 %shard_map.80 = bf16[16,80,128]{2,1,0:T(8,128)(2,1)} custom-call(s32[256]{0:T(256)S(1)} %reshape.50.r_0_, s32[3]{0:T(128)S(1)} %pad_add_fusion.ids_ref.r_1_, bf16[32,80,128]{2,1,0:T(8,128)(2,1)S(1)} %bitcast.16, f32[16,128]{1,0:T(8,128)S(1)} %get-tuple-element.51.r_3_), custom_call_target="tpu_custom_call" | custom-call | flops 10000000000 | bytes 30000000 | tf_op jit(solution)/shard_map/pallas_call | solution.py:281
  106.1 10.2 %all-to-all-start.5 = ((bf16[16,80,128]{2,1,0:T(8,128)(2,1)}), bf16[16,80,128]{2,1,0:T(8,128)(2,1)S(1)}, u32[]{:S(2)}, u32[]{:S(2)}) async-start(bf16[16,80,128]{2,1,0:T(8,128)(2,1)} %shard_map.80), calls=%async_computation.5 | async-start | bytes 655360 | tf_op jit(solution)/shard_map/all_to_all | solution.py:295
  116.3 2.8 %collective-permute-start.4 = (bf16[128,512]{1,0:T(8,128)(2,1)S(1)}, bf16[128,512]{1,0:T(8,128)(2,1)S(1)}, u32[]{:S(2)}, u32[]{:S(2)}) collective-permute-start(bf16[128,512]{1,0:T(8,128)(2,1)S(1)} %get-tuple-element.58), channel_id=1, source_target_pairs={{0,96},{32,0},{64,32},{96,64},{1,97},{33,1},{65,33},{97,65},{2,98}... | collective-permute-start | bytes 393224 | tf_op jit(solution)/shard_map/ppermute | solution.py:385
  119.1 3.1 %collective-permute-start.5 = (bf16[128,512]{1,0:T(8,128)(2,1)S(1)}, bf16[128,512]{1,0:T(8,128)(2,1)S(1)}, u32[]{:S(2)}, u32[]{:S(2)}) collective-permute-start(bf16[128,512]{1,0:T(8,128)(2,1)S(1)} %get-tuple-element.59), channel_id=1, source_target_pairs={{0,64},{32,96},{64,0},{96,32},{1,65},{33,97},{65,1},{97,33},{2,66}... | collective-permute-start | bytes 393224 | tf_op jit(solution)/shard_map/ppermute | solution.py:385
  124.1 2.2 %collective-permute-done.5.refs_2_ = bf16[128,512]{1,0:T(8,128)(2,1)S(1)} collective-permute-done((bf16[128,512]{1,0:T(8,128)(2,1)S(1)}, bf16[128,512]{1,0:T(8,128)(2,1)S(1)}, u32[]{:S(2)}, u32[]{:S(2)}) %collective-permute-start.5) | collective-permute-done | bytes 131104 | tf_op jit(solution)/shard_map/ppermute | solution.py:385
  126.3 3.6 %collective-permute-done.6.refs_3_ = bf16[128,512]{1,0:T(8,128)(2,1)S(1)} collective-permute-done((bf16[128,512]{1,0:T(8,128)(2,1)S(1)}, bf16[128,512]{1,0:T(8,128)(2,1)S(1)}, u32[]{:S(2)}, u32[]{:S(2)}) %collective-permute-start.6) | collective-permute-done | bytes 131104 | tf_op jit(solution)/shard_map/ppermute | solution.py:385
  131.9 10.4 %all-to-all-start.6 = ((bf16[32,80,128]{2,1,0:T(8,128)(2,1)}), bf16[32,80,128]{2,1,0:T(8,128)(2,1)S(1)}, u32[]{:S(2)}, u32[]{:S(2)}) async-start(bf16[32,80,128]{2,1,0:T(8,128)(2,1)} %shard_map.81), calls=%async_computation.6 | async-start | bytes 1310720 | tf_op jit(solution)/shard_map/all_to_all | solution.py:295
  143.7 11.6 %all-to-all-done.6.r_0_ = bf16[32,80,128]{2,1,0:T(8,128)(2,1)S(1)} async-done(((bf16[32,80,128]{2,1,0:T(8,128)(2,1)}), bf16[32,80,128]{2,1,0:T(8,128)(2,1)S(1)}, u32[]{:S(2)}, u32[]{:S(2)}) %all-to-all-start.6) | async-done | bytes 655392 | tf_op jit(solution)/shard_map/all_to_all | solution.py:295
  (33 shorter events, 16.1 us)
Async XLA Ops:
  2.1 28.9 %all-to-all-start = ((bf16[16,16,512]{2,1,0:T(8,128)(2,1)}), bf16[16,16,512]{2,1,0:T(8,128)(2,1)S(1)}, u32[]{:S(2)}, u32[]{:S(2)}) async-start(bf16[16,16,512]{2,1,0:T(8,128)(2,1)} %broadcast_in_dim.4), calls=%async_computation | async-start | bytes 524288 | tf_op jit(solution)/shard_map/all_to_all | solution.py:295
  17.9 1.0 copy-start.1
  19.0 0.7 copy-start.2
  19.7 0.7 copy-start.3
  20.3 0.7 copy-start.4
  21.6 7.5 %collective-permute-start = (bf16[144,512]{1,0:T(8,128)(2,1)S(1)}, bf16[144,512]{1,0:T(8,128)(2,1)S(1)}, u32[]{:S(2)}, u32[]{:S(2)}) collective-permute-start(bf16[144,512]{1,0:T(8,128)(2,1)S(1)} %get-tuple-element.36), channel_id=1, source_target_pairs={{0,32},{32,64},{64,96},{96,0},{1,33},{33,65},{65,97},{97,1},{2,34}... | collective-permute-start | bytes 442376 | tf_op jit(solution)/shard_map/ppermute | solution.py:321
  24.8 6.2 %collective-permute-start.1 = (bf16[144,512]{1,0:T(8,128)(2,1)S(1)}, bf16[144,512]{1,0:T(8,128)(2,1)S(1)}, u32[]{:S(2)}, u32[]{:S(2)}) collective-permute-start(bf16[144,512]{1,0:T(8,128)(2,1)S(1)} %get-tuple-element.37), channel_id=1, source_target_pairs={{0,96},{32,0},{64,32},{96,64},{1,97},{33,1},{65,33},{97,65},{2,98}... | collective-permute-start | bytes 442376 | tf_op jit(solution)/shard_map/ppermute | solution.py:321
  32.2 14.3 %all-to-all-start.1 = ((bf16[4,17,16,512]{3,2,1,0:T(8,128)(2,1)}), bf16[4,17,16,512]{3,2,1,0:T(8,128)(2,1)S(1)}, u32[]{:S(2)}, u32[]{:S(2)}) async-start(bf16[4,17,16,512]{3,2,1,0:T(8,128)(2,1)} %broadcast_in_dim.5), calls=%async_computation.1 | async-start | bytes 2228224 | tf_op jit(solution)/shard_map/all_to_all | solution.py:295
  36.4 7.4 %collective-permute-start.2 = (bf16[144,512]{1,0:T(8,128)(2,1)S(1)}, bf16[144,512]{1,0:T(8,128)(2,1)S(1)}, u32[]{:S(2)}, u32[]{:S(2)}) collective-permute-start(bf16[144,512]{1,0:T(8,128)(2,1)S(1)} %get-tuple-element.41), channel_id=1, source_target_pairs={{0,64},{32,96},{64,0},{96,32},{1,65},{33,97},{65,1},{97,33},{2,66}... | collective-permute-start | bytes 442376 | tf_op jit(solution)/shard_map/ppermute | solution.py:321
  46.4 11.9 %collective-permute-start.3 = (bf16[4,17,16,512]{3,2,1,0:T(8,128)(2,1)S(1)}, bf16[4,17,16,512]{3,2,1,0:T(8,128)(2,1)S(1)}, u32[]{:S(2)}, u32[]{:S(2)}) collective-permute-start(bf16[4,17,16,512]{3,2,1,0:T(8,128)(2,1)S(1)} %all-to-all-done.1.r_6_), channel_id=1, source_target_pairs={{0,16},{16,0},{1,17},{17,1},{2,18},{18,2},{3,19},{19,3},{4,20},{20... | collective-permute-start | bytes 3342344 | tf_op jit(solution)/shard_map/ppermute | solution.py:335
  83.7 17.3 %all-to-all-start.4 = ((bf16[8,4,80,128]{3,2,1,0:T(8,128)(2,1)}), bf16[8,4,80,128]{3,2,1,0:T(8,128)(2,1)S(1)}, u32[]{:S(2)}, u32[]{:S(2)}) async-start(bf16[8,4,80,128]{3,2,1,0:T(8,128)(2,1)} %get-tuple-element.50), calls=%async_computation.4 | async-start | bytes 1310720 | tf_op jit(solution)/shard_map/all_to_all | solution.py:295
  106.1 24.9 %all-to-all-start.5 = ((bf16[16,80,128]{2,1,0:T(8,128)(2,1)}), bf16[16,80,128]{2,1,0:T(8,128)(2,1)S(1)}, u32[]{:S(2)}, u32[]{:S(2)}) async-start(bf16[16,80,128]{2,1,0:T(8,128)(2,1)} %shard_map.80), calls=%async_computation.5 | async-start | bytes 655360 | tf_op jit(solution)/shard_map/all_to_all | solution.py:295
  116.3 7.8 %collective-permute-start.4 = (bf16[128,512]{1,0:T(8,128)(2,1)S(1)}, bf16[128,512]{1,0:T(8,128)(2,1)S(1)}, u32[]{:S(2)}, u32[]{:S(2)}) collective-permute-start(bf16[128,512]{1,0:T(8,128)(2,1)S(1)} %get-tuple-element.58), channel_id=1, source_target_pairs={{0,96},{32,0},{64,32},{96,64},{1,97},{33,1},{65,33},{97,65},{2,98}... | collective-permute-start | bytes 393224 | tf_op jit(solution)/shard_map/ppermute | solution.py:385
  119.1 7.2 %collective-permute-start.5 = (bf16[128,512]{1,0:T(8,128)(2,1)S(1)}, bf16[128,512]{1,0:T(8,128)(2,1)S(1)}, u32[]{:S(2)}, u32[]{:S(2)}) collective-permute-start(bf16[128,512]{1,0:T(8,128)(2,1)S(1)} %get-tuple-element.59), channel_id=1, source_target_pairs={{0,64},{32,96},{64,0},{96,32},{1,65},{33,97},{65,1},{97,33},{2,66}... | collective-permute-start | bytes 393224 | tf_op jit(solution)/shard_map/ppermute | solution.py:385
  122.2 7.7 %collective-permute-start.6 = (bf16[128,512]{1,0:T(8,128)(2,1)S(1)}, bf16[128,512]{1,0:T(8,128)(2,1)S(1)}, u32[]{:S(2)}, u32[]{:S(2)}) collective-permute-start(bf16[128,512]{1,0:T(8,128)(2,1)S(1)} %get-tuple-element.60), channel_id=1, source_target_pairs={{0,32},{32,64},{64,96},{96,0},{1,33},{33,65},{65,97},{97,1},{2,34}... | collective-permute-start | bytes 393224 | tf_op jit(solution)/shard_map/ppermute | solution.py:385
  131.9 23.4 %all-to-all-start.6 = ((bf16[32,80,128]{2,1,0:T(8,128)(2,1)}), bf16[32,80,128]{2,1,0:T(8,128)(2,1)S(1)}, u32[]{:S(2)}, u32[]{:S(2)}) async-start(bf16[32,80,128]{2,1,0:T(8,128)(2,1)} %shard_map.81), calls=%async_computation.6 | async-start | bytes 1310720 | tf_op jit(solution)/shard_map/all_to_all | solution.py:295
  142.3 13.0 %copy-start = (bf16[128,2048]{1,0:T(8,128)(2,1)S(1)}, bf16[128,2048]{1,0:T(8,128)(2,1)}, u32[]{:S(2)}) copy-start(bf16[128,2048]{1,0:T(8,128)(2,1)} %r_1_.1) | copy-start | bytes 1572868

commit v9 on v8

--- a/solution.py
+++ b/solution.py
@@ -78,6 +78,14 @@
     )
 
 
+def first_codes_kernel(piece, ids_ref, *refs):
+    *x_refs, out_ref = refs
+    order = atom_rows(ids_ref[2], piece)
+    for s, x_ref in enumerate(x_refs):
+        codes_t, sup_t = read_side(x_ref, x_ref.shape[0] - 16)
+        out_ref[s] = jnp.transpose(code_matrix(codes_t, sup_t, order)).astype(BF16)
+
+
 def refine_kernel(step, sizes, shards_ref, ids_ref, *refs):
     ny, nx, plen = sizes
     x_refs, (mine_ref, other_ref), refs = refs[:nx], refs[nx : nx + 2], refs[nx + 2 :]
@@ -89,13 +97,12 @@
     core = ids_ref[2]
     order = atom_rows(core, piece)
     if step == 0:
-        (grad_out,) = refs
+        matrix_ref, grad_out = refs
         last = mine_ref.shape[1] - 1
         names = [ref[j, last].astype(F32)[0:1] for ref in (mine_ref, other_ref) for j in range(ny)]
-        names = jnp.concatenate(names, axis=0)
+        names = jnp.concatenate(names, axis=0)[:, :128]
         for j in range(nx):
-            for t in range(0, nx * rows, width):
-                grad_out[j, SLOTS:, t : t + width] = names
+            grad_out[j, : 2 * ny, nx * rows :] = names
     elif step == 1:
         parts_ref, grad_out, codes_out = refs
     else:
@@ -107,9 +114,9 @@
         mine = slice(s * 128, (s + 1) * 128)
         codes_t, sup_t = read_side(x_refs[s], rows)
         if step > 0:
-            moved = parts_ref[0, :SLOTS, at]
+            moved = parts_ref[0, :, at]
             for j in range(1, nx):
-                moved = moved + parts_ref[j, :SLOTS, at]
+                moved = moved + parts_ref[j, :, at]
             moved = 1.5 * (moved / plen)
         if step == 1:
             codes_t = codes_t + moved
@@ -118,8 +125,11 @@
             codes_t = codes_ref[:, mine] + moved
             if s == 0:
                 codes_out[...] = codes_t
-        upright = code_matrix(codes_t, sup_t, order)
-        matrix = jnp.transpose(upright).astype(BF16)
+        if step == 0:
+            matrix = matrix_ref[s]
+        else:
+            upright = code_matrix(codes_t, sup_t, order)
+            matrix = jnp.transpose(upright).astype(BF16)
         scores = []
         outs = [[] for _ in range(width // chunk)]
         for b in range(blocks):
@@ -150,7 +160,7 @@
         if step < 2:
             grad_t = pick(jnp.transpose(jnp.concatenate(scores, axis=0)), sup_t, order)
             for j in range(nx):
-                grad_out[j, :SLOTS, at] = grad_t
+                grad_out[j, :, at] = grad_t
             continue
         merged_t = pick(upright.astype(BF16).astype(F32), sup_t, order)
         side_t = jnp.concatenate([merged_t, sup_t], axis=0).astype(BF16)
@@ -339,15 +349,23 @@
     sizes = (ny, nx, plen)
     takes = "ss" + "v" * (nx + 2)
     grads = sds((nx, SLOTS, nx * rows), F32)
+    matrices = call(
+        functools.partial(first_codes_kernel, piece),
+        "s" + "v" * nx,
+        sds((nx, rows, 256), BF16),
+        [],
+        ids, *held,
+    )
     first = call(
         lambda *r: refine_kernel(0, sizes, *r),
-        takes,
-        sds((nx, SLOTS + ny * nc, nx * rows), F32),
+        takes + "v",
+        sds((nx, SLOTS, nx * rows + 128), F32),
         [],
         *common,
+        matrices,
     )
     first = exchange(first, "x")
-    shards = first[:, SLOTS:, : 2 * blocks].astype(jnp.int32).reshape(-1)
+    shards = first[:, : ny * nc, nx * rows : nx * rows + 2 * blocks].astype(jnp.int32).reshape(-1)
     second, codes_1 = call(
         lambda *r: refine_kernel(1, sizes, *r),
         takes + "v",

time: 158 us -> 157 us (level)
    pallas_call x8 -> x9, Pallas kernels: 19.2 us -> 20.2 us  [call(): pl.pallas_call(kernel, out_shape=outs, in_specs=[pl.BlockSpec(memory_spac...]
  transfers between devices with their start and end apart: 12 -> 12, of which waited for: 10 -> 10; matrix products, arithmetic and copies ran while one was open for 0% -> 0% of each run, Pallas kernels for 1% -> 2%
where the time goes in v9:
time: 157 us; the launch traced here: 156 us
  starting transfers between devices  75.3 us (48%)
  waiting for transfers between devices  38.6 us (25%)
  Pallas kernels  20.2 us (13%)
  blocking collectives  15.2 us (10%)
  local copies, waits for them, and re-layouts  6.01 us (4%)
    all_to_all x5, starting transfers between devices, exchange(): return lax.all_to_all(x, axes, split_axis=0, concat_axis=0, tiled=True)  46.8 us
    all_to_all x5, waiting for transfers between devices, exchange(): return lax.all_to_all(x, axes, split_axis=0, concat_axis=0, tiled=True)  26.4 us
    pallas_call x9, Pallas kernels, call(): pl.pallas_call(kernel, out_shape=outs, in_specs=[pl.BlockSpec(memory_spac...  20.2 us
    all_to_all x2, blocking collectives, exchange(): return lax.all_to_all(x, axes, split_axis=0, concat_axis=0, tiled=True)  15.2 us
    ppermute x3, starting transfers between devices, ahead(): return lax.ppermute(sent, 'x', [(i, (i + j) % nx) for i in range(nx)])  11.1 us
    ppermute x1, starting transfers between devices, body(): other = lax.ppermute(mine, 'c', [(0, 1), (1, 0)])  9.51 us
    ppermute x3, starting transfers between devices, body(): lax.ppermute(home[j], 'x', [(i, (i - j) % nx) for i in range(nx)])  7.81 us
    ppermute x3, waiting for transfers between devices, body(): lax.ppermute(home[j], 'x', [(i, (i - j) % nx) for i in range(nx)])  5.77 us
  transfers between devices with their start and end apart: 12, of which 10 were waited for; matrix products, arithmetic and copies ran while one was open for 0% of the time, Pallas kernels for 2%

profile of v9, /device:TPU:1, one launch (start us, length us, event | category | flops | bytes accessed | tf_op | source)
XLA Modules:
  0.0 156.2 jit_solution(16777190839532576084)
XLA Ops:
  2.1 15.7 %all-to-all-start = ((bf16[16,16,512]{2,1,0:T(8,128)(2,1)}), bf16[16,16,512]{2,1,0:T(8,128)(2,1)S(1)}, u32[]{:S(2)}, u32[]{:S(2)}) async-start(bf16[16,16,512]{2,1,0:T(8,128)(2,1)} %broadcast_in_dim.4), calls=%async_computation | async-start | bytes 524288 | tf_op jit(solution)/shard_map/all_to_all | solution.py:305
  21.6 3.1 %collective-permute-start = (bf16[144,512]{1,0:T(8,128)(2,1)S(1)}, bf16[144,512]{1,0:T(8,128)(2,1)S(1)}, u32[]{:S(2)}, u32[]{:S(2)}) collective-permute-start(bf16[144,512]{1,0:T(8,128)(2,1)S(1)} %get-tuple-element.36), channel_id=1, source_target_pairs={{0,32},{32,64},{64,96},{96,0},{1,33},{33,65},{65,97},{97,1},{2,34}... | collective-permute-start | bytes 442376 | tf_op jit(solution)/shard_map/ppermute | solution.py:331
  24.8 3.4 %collective-permute-start.1 = (bf16[144,512]{1,0:T(8,128)(2,1)S(1)}, bf16[144,512]{1,0:T(8,128)(2,1)S(1)}, u32[]{:S(2)}, u32[]{:S(2)}) collective-permute-start(bf16[144,512]{1,0:T(8,128)(2,1)S(1)} %get-tuple-element.37), channel_id=1, source_target_pairs={{0,96},{32,0},{64,32},{96,64},{1,97},{33,1},{65,33},{97,65},{2,98}... | collective-permute-start | bytes 442376 | tf_op jit(solution)/shard_map/ppermute | solution.py:331
  32.2 4.2 %all-to-all-start.1 = ((bf16[4,17,16,512]{3,2,1,0:T(8,128)(2,1)}), bf16[4,17,16,512]{3,2,1,0:T(8,128)(2,1)S(1)}, u32[]{:S(2)}, u32[]{:S(2)}) async-start(bf16[4,17,16,512]{3,2,1,0:T(8,128)(2,1)} %broadcast_in_dim.5), calls=%async_computation.1 | async-start | bytes 2228224 | tf_op jit(solution)/shard_map/all_to_all | solution.py:305
  36.4 4.6 %collective-permute-start.2 = (bf16[144,512]{1,0:T(8,128)(2,1)S(1)}, bf16[144,512]{1,0:T(8,128)(2,1)S(1)}, u32[]{:S(2)}, u32[]{:S(2)}) collective-permute-start(bf16[144,512]{1,0:T(8,128)(2,1)S(1)} %get-tuple-element.41), channel_id=1, source_target_pairs={{0,64},{32,96},{64,0},{96,32},{1,65},{33,97},{65,1},{97,33},{2,66}... | collective-permute-start | bytes 442376 | tf_op jit(solution)/shard_map/ppermute | solution.py:331
  41.0 2.7 %collective-permute-done.2.refs_2_.r_4_ = bf16[144,512]{1,0:T(8,128)(2,1)S(1)} collective-permute-done((bf16[144,512]{1,0:T(8,128)(2,1)S(1)}, bf16[144,512]{1,0:T(8,128)(2,1)S(1)}, u32[]{:S(2)}, u32[]{:S(2)}) %collective-permute-start.2) | collective-permute-done | bytes 147488 | tf_op jit(solution)/shard_map/ppermute | solution.py:331
  43.7 2.7 %all-to-all-done.1.r_6_ = bf16[4,17,16,512]{3,2,1,0:T(8,128)(2,1)S(1)} async-done(((bf16[4,17,16,512]{3,2,1,0:T(8,128)(2,1)}), bf16[4,17,16,512]{3,2,1,0:T(8,128)(2,1)S(1)}, u32[]{:S(2)}, u32[]{:S(2)}) %all-to-all-start.1) | async-done | bytes 1114144 | tf_op jit(solution)/shard_map/all_to_all | solution.py:305
  46.4 9.5 %collective-permute-start.3 = (bf16[4,17,16,512]{3,2,1,0:T(8,128)(2,1)S(1)}, bf16[4,17,16,512]{3,2,1,0:T(8,128)(2,1)S(1)}, u32[]{:S(2)}, u32[]{:S(2)}) collective-permute-start(bf16[4,17,16,512]{3,2,1,0:T(8,128)(2,1)S(1)} %all-to-all-done.1.r_6_), channel_id=1, source_target_pairs={{0,16},{16,0},{1,17},{17,1},{2,18},{18,2},{3,19},{19,3},{4,20},{20... | collective-permute-start | bytes 3342344 | tf_op jit(solution)/shard_map/ppermute | solution.py:345
  58.3 3.2 %shard_map.78 = f32[4,8,640]{2,1,0:T(8,128)S(1)} custom-call(s32[32]{0:T(128)S(1)} %maximum_convert_fusion.r_0_, s32[3]{0:T(128)S(1)} %pad_add_fusion.ids_ref.r_1_, bf16[144,512]{1,0:T(8,128)(2,1)S(1)} %get-tuple-element.43.refs_0_.r_2_, bf16[144,512]{1,0:T(8,128)(2,1)S(1)} %collective-permute-done.refs_1_.r_3_, ...), custom_call_target="tpu_custom_call" | custom-call | flops 1000000000 | bytes 3000000 | tf_op jit(solution)/shard_map/pallas_call | solution.py:291
  61.5 8.4 %all_to_all.35.r_8_ = f32[4,8,640]{2,1,0:T(8,128)S(1)} all-to-all(f32[4,8,640]{2,1,0:T(8,128)S(1)} %shard_map.78), channel_id=1, replica_groups=mesh['y'=4,'x'=4,'c'=2,'z'=16] {'x'}, dimensions={0} | all-to-all | bytes 163840 | tf_op jit(solution)/shard_map/all_to_all | solution.py:305
  69.9 3.4 %shard_map.79 = (f32[4,8,512]{2,1,0:T(8,128)S(1)}, f32[8,512]{1,0:T(8,128)S(1)}) custom-call(s32[32]{0:T(128)S(1)} %maximum_convert_fusion.r_0_, s32[3]{0:T(128)S(1)} %pad_add_fusion.ids_ref.r_1_, bf16[144,512]{1,0:T(8,128)(2,1)S(1)} %get-tuple-element.43.refs_0_.r_2_, bf16[144,512]{1,0:T(8,128)(2,1)S(1)} %collective-permute-done.refs_1_.r_3_, ...), custom_call_target="tpu_custom_call" | custom-call | flops 1000000000 | bytes 3000000 | tf_op jit(solution)/shard_map/pallas_call | solution.py:291
  73.3 6.8 %all_to_all.36.r_8_ = f32[4,8,512]{2,1,0:T(8,128)S(1)} all-to-all(f32[4,8,512]{2,1,0:T(8,128)S(1)} %get-tuple-element.48), channel_id=1, replica_groups=mesh['y'=4,'x'=4,'c'=2,'z'=16] {'x'}, dimensions={0} | all-to-all | bytes 131072 | tf_op jit(solution)/shard_map/all_to_all | solution.py:305
  80.1 3.1 %shard_map.80 = (bf16[128,512]{1,0:T(8,128)(2,1)S(1)}, bf16[128,512]{1,0:T(8,128)(2,1)S(1)}, bf16[128,512]{1,0:T(8,128)(2,1)S(1)}, bf16[128,512]{1,0:T(8,128)(2,...) custom-call(s32[32]{0:T(128)S(1)} %maximum_convert_fusion.r_0_, ...), custom_call_target="tpu_custom_call" | custom-call | flops 1000000000 | bytes 3000000 | tf_op jit(solution)/shard_map/pallas_call | solution.py:291
  83.2 6.4 %all-to-all-start.4 = ((bf16[8,4,80,128]{3,2,1,0:T(8,128)(2,1)}), bf16[8,4,80,128]{3,2,1,0:T(8,128)(2,1)S(1)}, u32[]{:S(2)}, u32[]{:S(2)}) async-start(bf16[8,4,80,128]{3,2,1,0:T(8,128)(2,1)} %get-tuple-element.50), calls=%async_computation.4 | async-start | bytes 1310720 | tf_op jit(solution)/shard_map/all_to_all | solution.py:305
  89.7 10.8 %all-to-all-done.4 = bf16[8,4,80,128]{3,2,1,0:T(8,128)(2,1)S(1)} async-done(((bf16[8,4,80,128]{3,2,1,0:T(8,128)(2,1)}), bf16[8,4,80,128]{3,2,1,0:T(8,128)(2,1)S(1)}, u32[]{:S(2)}, u32[]{:S(2)}) %all-to-all-start.4) | async-done | bytes 655392 | tf_op jit(solution)/shard_map/all_to_all | solution.py:305
  100.5 5.1 %shard_map.81 = bf16[16,80,128]{2,1,0:T(8,128)(2,1)} custom-call(s32[256]{0:T(256)S(1)} %reshape.50.r_0_, s32[3]{0:T(128)S(1)} %pad_add_fusion.ids_ref.r_1_, bf16[32,80,128]{2,1,0:T(8,128)(2,1)S(1)} %bitcast.16, f32[16,128]{1,0:T(8,128)S(1)} %get-tuple-element.51.r_3_), custom_call_target="tpu_custom_call" | custom-call | flops 10000000000 | bytes 30000000 | tf_op jit(solution)/shard_map/pallas_call | solution.py:291
  105.7 10.2 %all-to-all-start.5 = ((bf16[16,80,128]{2,1,0:T(8,128)(2,1)}), bf16[16,80,128]{2,1,0:T(8,128)(2,1)S(1)}, u32[]{:S(2)}, u32[]{:S(2)}) async-start(bf16[16,80,128]{2,1,0:T(8,128)(2,1)} %shard_map.81), calls=%async_computation.5 | async-start | bytes 655360 | tf_op jit(solution)/shard_map/all_to_all | solution.py:305
  115.8 2.8 %collective-permute-start.4 = (bf16[128,512]{1,0:T(8,128)(2,1)S(1)}, bf16[128,512]{1,0:T(8,128)(2,1)S(1)}, u32[]{:S(2)}, u32[]{:S(2)}) collective-permute-start(bf16[128,512]{1,0:T(8,128)(2,1)S(1)} %get-tuple-element.58), channel_id=1, source_target_pairs={{0,96},{32,0},{64,32},{96,64},{1,97},{33,1},{65,33},{97,65},{2,98}... | collective-permute-start | bytes 393224 | tf_op jit(solution)/shard_map/ppermute | solution.py:403
  118.6 3.1 %collective-permute-start.5 = (bf16[128,512]{1,0:T(8,128)(2,1)S(1)}, bf16[128,512]{1,0:T(8,128)(2,1)S(1)}, u32[]{:S(2)}, u32[]{:S(2)}) collective-permute-start(bf16[128,512]{1,0:T(8,128)(2,1)S(1)} %get-tuple-element.59), channel_id=1, source_target_pairs={{0,64},{32,96},{64,0},{96,32},{1,65},{33,97},{65,1},{97,33},{2,66}... | collective-permute-start | bytes 393224 | tf_op jit(solution)/shard_map/ppermute | solution.py:403
  121.8 1.9 %collective-permute-start.6 = (bf16[128,512]{1,0:T(8,128)(2,1)S(1)}, bf16[128,512]{1,0:T(8,128)(2,1)S(1)}, u32[]{:S(2)}, u32[]{:S(2)}) collective-permute-start(bf16[128,512]{1,0:T(8,128)(2,1)S(1)} %get-tuple-element.60), channel_id=1, source_target_pairs={{0,32},{32,64},{64,96},{96,0},{1,33},{33,65},{65,97},{97,1},{2,34}... | collective-permute-start | bytes 393224 | tf_op jit(solution)/shard_map/ppermute | solution.py:403
  123.7 2.2 %collective-permute-done.5.refs_2_ = bf16[128,512]{1,0:T(8,128)(2,1)S(1)} collective-permute-done((bf16[128,512]{1,0:T(8,128)(2,1)S(1)}, bf16[128,512]{1,0:T(8,128)(2,1)S(1)}, u32[]{:S(2)}, u32[]{:S(2)}) %collective-permute-start.5) | collective-permute-done | bytes 131104 | tf_op jit(solution)/shard_map/ppermute | solution.py:403
  125.9 3.6 %collective-permute-done.6.refs_3_ = bf16[128,512]{1,0:T(8,128)(2,1)S(1)} collective-permute-done((bf16[128,512]{1,0:T(8,128)(2,1)S(1)}, bf16[128,512]{1,0:T(8,128)(2,1)S(1)}, u32[]{:S(2)}, u32[]{:S(2)}) %collective-permute-start.6) | collective-permute-done | bytes 131104 | tf_op jit(solution)/shard_map/ppermute | solution.py:403
  131.5 10.3 %all-to-all-start.6 = ((bf16[32,80,128]{2,1,0:T(8,128)(2,1)}), bf16[32,80,128]{2,1,0:T(8,128)(2,1)S(1)}, u32[]{:S(2)}, u32[]{:S(2)}) async-start(bf16[32,80,128]{2,1,0:T(8,128)(2,1)} %shard_map.82), calls=%async_computation.6 | async-start | bytes 1310720 | tf_op jit(solution)/shard_map/all_to_all | solution.py:305
  143.2 11.6 %all-to-all-done.6.r_0_ = bf16[32,80,128]{2,1,0:T(8,128)(2,1)S(1)} async-done(((bf16[32,80,128]{2,1,0:T(8,128)(2,1)}), bf16[32,80,128]{2,1,0:T(8,128)(2,1)S(1)}, u32[]{:S(2)}, u32[]{:S(2)}) %all-to-all-start.6) | async-done | bytes 655392 | tf_op jit(solution)/shard_map/all_to_all | solution.py:305
  (34 shorter events, 16.5 us)
Async XLA Ops:
  2.1 28.9 %all-to-all-start = ((bf16[16,16,512]{2,1,0:T(8,128)(2,1)}), bf16[16,16,512]{2,1,0:T(8,128)(2,1)S(1)}, u32[]{:S(2)}, u32[]{:S(2)}) async-start(bf16[16,16,512]{2,1,0:T(8,128)(2,1)} %broadcast_in_dim.4), calls=%async_computation | async-start | bytes 524288 | tf_op jit(solution)/shard_map/all_to_all | solution.py:305
  17.9 1.0 copy-start.1
  19.0 0.7 copy-start.2
  19.7 0.7 copy-start.3
  20.3 0.7 copy-start.4
  21.6 7.5 %collective-permute-start = (bf16[144,512]{1,0:T(8,128)(2,1)S(1)}, bf16[144,512]{1,0:T(8,128)(2,1)S(1)}, u32[]{:S(2)}, u32[]{:S(2)}) collective-permute-start(bf16[144,512]{1,0:T(8,128)(2,1)S(1)} %get-tuple-element.36), channel_id=1, source_target_pairs={{0,32},{32,64},{64,96},{96,0},{1,33},{33,65},{65,97},{97,1},{2,34}... | collective-permute-start | bytes 442376 | tf_op jit(solution)/shard_map/ppermute | solution.py:331
  24.8 6.2 %collective-permute-start.1 = (bf16[144,512]{1,0:T(8,128)(2,1)S(1)}, bf16[144,512]{1,0:T(8,128)(2,1)S(1)}, u32[]{:S(2)}, u32[]{:S(2)}) collective-permute-start(bf16[144,512]{1,0:T(8,128)(2,1)S(1)} %get-tuple-element.37), channel_id=1, source_target_pairs={{0,96},{32,0},{64,32},{96,64},{1,97},{33,1},{65,33},{97,65},{2,98}... | collective-permute-start | bytes 442376 | tf_op jit(solution)/shard_map/ppermute | solution.py:331
  32.2 14.3 %all-to-all-start.1 = ((bf16[4,17,16,512]{3,2,1,0:T(8,128)(2,1)}), bf16[4,17,16,512]{3,2,1,0:T(8,128)(2,1)S(1)}, u32[]{:S(2)}, u32[]{:S(2)}) async-start(bf16[4,17,16,512]{3,2,1,0:T(8,128)(2,1)} %broadcast_in_dim.5), calls=%async_computation.1 | async-start | bytes 2228224 | tf_op jit(solution)/shard_map/all_to_all | solution.py:305
  36.4 7.4 %collective-permute-start.2 = (bf16[144,512]{1,0:T(8,128)(2,1)S(1)}, bf16[144,512]{1,0:T(8,128)(2,1)S(1)}, u32[]{:S(2)}, u32[]{:S(2)}) collective-permute-start(bf16[144,512]{1,0:T(8,128)(2,1)S(1)} %get-tuple-element.41), channel_id=1, source_target_pairs={{0,64},{32,96},{64,0},{96,32},{1,65},{33,97},{65,1},{97,33},{2,66}... | collective-permute-start | bytes 442376 | tf_op jit(solution)/shard_map/ppermute | solution.py:331
  46.4 11.9 %collective-permute-start.3 = (bf16[4,17,16,512]{3,2,1,0:T(8,128)(2,1)S(1)}, bf16[4,17,16,512]{3,2,1,0:T(8,128)(2,1)S(1)}, u32[]{:S(2)}, u32[]{:S(2)}) collective-permute-start(bf16[4,17,16,512]{3,2,1,0:T(8,128)(2,1)S(1)} %all-to-all-done.1.r_6_), channel_id=1, source_target_pairs={{0,16},{16,0},{1,17},{17,1},{2,18},{18,2},{3,19},{19,3},{4,20},{20... | collective-permute-start | bytes 3342344 | tf_op jit(solution)/shard_map/ppermute | solution.py:345
  83.2 17.3 %all-to-all-start.4 = ((bf16[8,4,80,128]{3,2,1,0:T(8,128)(2,1)}), bf16[8,4,80,128]{3,2,1,0:T(8,128)(2,1)S(1)}, u32[]{:S(2)}, u32[]{:S(2)}) async-start(bf16[8,4,80,128]{3,2,1,0:T(8,128)(2,1)} %get-tuple-element.50), calls=%async_computation.4 | async-start | bytes 1310720 | tf_op jit(solution)/shard_map/all_to_all | solution.py:305
  105.7 24.9 %all-to-all-start.5 = ((bf16[16,80,128]{2,1,0:T(8,128)(2,1)}), bf16[16,80,128]{2,1,0:T(8,128)(2,1)S(1)}, u32[]{:S(2)}, u32[]{:S(2)}) async-start(bf16[16,80,128]{2,1,0:T(8,128)(2,1)} %shard_map.81), calls=%async_computation.5 | async-start | bytes 655360 | tf_op jit(solution)/shard_map/all_to_all | solution.py:305
  115.8 7.8 %collective-permute-start.4 = (bf16[128,512]{1,0:T(8,128)(2,1)S(1)}, bf16[128,512]{1,0:T(8,128)(2,1)S(1)}, u32[]{:S(2)}, u32[]{:S(2)}) collective-permute-start(bf16[128,512]{1,0:T(8,128)(2,1)S(1)} %get-tuple-element.58), channel_id=1, source_target_pairs={{0,96},{32,0},{64,32},{96,64},{1,97},{33,1},{65,33},{97,65},{2,98}... | collective-permute-start | bytes 393224 | tf_op jit(solution)/shard_map/ppermute | solution.py:403
  118.6 7.2 %collective-permute-start.5 = (bf16[128,512]{1,0:T(8,128)(2,1)S(1)}, bf16[128,512]{1,0:T(8,128)(2,1)S(1)}, u32[]{:S(2)}, u32[]{:S(2)}) collective-permute-start(bf16[128,512]{1,0:T(8,128)(2,1)S(1)} %get-tuple-element.59), channel_id=1, source_target_pairs={{0,64},{32,96},{64,0},{96,32},{1,65},{33,97},{65,1},{97,33},{2,66}... | collective-permute-start | bytes 393224 | tf_op jit(solution)/shard_map/ppermute | solution.py:403
  121.8 7.7 %collective-permute-start.6 = (bf16[128,512]{1,0:T(8,128)(2,1)S(1)}, bf16[128,512]{1,0:T(8,128)(2,1)S(1)}, u32[]{:S(2)}, u32[]{:S(2)}) collective-permute-start(bf16[128,512]{1,0:T(8,128)(2,1)S(1)} %get-tuple-element.60), channel_id=1, source_target_pairs={{0,32},{32,64},{64,96},{96,0},{1,33},{33,65},{65,97},{97,1},{2,34}... | collective-permute-start | bytes 393224 | tf_op jit(solution)/shard_map/ppermute | solution.py:403
  131.5 23.3 %all-to-all-start.6 = ((bf16[32,80,128]{2,1,0:T(8,128)(2,1)}), bf16[32,80,128]{2,1,0:T(8,128)(2,1)S(1)}, u32[]{:S(2)}, u32[]{:S(2)}) async-start(bf16[32,80,128]{2,1,0:T(8,128)(2,1)} %shard_map.82), calls=%async_computation.6 | async-start | bytes 1310720 | tf_op jit(solution)/shard_map/all_to_all | solution.py:305
  141.9 13.0 %copy-start = (bf16[128,2048]{1,0:T(8,128)(2,1)S(1)}, bf16[128,2048]{1,0:T(8,128)(2,1)}, u32[]{:S(2)}) copy-start(bf16[128,2048]{1,0:T(8,128)(2,1)} %r_1_.1) | copy-start | bytes 1572868

commit v10 on v9

--- a/solution.py
+++ b/solution.py
@@ -29,12 +29,7 @@
     third = rest - second
     top = jnp.concatenate([first, second], axis=0).astype(BF16)
     low = jnp.concatenate([third, sup_ref[...].astype(F32)], axis=0).astype(BF16)
-    lane = lax.broadcasted_iota(jnp.int32, (16, 128), 1)
-    names = jnp.zeros((16, 128), jnp.int32)
-    for b in range(names_ref.shape[1]):
-        for h in range(2):
-            names = jnp.where(lane == 2 * b + h, names_ref[h, b], names)
-    names = names.astype(F32).astype(BF16)
+    names = names_row(names_ref)
     for j in range(count):
         start = pl.multiple_of(((ids_ref[1] + j) & (count - 1)) * width, 128)
         outs[j][:rows, :] = x_ref[:, pl.ds(start, width)]
@@ -45,6 +40,24 @@
             outs[j][rows : rows + 16, t : t + 128] = jnp.zeros((16, 128), BF16)
 
 
+def names_row(names_ref):
+    lane = lax.broadcasted_iota(jnp.int32, (16, 128), 1)
+    names = jnp.zeros((16, 128), jnp.int32)
+    for b in range(names_ref.shape[1]):
+        for h in range(2):
+            names = jnp.where(lane == 2 * b + h, names_ref[h, b], names)
+    return names.astype(F32).astype(BF16)
+
+
+def copies_kernel(names_ref, atoms_ref, out_ref):
+    names = names_row(names_ref)
+    shards, piece, width = atoms_ref.shape
+    for j in range(out_ref.shape[0]):
+        out_ref[j, :shards] = atoms_ref[...]
+        out_ref[j, shards] = jnp.zeros((piece, width), BF16)
+        out_ref[j, shards, :16, :128] = names
+
+
 def read_side(x_ref, rows):
     top = x_ref[rows : rows + 16, :128].astype(F32)
     low = x_ref[rows : rows + 16, 128:256].astype(F32)
@@ -93,7 +106,7 @@
     rows = height - 16
     piece = mine_ref.shape[2]
     blocks = rows // 32
-    chunk = min(256, width)
+    chunk = width
     core = ids_ref[2]
     order = atom_rows(core, piece)
     if step == 0:
@@ -334,11 +347,10 @@
     by_z, far, *near = lax.optimization_barrier(
         (by_z, packed[nx // 2], *(h for h in held[1:] if h is not None))
     )
-    own_names = jnp.pad(
-        block_shards.reshape(1, 1, -1).astype(BF16),
-        ((0, 0), (0, piece - 1), (0, width - 2 * blocks)),
-    )
-    mine = spread(jnp.concatenate([by_z, own_names], axis=0), "y", ny)
+    copies = call(
+        copies_kernel, "sv", sds((ny, nz + 1, piece, width), BF16), [], block_shards.T, by_z
+    )
+    mine = exchange(copies, "y")
     near.insert(nx // 2 - 1, ahead(far, nx // 2))
     held = [packed[0], *near]
     mine, *held = lax.optimization_barrier((mine, *held))

time: 157 us -> 157 us (level)
    pallas_call x9 -> x10, Pallas kernels: 20.2 us -> 21.3 us  [call(): pl.pallas_call(kernel, out_shape=outs, in_specs=[pl.BlockSpec(memory_spac...]
where the time goes in v10:
time: 157 us; the launch traced here: 156 us
  starting transfers between devices  75.3 us (48%)
  waiting for transfers between devices  38.8 us (25%)
  Pallas kernels  21.3 us (14%)
  blocking collectives  15.2 us (10%)
  local copies, waits for them, and re-layouts  4.66 us (3%)
    all_to_all x5, starting transfers between devices, exchange(): return lax.all_to_all(x, axes, split_axis=0, concat_axis=0, tiled=True)  46.9 us
    all_to_all x5, waiting for transfers between devices, exchange(): return lax.all_to_all(x, axes, split_axis=0, concat_axis=0, tiled=True)  26.3 us
    pallas_call x10, Pallas kernels, call(): pl.pallas_call(kernel, out_shape=outs, in_specs=[pl.BlockSpec(memory_spac...  21.3 us
    all_to_all x2, blocking collectives, exchange(): return lax.all_to_all(x, axes, split_axis=0, concat_axis=0, tiled=True)  15.2 us
    ppermute x3, starting transfers between devices, ahead(): return lax.ppermute(sent, 'x', [(i, (i + j) % nx) for i in range(nx)])  11.1 us
    ppermute x1, starting transfers between devices, body(): other = lax.ppermute(mine, 'c', [(0, 1), (1, 0)])  9.51 us
    ppermute x3, starting transfers between devices, body(): lax.ppermute(home[j], 'x', [(i, (i - j) % nx) for i in range(nx)])  7.81 us
    ppermute x3, waiting for transfers between devices, body(): lax.ppermute(home[j], 'x', [(i, (i - j) % nx) for i in range(nx)])  5.77 us
  transfers between devices with their start and end apart: 12, of which 10 were waited for; matrix products, arithmetic and copies ran while one was open for 0% of the time, Pallas kernels for 2%

profile of v10, /device:TPU:1, one launch (start us, length us, event | category | flops | bytes accessed | tf_op | source)
XLA Modules:
  0.0 156.2 jit_solution(17957291025373595702)
XLA Ops:
  2.1 15.7 %all-to-all-start = ((bf16[16,16,512]{2,1,0:T(8,128)(2,1)}), bf16[16,16,512]{2,1,0:T(8,128)(2,1)S(1)}, u32[]{:S(2)}, u32[]{:S(2)}) async-start(bf16[16,16,512]{2,1,0:T(8,128)(2,1)} %broadcast_in_dim.2), calls=%async_computation | async-start | bytes 524288 | tf_op jit(solution)/shard_map/all_to_all | solution.py:318
  21.6 3.1 %collective-permute-start = (bf16[144,512]{1,0:T(8,128)(2,1)S(1)}, bf16[144,512]{1,0:T(8,128)(2,1)S(1)}, u32[]{:S(2)}, u32[]{:S(2)}) collective-permute-start(bf16[144,512]{1,0:T(8,128)(2,1)S(1)} %get-tuple-element.36), channel_id=1, source_target_pairs={{0,32},{32,64},{64,96},{96,0},{1,33},{33,65},{65,97},{97,1},{2,34}... | collective-permute-start | bytes 442376 | tf_op jit(solution)/shard_map/ppermute | solution.py:344
  24.8 3.4 %collective-permute-start.1 = (bf16[144,512]{1,0:T(8,128)(2,1)S(1)}, bf16[144,512]{1,0:T(8,128)(2,1)S(1)}, u32[]{:S(2)}, u32[]{:S(2)}) collective-permute-start(bf16[144,512]{1,0:T(8,128)(2,1)S(1)} %get-tuple-element.37), channel_id=1, source_target_pairs={{0,96},{32,0},{64,32},{96,64},{1,97},{33,1},{65,33},{97,65},{2,98}... | collective-permute-start | bytes 442376 | tf_op jit(solution)/shard_map/ppermute | solution.py:344
  32.6 4.2 %all-to-all-start.1 = ((bf16[4,17,16,512]{3,2,1,0:T(8,128)(2,1)}), bf16[4,17,16,512]{3,2,1,0:T(8,128)(2,1)S(1)}, u32[]{:S(2)}, u32[]{:S(2)}) async-start(bf16[4,17,16,512]{3,2,1,0:T(8,128)(2,1)} %shard_map.77), calls=%async_computation.1 | async-start | bytes 2228224 | tf_op jit(solution)/shard_map/all_to_all | solution.py:318
  36.8 4.6 %collective-permute-start.2 = (bf16[144,512]{1,0:T(8,128)(2,1)S(1)}, bf16[144,512]{1,0:T(8,128)(2,1)S(1)}, u32[]{:S(2)}, u32[]{:S(2)}) collective-permute-start(bf16[144,512]{1,0:T(8,128)(2,1)S(1)} %get-tuple-element.41), channel_id=1, source_target_pairs={{0,64},{32,96},{64,0},{96,32},{1,65},{33,97},{65,1},{97,33},{2,66}... | collective-permute-start | bytes 442376 | tf_op jit(solution)/shard_map/ppermute | solution.py:344
  41.5 2.7 %collective-permute-done.2.refs_2_.r_4_ = bf16[144,512]{1,0:T(8,128)(2,1)S(1)} collective-permute-done((bf16[144,512]{1,0:T(8,128)(2,1)S(1)}, bf16[144,512]{1,0:T(8,128)(2,1)S(1)}, u32[]{:S(2)}, u32[]{:S(2)}) %collective-permute-start.2) | collective-permute-done | bytes 147488 | tf_op jit(solution)/shard_map/ppermute | solution.py:344
  44.2 2.7 %all-to-all-done.1.r_6_ = bf16[4,17,16,512]{3,2,1,0:T(8,128)(2,1)S(1)} async-done(((bf16[4,17,16,512]{3,2,1,0:T(8,128)(2,1)}), bf16[4,17,16,512]{3,2,1,0:T(8,128)(2,1)S(1)}, u32[]{:S(2)}, u32[]{:S(2)}) %all-to-all-start.1) | async-done | bytes 1114144 | tf_op jit(solution)/shard_map/all_to_all | solution.py:318
  46.9 9.5 %collective-permute-start.3 = (bf16[4,17,16,512]{3,2,1,0:T(8,128)(2,1)S(1)}, bf16[4,17,16,512]{3,2,1,0:T(8,128)(2,1)S(1)}, u32[]{:S(2)}, u32[]{:S(2)}) collective-permute-start(bf16[4,17,16,512]{3,2,1,0:T(8,128)(2,1)S(1)} %all-to-all-done.1.r_6_), channel_id=1, source_target_pairs={{0,16},{16,0},{1,17},{17,1},{2,18},{18,2},{3,19},{19,3},{4,20},{20... | collective-permute-start | bytes 3342344 | tf_op jit(solution)/shard_map/ppermute | solution.py:357
  58.8 2.9 %shard_map.79 = f32[4,8,640]{2,1,0:T(8,128)S(1)} custom-call(s32[32]{0:T(128)S(1)} %maximum_convert_fusion.r_0_, s32[3]{0:T(128)S(1)} %pad_add_fusion.ids_ref.r_1_, bf16[144,512]{1,0:T(8,128)(2,1)S(1)} %get-tuple-element.43.refs_0_.r_2_, bf16[144,512]{1,0:T(8,128)(2,1)S(1)} %collective-permute-done.refs_1_.r_3_, ...), custom_call_target="tpu_custom_call" | custom-call | flops 1000000000 | bytes 3000000 | tf_op jit(solution)/shard_map/pallas_call | solution.py:304
  61.7 8.4 %all_to_all.35.r_8_ = f32[4,8,640]{2,1,0:T(8,128)S(1)} all-to-all(f32[4,8,640]{2,1,0:T(8,128)S(1)} %shard_map.79), channel_id=1, replica_groups=mesh['y'=4,'x'=4,'c'=2,'z'=16] {'x'}, dimensions={0} | all-to-all | bytes 163840 | tf_op jit(solution)/shard_map/all_to_all | solution.py:318
  70.1 3.1 %shard_map.80 = (f32[4,8,512]{2,1,0:T(8,128)S(1)}, f32[8,512]{1,0:T(8,128)S(1)}) custom-call(s32[32]{0:T(128)S(1)} %maximum_convert_fusion.r_0_, s32[3]{0:T(128)S(1)} %pad_add_fusion.ids_ref.r_1_, bf16[144,512]{1,0:T(8,128)(2,1)S(1)} %get-tuple-element.43.refs_0_.r_2_, bf16[144,512]{1,0:T(8,128)(2,1)S(1)} %collective-permute-done.refs_1_.r_3_, ...), custom_call_target="tpu_custom_call" | custom-call | flops 1000000000 | bytes 3000000 | tf_op jit(solution)/shard_map/pallas_call | solution.py:304
  73.2 6.8 %all_to_all.36.r_8_ = f32[4,8,512]{2,1,0:T(8,128)S(1)} all-to-all(f32[4,8,512]{2,1,0:T(8,128)S(1)} %get-tuple-element.48), channel_id=1, replica_groups=mesh['y'=4,'x'=4,'c'=2,'z'=16] {'x'}, dimensions={0} | all-to-all | bytes 131072 | tf_op jit(solution)/shard_map/all_to_all | solution.py:318
  80.1 3.1 %shard_map.81 = (bf16[128,512]{1,0:T(8,128)(2,1)S(1)}, bf16[128,512]{1,0:T(8,128)(2,1)S(1)}, bf16[128,512]{1,0:T(8,128)(2,1)S(1)}, bf16[128,512]{1,0:T(8,128)(2,...) custom-call(s32[32]{0:T(128)S(1)} %maximum_convert_fusion.r_0_, ...), custom_call_target="tpu_custom_call" | custom-call | flops 1000000000 | bytes 3000000 | tf_op jit(solution)/shard_map/pallas_call | solution.py:304
  83.2 6.4 %all-to-all-start.4 = ((bf16[8,4,80,128]{3,2,1,0:T(8,128)(2,1)}), bf16[8,4,80,128]{3,2,1,0:T(8,128)(2,1)S(1)}, u32[]{:S(2)}, u32[]{:S(2)}) async-start(bf16[8,4,80,128]{3,2,1,0:T(8,128)(2,1)} %get-tuple-element.50), calls=%async_computation.4 | async-start | bytes 1310720 | tf_op jit(solution)/shard_map/all_to_all | solution.py:318
  89.7 10.8 %all-to-all-done.4 = bf16[8,4,80,128]{3,2,1,0:T(8,128)(2,1)S(1)} async-done(((bf16[8,4,80,128]{3,2,1,0:T(8,128)(2,1)}), bf16[8,4,80,128]{3,2,1,0:T(8,128)(2,1)S(1)}, u32[]{:S(2)}, u32[]{:S(2)}) %all-to-all-start.4) | async-done | bytes 655392 | tf_op jit(solution)/shard_map/all_to_all | solution.py:318
  100.5 5.1 %shard_map.82 = bf16[16,80,128]{2,1,0:T(8,128)(2,1)} custom-call(s32[256]{0:T(256)S(1)} %reshape.35.r_0_, s32[3]{0:T(128)S(1)} %pad_add_fusion.ids_ref.r_1_, bf16[32,80,128]{2,1,0:T(8,128)(2,1)S(1)} %bitcast.16, f32[16,128]{1,0:T(8,128)S(1)} %get-tuple-element.51.r_3_), custom_call_target="tpu_custom_call" | custom-call | flops 10000000000 | bytes 30000000 | tf_op jit(solution)/shard_map/pallas_call | solution.py:304
  105.6 10.2 %all-to-all-start.5 = ((bf16[16,80,128]{2,1,0:T(8,128)(2,1)}), bf16[16,80,128]{2,1,0:T(8,128)(2,1)S(1)}, u32[]{:S(2)}, u32[]{:S(2)}) async-start(bf16[16,80,128]{2,1,0:T(8,128)(2,1)} %shard_map.82), calls=%async_computation.5 | async-start | bytes 655360 | tf_op jit(solution)/shard_map/all_to_all | solution.py:318
  115.8 2.8 %collective-permute-start.4 = (bf16[128,512]{1,0:T(8,128)(2,1)S(1)}, bf16[128,512]{1,0:T(8,128)(2,1)S(1)}, u32[]{:S(2)}, u32[]{:S(2)}) collective-permute-start(bf16[128,512]{1,0:T(8,128)(2,1)S(1)} %get-tuple-element.58), channel_id=1, source_target_pairs={{0,96},{32,0},{64,32},{96,64},{1,97},{33,1},{65,33},{97,65},{2,98}... | collective-permute-start | bytes 393224 | tf_op jit(solution)/shard_map/ppermute | solution.py:415
  118.6 3.1 %collective-permute-start.5 = (bf16[128,512]{1,0:T(8,128)(2,1)S(1)}, bf16[128,512]{1,0:T(8,128)(2,1)S(1)}, u32[]{:S(2)}, u32[]{:S(2)}) collective-permute-start(bf16[128,512]{1,0:T(8,128)(2,1)S(1)} %get-tuple-element.59), channel_id=1, source_target_pairs={{0,64},{32,96},{64,0},{96,32},{1,65},{33,97},{65,1},{97,33},{2,66}... | collective-permute-start | bytes 393224 | tf_op jit(solution)/shard_map/ppermute | solution.py:415
  121.7 1.9 %collective-permute-start.6 = (bf16[128,512]{1,0:T(8,128)(2,1)S(1)}, bf16[128,512]{1,0:T(8,128)(2,1)S(1)}, u32[]{:S(2)}, u32[]{:S(2)}) collective-permute-start(bf16[128,512]{1,0:T(8,128)(2,1)S(1)} %get-tuple-element.60), channel_id=1, source_target_pairs={{0,32},{32,64},{64,96},{96,0},{1,33},{33,65},{65,97},{97,1},{2,34}... | collective-permute-start | bytes 393224 | tf_op jit(solution)/shard_map/ppermute | solution.py:415
  123.7 2.2 %collective-permute-done.5.refs_2_ = bf16[128,512]{1,0:T(8,128)(2,1)S(1)} collective-permute-done((bf16[128,512]{1,0:T(8,128)(2,1)S(1)}, bf16[128,512]{1,0:T(8,128)(2,1)S(1)}, u32[]{:S(2)}, u32[]{:S(2)}) %collective-permute-start.5) | collective-permute-done | bytes 131104 | tf_op jit(solution)/shard_map/ppermute | solution.py:415
  125.8 3.6 %collective-permute-done.6.refs_3_ = bf16[128,512]{1,0:T(8,128)(2,1)S(1)} collective-permute-done((bf16[128,512]{1,0:T(8,128)(2,1)S(1)}, bf16[128,512]{1,0:T(8,128)(2,1)S(1)}, u32[]{:S(2)}, u32[]{:S(2)}) %collective-permute-start.6) | collective-permute-done | bytes 131104 | tf_op jit(solution)/shard_map/ppermute | solution.py:415
  131.5 10.4 %all-to-all-start.6 = ((bf16[32,80,128]{2,1,0:T(8,128)(2,1)}), bf16[32,80,128]{2,1,0:T(8,128)(2,1)S(1)}, u32[]{:S(2)}, u32[]{:S(2)}) async-start(bf16[32,80,128]{2,1,0:T(8,128)(2,1)} %shard_map.83), calls=%async_computation.6 | async-start | bytes 1310720 | tf_op jit(solution)/shard_map/all_to_all | solution.py:318
  143.2 11.6 %all-to-all-done.6.r_0_ = bf16[32,80,128]{2,1,0:T(8,128)(2,1)S(1)} async-done(((bf16[32,80,128]{2,1,0:T(8,128)(2,1)}), bf16[32,80,128]{2,1,0:T(8,128)(2,1)S(1)}, u32[]{:S(2)}, u32[]{:S(2)}) %all-to-all-start.6) | async-done | bytes 655392 | tf_op jit(solution)/shard_map/all_to_all | solution.py:318
  (32 shorter events, 16.9 us)
Async XLA Ops:
  2.1 28.9 %all-to-all-start = ((bf16[16,16,512]{2,1,0:T(8,128)(2,1)}), bf16[16,16,512]{2,1,0:T(8,128)(2,1)S(1)}, u32[]{:S(2)}, u32[]{:S(2)}) async-start(bf16[16,16,512]{2,1,0:T(8,128)(2,1)} %broadcast_in_dim.2), calls=%async_computation | async-start | bytes 524288 | tf_op jit(solution)/shard_map/all_to_all | solution.py:318
  17.9 1.0 copy-start.1
  19.0 0.7 copy-start.2
  19.7 0.7 copy-start.3
  20.3 0.7 copy-start.4
  21.0 10.0 %copy-start.5 = (s32[4,2]{0,1:T(2,128)S(1)}, s32[4,2]{0,1:T(2,128)}, u32[]{:S(2)}) copy-start(s32[4,2]{0,1:T(2,128)} %param.8) | copy-start | bytes 100
  21.6 7.5 %collective-permute-start = (bf16[144,512]{1,0:T(8,128)(2,1)S(1)}, bf16[144,512]{1,0:T(8,128)(2,1)S(1)}, u32[]{:S(2)}, u32[]{:S(2)}) collective-permute-start(bf16[144,512]{1,0:T(8,128)(2,1)S(1)} %get-tuple-element.36), channel_id=1, source_target_pairs={{0,32},{32,64},{64,96},{96,0},{1,33},{33,65},{65,97},{97,1},{2,34}... | collective-permute-start | bytes 442376 | tf_op jit(solution)/shard_map/ppermute | solution.py:344
  24.8 6.2 %collective-permute-start.1 = (bf16[144,512]{1,0:T(8,128)(2,1)S(1)}, bf16[144,512]{1,0:T(8,128)(2,1)S(1)}, u32[]{:S(2)}, u32[]{:S(2)}) collective-permute-start(bf16[144,512]{1,0:T(8,128)(2,1)S(1)} %get-tuple-element.37), channel_id=1, source_target_pairs={{0,96},{32,0},{64,32},{96,64},{1,97},{33,1},{65,33},{97,65},{2,98}... | collective-permute-start | bytes 442376 | tf_op jit(solution)/shard_map/ppermute | solution.py:344
  32.6 14.3 %all-to-all-start.1 = ((bf16[4,17,16,512]{3,2,1,0:T(8,128)(2,1)}), bf16[4,17,16,512]{3,2,1,0:T(8,128)(2,1)S(1)}, u32[]{:S(2)}, u32[]{:S(2)}) async-start(bf16[4,17,16,512]{3,2,1,0:T(8,128)(2,1)} %shard_map.77), calls=%async_computation.1 | async-start | bytes 2228224 | tf_op jit(solution)/shard_map/all_to_all | solution.py:318
  36.8 7.4 %collective-permute-start.2 = (bf16[144,512]{1,0:T(8,128)(2,1)S(1)}, bf16[144,512]{1,0:T(8,128)(2,1)S(1)}, u32[]{:S(2)}, u32[]{:S(2)}) collective-permute-start(bf16[144,512]{1,0:T(8,128)(2,1)S(1)} %get-tuple-element.41), channel_id=1, source_target_pairs={{0,64},{32,96},{64,0},{96,32},{1,65},{33,97},{65,1},{97,33},{2,66}... | collective-permute-start | bytes 442376 | tf_op jit(solution)/shard_map/ppermute | solution.py:344
  46.9 11.9 %collective-permute-start.3 = (bf16[4,17,16,512]{3,2,1,0:T(8,128)(2,1)S(1)}, bf16[4,17,16,512]{3,2,1,0:T(8,128)(2,1)S(1)}, u32[]{:S(2)}, u32[]{:S(2)}) collective-permute-start(bf16[4,17,16,512]{3,2,1,0:T(8,128)(2,1)S(1)} %all-to-all-done.1.r_6_), channel_id=1, source_target_pairs={{0,16},{16,0},{1,17},{17,1},{2,18},{18,2},{3,19},{19,3},{4,20},{20... | collective-permute-start | bytes 3342344 | tf_op jit(solution)/shard_map/ppermute | solution.py:357
  83.2 17.3 %all-to-all-start.4 = ((bf16[8,4,80,128]{3,2,1,0:T(8,128)(2,1)}), bf16[8,4,80,128]{3,2,1,0:T(8,128)(2,1)S(1)}, u32[]{:S(2)}, u32[]{:S(2)}) async-start(bf16[8,4,80,128]{3,2,1,0:T(8,128)(2,1)} %get-tuple-element.50), calls=%async_computation.4 | async-start | bytes 1310720 | tf_op jit(solution)/shard_map/all_to_all | solution.py:318
  105.6 24.9 %all-to-all-start.5 = ((bf16[16,80,128]{2,1,0:T(8,128)(2,1)}), bf16[16,80,128]{2,1,0:T(8,128)(2,1)S(1)}, u32[]{:S(2)}, u32[]{:S(2)}) async-start(bf16[16,80,128]{2,1,0:T(8,128)(2,1)} %shard_map.82), calls=%async_computation.5 | async-start | bytes 655360 | tf_op jit(solution)/shard_map/all_to_all | solution.py:318
  115.8 7.8 %collective-permute-start.4 = (bf16[128,512]{1,0:T(8,128)(2,1)S(1)}, bf16[128,512]{1,0:T(8,128)(2,1)S(1)}, u32[]{:S(2)}, u32[]{:S(2)}) collective-permute-start(bf16[128,512]{1,0:T(8,128)(2,1)S(1)} %get-tuple-element.58), channel_id=1, source_target_pairs={{0,96},{32,0},{64,32},{96,64},{1,97},{33,1},{65,33},{97,65},{2,98}... | collective-permute-start | bytes 393224 | tf_op jit(solution)/shard_map/ppermute | solution.py:415
  118.6 7.2 %collective-permute-start.5 = (bf16[128,512]{1,0:T(8,128)(2,1)S(1)}, bf16[128,512]{1,0:T(8,128)(2,1)S(1)}, u32[]{:S(2)}, u32[]{:S(2)}) collective-permute-start(bf16[128,512]{1,0:T(8,128)(2,1)S(1)} %get-tuple-element.59), channel_id=1, source_target_pairs={{0,64},{32,96},{64,0},{96,32},{1,65},{33,97},{65,1},{97,33},{2,66}... | collective-permute-start | bytes 393224 | tf_op jit(solution)/shard_map/ppermute | solution.py:415
  121.7 7.7 %collective-permute-start.6 = (bf16[128,512]{1,0:T(8,128)(2,1)S(1)}, bf16[128,512]{1,0:T(8,128)(2,1)S(1)}, u32[]{:S(2)}, u32[]{:S(2)}) collective-permute-start(bf16[128,512]{1,0:T(8,128)(2,1)S(1)} %get-tuple-element.60), channel_id=1, source_target_pairs={{0,32},{32,64},{64,96},{96,0},{1,33},{33,65},{65,97},{97,1},{2,34}... | collective-permute-start | bytes 393224 | tf_op jit(solution)/shard_map/ppermute | solution.py:415
  131.5 23.4 %all-to-all-start.6 = ((bf16[32,80,128]{2,1,0:T(8,128)(2,1)}), bf16[32,80,128]{2,1,0:T(8,128)(2,1)S(1)}, u32[]{:S(2)}, u32[]{:S(2)}) async-start(bf16[32,80,128]{2,1,0:T(8,128)(2,1)} %shard_map.83), calls=%async_computation.6 | async-start | bytes 1310720 | tf_op jit(solution)/shard_map/all_to_all | solution.py:318
  141.8 13.0 %copy-start = (bf16[128,2048]{1,0:T(8,128)(2,1)S(1)}, bf16[128,2048]{1,0:T(8,128)(2,1)}, u32[]{:S(2)}) copy-start(bf16[128,2048]{1,0:T(8,128)(2,1)} %r_1_.1) | copy-start | bytes 1572868

commit v11 on v10

--- a/solution.py
+++ b/solution.py
@@ -299,7 +299,7 @@
         ).astype(BF16)
 
 
-def call(kernel, ins, outs, scratch, *args, us=1):
+def call(kernel, ins, outs, scratch, *args, us=1, limit=VMEM_LIMIT):
     spaces = {"v": pltpu.VMEM, "s": pltpu.SMEM}
     return pl.pallas_call(
         kernel,
@@ -310,7 +310,7 @@
         cost_estimate=pl.CostEstimate(
             flops=us * 10**9, bytes_accessed=us * 3 * 10**6, transcendentals=0
         ),
-        compiler_params=pltpu.CompilerParams(vmem_limit_bytes=VMEM_LIMIT),
+        compiler_params=pltpu.CompilerParams(vmem_limit_bytes=limit),
     )(*args)
 
 
@@ -336,7 +336,7 @@
         "ssvvv",
         tuple(sds((rows + 16, width), BF16) for _ in range(nx)),
         [],
-        block_shards.T, ids, patches, codes.T, support.T,
+        block_shards.T, ids, patches, codes.T, support.T, limit=56 * 1024 * 1024,
     )
     own = lax.dynamic_slice(dictionary, ((y * nc + c) * piece, x * width), (piece, width))
     by_z = spread(own, "z", nz).reshape(nz, piece, width)

time: 157 us -> 157 us (level)
  local copies, waits for them, and re-layouts: 4.66 us -> 1.58 us
    unnamed x12 -> x10, local copies, waits for them, and re-layouts: 3.1 us -> 0.02 us
  transfers between devices with their start and end apart: 12 -> 12, of which waited for: 10 -> 11; matrix products, arithmetic and copies ran while one was open for 0% -> 1% of each run, Pallas kernels for 2% -> 3%
where the time goes in v11:
time: 157 us; the launch traced here: 156 us
  starting transfers between devices  75.2 us (48%)
  waiting for transfers between devices  40.1 us (26%)
  Pallas kernels  22.6 us (14%)
  blocking collectives  15.2 us (10%)
  local copies, waits for them, and re-layouts  1.58 us (1%)
    all_to_all x5, starting transfers between devices, exchange(): return lax.all_to_all(x, axes, split_axis=0, concat_axis=0, tiled=True)  46.8 us
    all_to_all x5, waiting for transfers between devices, exchange(): return lax.all_to_all(x, axes, split_axis=0, concat_axis=0, tiled=True)  27.4 us
    pallas_call x10, Pallas kernels, call(): pl.pallas_call(kernel, out_shape=outs, in_specs=[pl.BlockSpec(memory_spac...  22.6 us
    all_to_all x2, blocking collectives, exchange(): return lax.all_to_all(x, axes, split_axis=0, concat_axis=0, tiled=True)  15.2 us
    ppermute x3, starting transfers between devices, ahead(): return lax.ppermute(sent, 'x', [(i, (i + j) % nx) for i in range(nx)])  11.1 us
    ppermute x1, starting transfers between devices, body(): other = lax.ppermute(mine, 'c', [(0, 1), (1, 0)])  9.51 us
    ppermute x3, starting transfers between devices, body(): lax.ppermute(home[j], 'x', [(i, (i - j) % nx) for i in range(nx)])  7.81 us
    ppermute x3, waiting for transfers between devices, body(): lax.ppermute(home[j], 'x', [(i, (i - j) % nx) for i in range(nx)])  5.77 us
  transfers between devices with their start and end apart: 12, of which 11 were waited for; matrix products, arithmetic and copies ran while one was open for 1% of the time, Pallas kernels for 3%

profile of v11, /device:TPU:1, one launch (start us, length us, event | category | flops | bytes accessed | tf_op | source)
XLA Modules:
  0.0 156.2 jit_solution(7125528524209829015)
XLA Ops:
  2.1 15.7 %all-to-all-start = ((bf16[16,16,512]{2,1,0:T(8,128)(2,1)}), bf16[16,16,512]{2,1,0:T(8,128)(2,1)S(1)}, u32[]{:S(2)}, u32[]{:S(2)}) async-start(bf16[16,16,512]{2,1,0:T(8,128)(2,1)} %broadcast_in_dim.2), calls=%async_computation | async-start | bytes 524288 | tf_op jit(solution)/shard_map/all_to_all | solution.py:318
  20.4 3.1 %collective-permute-start = (bf16[144,512]{1,0:T(8,128)(2,1)}, bf16[144,512]{1,0:T(8,128)(2,1)S(1)}, u32[]{:S(2)}, u32[]{:S(2)}) collective-permute-start(bf16[144,512]{1,0:T(8,128)(2,1)} %get-tuple-element.36), channel_id=1, source_target_pairs={{0,32},{32,64},{64,96},{96,0},{1,33},{33,65},{65,97},{97,1},{2,34}... | collective-permute-start | bytes 442376 | tf_op jit(solution)/shard_map/ppermute | solution.py:344
  23.5 3.4 %collective-permute-start.1 = (bf16[144,512]{1,0:T(8,128)(2,1)}, bf16[144,512]{1,0:T(8,128)(2,1)S(1)}, u32[]{:S(2)}, u32[]{:S(2)}) collective-permute-start(bf16[144,512]{1,0:T(8,128)(2,1)} %get-tuple-element.37), channel_id=1, source_target_pairs={{0,96},{32,0},{64,32},{96,64},{1,97},{33,1},{65,33},{97,65},{2,98}... | collective-permute-start | bytes 442376 | tf_op jit(solution)/shard_map/ppermute | solution.py:344
  32.6 4.3 %all-to-all-start.1 = ((bf16[4,17,16,512]{3,2,1,0:T(8,128)(2,1)}), bf16[4,17,16,512]{3,2,1,0:T(8,128)(2,1)S(1)}, u32[]{:S(2)}, u32[]{:S(2)}) async-start(bf16[4,17,16,512]{3,2,1,0:T(8,128)(2,1)} %shard_map.77), calls=%async_computation.1 | async-start | bytes 2228224 | tf_op jit(solution)/shard_map/all_to_all | solution.py:318
  37.0 4.6 %collective-permute-start.2 = (bf16[144,512]{1,0:T(8,128)(2,1)S(1)}, bf16[144,512]{1,0:T(8,128)(2,1)S(1)}, u32[]{:S(2)}, u32[]{:S(2)}) collective-permute-start(bf16[144,512]{1,0:T(8,128)(2,1)S(1)} %copy-done.4), channel_id=1, source_target_pairs={{0,64},{32,96},{64,0},{96,32},{1,65},{33,97},{65,1},{97,33},{2,66}... | collective-permute-start | bytes 442376 | tf_op jit(solution)/shard_map/ppermute | solution.py:344
  41.6 2.7 %collective-permute-done.2.refs_2_.r_4_ = bf16[144,512]{1,0:T(8,128)(2,1)S(1)} collective-permute-done((bf16[144,512]{1,0:T(8,128)(2,1)S(1)}, bf16[144,512]{1,0:T(8,128)(2,1)S(1)}, u32[]{:S(2)}, u32[]{:S(2)}) %collective-permute-start.2) | collective-permute-done | bytes 147488 | tf_op jit(solution)/shard_map/ppermute | solution.py:344
  44.3 2.7 %all-to-all-done.1.r_6_ = bf16[4,17,16,512]{3,2,1,0:T(8,128)(2,1)S(1)} async-done(((bf16[4,17,16,512]{3,2,1,0:T(8,128)(2,1)}), bf16[4,17,16,512]{3,2,1,0:T(8,128)(2,1)S(1)}, u32[]{:S(2)}, u32[]{:S(2)}) %all-to-all-start.1) | async-done | bytes 1114144 | tf_op jit(solution)/shard_map/all_to_all | solution.py:318
  47.0 9.5 %collective-permute-start.3 = (bf16[4,17,16,512]{3,2,1,0:T(8,128)(2,1)S(1)}, bf16[4,17,16,512]{3,2,1,0:T(8,128)(2,1)S(1)}, u32[]{:S(2)}, u32[]{:S(2)}) collective-permute-start(bf16[4,17,16,512]{3,2,1,0:T(8,128)(2,1)S(1)} %all-to-all-done.1.r_6_), channel_id=1, source_target_pairs={{0,16},{16,0},{1,17},{17,1},{2,18},{18,2},{3,19},{19,3},{4,20},{20... | collective-permute-start | bytes 3342344 | tf_op jit(solution)/shard_map/ppermute | solution.py:357
  58.9 2.9 %shard_map.79 = f32[4,8,640]{2,1,0:T(8,128)S(1)} custom-call(s32[32]{0:T(128)S(1)} %maximum_convert_fusion.r_0_, s32[3]{0:T(128)S(1)} %copy-done.1, bf16[144,512]{1,0:T(8,128)(2,1)S(1)} %copy-done.2, bf16[144,512]{1,0:T(8,128)(2,1)S(1)} %collective-permute-done.refs_1_.r_3_, bf16[144,512]{1,0:T(8,128)(2,1)S(1)} %collective-permute-done.2.refs_2_.r_4_, ...), custom_call_target="tpu_custom_call" | custom-call | flops 1000000000 | bytes 3000000 | tf_op jit(solution)/shard_map/pallas_call | solution.py:304
  61.9 8.4 %all_to_all.35.r_8_ = f32[4,8,640]{2,1,0:T(8,128)S(1)} all-to-all(f32[4,8,640]{2,1,0:T(8,128)S(1)} %shard_map.79), channel_id=1, replica_groups=mesh['y'=4,'x'=4,'c'=2,'z'=16] {'x'}, dimensions={0} | all-to-all | bytes 163840 | tf_op jit(solution)/shard_map/all_to_all | solution.py:318
  70.2 3.1 %shard_map.80 = (f32[4,8,512]{2,1,0:T(8,128)S(1)}, f32[8,512]{1,0:T(8,128)S(1)}) custom-call(s32[32]{0:T(128)S(1)} %maximum_convert_fusion.r_0_, s32[3]{0:T(128)S(1)} %copy-done.1, bf16[144,512]{1,0:T(8,128)(2,1)S(1)} %copy-done.2, bf16[144,512]{1,0:T(8,128)(2,1)S(1)} %collective-permute-done.refs_1_.r_3_, ...), custom_call_target="tpu_custom_call" | custom-call | flops 1000000000 | bytes 3000000 | tf_op jit(solution)/shard_map/pallas_call | solution.py:304
  73.4 6.8 %all_to_all.36.r_8_ = f32[4,8,512]{2,1,0:T(8,128)S(1)} all-to-all(f32[4,8,512]{2,1,0:T(8,128)S(1)} %get-tuple-element.48), channel_id=1, replica_groups=mesh['y'=4,'x'=4,'c'=2,'z'=16] {'x'}, dimensions={0} | all-to-all | bytes 131072 | tf_op jit(solution)/shard_map/all_to_all | solution.py:318
  80.2 3.1 %shard_map.81 = (bf16[128,512]{1,0:T(8,128)(2,1)S(1)}, bf16[128,512]{1,0:T(8,128)(2,1)S(1)}, bf16[128,512]{1,0:T(8,128)(2,1)S(1)}, bf16[128,512]{1,0:T(8,128)(2,...) custom-call(s32[32]{0:T(128)S(1)} %maximum_convert_fusion.r_0_, s32[3]{0:T(128)S(1)} %copy-done.1, ...), custom_call_target="tpu_custom_call" | custom-call | flops 1000000000 | bytes 3000000 | tf_op jit(solution)/shard_map/pallas_call | solution.py:304
  83.4 6.4 %all-to-all-start.4 = ((bf16[8,4,80,128]{3,2,1,0:T(8,128)(2,1)}), bf16[8,4,80,128]{3,2,1,0:T(8,128)(2,1)S(1)}, u32[]{:S(2)}, u32[]{:S(2)}) async-start(bf16[8,4,80,128]{3,2,1,0:T(8,128)(2,1)} %get-tuple-element.50), calls=%async_computation.4 | async-start | bytes 1310720 | tf_op jit(solution)/shard_map/all_to_all | solution.py:318
  89.9 10.8 %all-to-all-done.4 = bf16[8,4,80,128]{3,2,1,0:T(8,128)(2,1)S(1)} async-done(((bf16[8,4,80,128]{3,2,1,0:T(8,128)(2,1)}), bf16[8,4,80,128]{3,2,1,0:T(8,128)(2,1)S(1)}, u32[]{:S(2)}, u32[]{:S(2)}) %all-to-all-start.4) | async-done | bytes 655392 | tf_op jit(solution)/shard_map/all_to_all | solution.py:318
  100.7 5.1 %shard_map.82 = bf16[16,80,128]{2,1,0:T(8,128)(2,1)} custom-call(s32[256]{0:T(256)S(1)} %reshape.35.r_0_, s32[3]{0:T(128)S(1)} %copy-done.1, bf16[32,80,128]{2,1,0:T(8,128)(2,1)S(1)} %bitcast.16, f32[16,128]{1,0:T(8,128)S(1)} %get-tuple-element.51.r_3_), custom_call_target="tpu_custom_call" | custom-call | flops 10000000000 | bytes 30000000 | tf_op jit(solution)/shard_map/pallas_call | solution.py:304
  105.8 10.0 %all-to-all-start.5 = ((bf16[16,80,128]{2,1,0:T(8,128)(2,1)}), bf16[16,80,128]{2,1,0:T(8,128)(2,1)S(1)}, u32[]{:S(2)}, u32[]{:S(2)}) async-start(bf16[16,80,128]{2,1,0:T(8,128)(2,1)} %shard_map.82), calls=%async_computation.5 | async-start | bytes 655360 | tf_op jit(solution)/shard_map/all_to_all | solution.py:318
  115.8 2.8 %collective-permute-start.4 = (bf16[128,512]{1,0:T(8,128)(2,1)S(1)}, bf16[128,512]{1,0:T(8,128)(2,1)S(1)}, u32[]{:S(2)}, u32[]{:S(2)}) collective-permute-start(bf16[128,512]{1,0:T(8,128)(2,1)S(1)} %get-tuple-element.58), channel_id=1, source_target_pairs={{0,96},{32,0},{64,32},{96,64},{1,97},{33,1},{65,33},{97,65},{2,98}... | collective-permute-start | bytes 393224 | tf_op jit(solution)/shard_map/ppermute | solution.py:415
  118.6 3.1 %collective-permute-start.5 = (bf16[128,512]{1,0:T(8,128)(2,1)S(1)}, bf16[128,512]{1,0:T(8,128)(2,1)S(1)}, u32[]{:S(2)}, u32[]{:S(2)}) collective-permute-start(bf16[128,512]{1,0:T(8,128)(2,1)S(1)} %get-tuple-element.59), channel_id=1, source_target_pairs={{0,64},{32,96},{64,0},{96,32},{1,65},{33,97},{65,1},{97,33},{2,66}... | collective-permute-start | bytes 393224 | tf_op jit(solution)/shard_map/ppermute | solution.py:415
  121.7 1.9 %collective-permute-start.6 = (bf16[128,512]{1,0:T(8,128)(2,1)S(1)}, bf16[128,512]{1,0:T(8,128)(2,1)S(1)}, u32[]{:S(2)}, u32[]{:S(2)}) collective-permute-start(bf16[128,512]{1,0:T(8,128)(2,1)S(1)} %get-tuple-element.60), channel_id=1, source_target_pairs={{0,32},{32,64},{64,96},{96,0},{1,33},{33,65},{65,97},{97,1},{2,34}... | collective-permute-start | bytes 393224 | tf_op jit(solution)/shard_map/ppermute | solution.py:415
  123.6 2.2 %collective-permute-done.5.refs_2_ = bf16[128,512]{1,0:T(8,128)(2,1)S(1)} collective-permute-done((bf16[128,512]{1,0:T(8,128)(2,1)S(1)}, bf16[128,512]{1,0:T(8,128)(2,1)S(1)}, u32[]{:S(2)}, u32[]{:S(2)}) %collective-permute-start.5) | collective-permute-done | bytes 131104 | tf_op jit(solution)/shard_map/ppermute | solution.py:415
  125.8 3.6 %collective-permute-done.6.refs_3_ = bf16[128,512]{1,0:T(8,128)(2,1)S(1)} collective-permute-done((bf16[128,512]{1,0:T(8,128)(2,1)S(1)}, bf16[128,512]{1,0:T(8,128)(2,1)S(1)}, u32[]{:S(2)}, u32[]{:S(2)}) %collective-permute-start.6) | collective-permute-done | bytes 131104 | tf_op jit(solution)/shard_map/ppermute | solution.py:415
  131.5 10.3 %all-to-all-start.6 = ((bf16[32,80,128]{2,1,0:T(8,128)(2,1)}), bf16[32,80,128]{2,1,0:T(8,128)(2,1)S(1)}, u32[]{:S(2)}, u32[]{:S(2)}) async-start(bf16[32,80,128]{2,1,0:T(8,128)(2,1)} %shard_map.83), calls=%async_computation.6 | async-start | bytes 1310720 | tf_op jit(solution)/shard_map/all_to_all | solution.py:318
  143.2 11.6 %all-to-all-done.6.r_0_ = bf16[32,80,128]{2,1,0:T(8,128)(2,1)S(1)} async-done(((bf16[32,80,128]{2,1,0:T(8,128)(2,1)}), bf16[32,80,128]{2,1,0:T(8,128)(2,1)S(1)}, u32[]{:S(2)}, u32[]{:S(2)}) %all-to-all-start.6) | async-done | bytes 655392 | tf_op jit(solution)/shard_map/all_to_all | solution.py:318
  (30 shorter events, 17.0 us)
Async XLA Ops:
  2.1 28.9 %all-to-all-start = ((bf16[16,16,512]{2,1,0:T(8,128)(2,1)}), bf16[16,16,512]{2,1,0:T(8,128)(2,1)S(1)}, u32[]{:S(2)}, u32[]{:S(2)}) async-start(bf16[16,16,512]{2,1,0:T(8,128)(2,1)} %broadcast_in_dim.2), calls=%async_computation | async-start | bytes 524288 | tf_op jit(solution)/shard_map/all_to_all | solution.py:318
  18.5 12.5 %copy-start.3 = (s32[4,2]{0,1:T(2,128)S(1)}, s32[4,2]{0,1:T(2,128)}, u32[]{:S(2)}) copy-start(s32[4,2]{0,1:T(2,128)} %param.8) | copy-start | bytes 100
  20.4 7.7 %collective-permute-start = (bf16[144,512]{1,0:T(8,128)(2,1)}, bf16[144,512]{1,0:T(8,128)(2,1)S(1)}, u32[]{:S(2)}, u32[]{:S(2)}) collective-permute-start(bf16[144,512]{1,0:T(8,128)(2,1)} %get-tuple-element.36), channel_id=1, source_target_pairs={{0,32},{32,64},{64,96},{96,0},{1,33},{33,65},{65,97},{97,1},{2,34}... | collective-permute-start | bytes 442376 | tf_op jit(solution)/shard_map/ppermute | solution.py:344
  23.5 6.4 %collective-permute-start.1 = (bf16[144,512]{1,0:T(8,128)(2,1)}, bf16[144,512]{1,0:T(8,128)(2,1)S(1)}, u32[]{:S(2)}, u32[]{:S(2)}) collective-permute-start(bf16[144,512]{1,0:T(8,128)(2,1)} %get-tuple-element.37), channel_id=1, source_target_pairs={{0,96},{32,0},{64,32},{96,64},{1,97},{33,1},{65,33},{97,65},{2,98}... | collective-permute-start | bytes 442376 | tf_op jit(solution)/shard_map/ppermute | solution.py:344
  32.6 4.3 %copy-start.4 = (bf16[144,512]{1,0:T(8,128)(2,1)S(1)}, bf16[144,512]{1,0:T(8,128)(2,1)}, u32[]{:S(2)}) copy-start(bf16[144,512]{1,0:T(8,128)(2,1)} %get-tuple-element.41) | copy-start | bytes 442372
  32.6 23.9 %copy-start.1 = (s32[3]{0:T(128)S(1)}, s32[3]{0:T(128)}, u32[]{:S(2)}) copy-start(s32[3]{0:T(128)} %pad_add_fusion.ids_ref.r_1_) | copy-start | bytes 40
  32.6 23.9 %copy-start.2 = (bf16[144,512]{1,0:T(8,128)(2,1)S(1)}, bf16[144,512]{1,0:T(8,128)(2,1)}, u32[]{:S(2)}) copy-start(bf16[144,512]{1,0:T(8,128)(2,1)} %get-tuple-element.43.refs_0_.r_2_) | copy-start | bytes 442372
  32.6 14.4 %all-to-all-start.1 = ((bf16[4,17,16,512]{3,2,1,0:T(8,128)(2,1)}), bf16[4,17,16,512]{3,2,1,0:T(8,128)(2,1)S(1)}, u32[]{:S(2)}, u32[]{:S(2)}) async-start(bf16[4,17,16,512]{3,2,1,0:T(8,128)(2,1)} %shard_map.77), calls=%async_computation.1 | async-start | bytes 2228224 | tf_op jit(solution)/shard_map/all_to_all | solution.py:318
  37.0 7.4 %collective-permute-start.2 = (bf16[144,512]{1,0:T(8,128)(2,1)S(1)}, bf16[144,512]{1,0:T(8,128)(2,1)S(1)}, u32[]{:S(2)}, u32[]{:S(2)}) collective-permute-start(bf16[144,512]{1,0:T(8,128)(2,1)S(1)} %copy-done.4), channel_id=1, source_target_pairs={{0,64},{32,96},{64,0},{96,32},{1,65},{33,97},{65,1},{97,33},{2,66}... | collective-permute-start | bytes 442376 | tf_op jit(solution)/shard_map/ppermute | solution.py:344
  47.0 11.9 %collective-permute-start.3 = (bf16[4,17,16,512]{3,2,1,0:T(8,128)(2,1)S(1)}, bf16[4,17,16,512]{3,2,1,0:T(8,128)(2,1)S(1)}, u32[]{:S(2)}, u32[]{:S(2)}) collective-permute-start(bf16[4,17,16,512]{3,2,1,0:T(8,128)(2,1)S(1)} %all-to-all-done.1.r_6_), channel_id=1, source_target_pairs={{0,16},{16,0},{1,17},{17,1},{2,18},{18,2},{3,19},{19,3},{4,20},{20... | collective-permute-start | bytes 3342344 | tf_op jit(solution)/shard_map/ppermute | solution.py:357
  83.4 17.3 %all-to-all-start.4 = ((bf16[8,4,80,128]{3,2,1,0:T(8,128)(2,1)}), bf16[8,4,80,128]{3,2,1,0:T(8,128)(2,1)S(1)}, u32[]{:S(2)}, u32[]{:S(2)}) async-start(bf16[8,4,80,128]{3,2,1,0:T(8,128)(2,1)} %get-tuple-element.50), calls=%async_computation.4 | async-start | bytes 1310720 | tf_op jit(solution)/shard_map/all_to_all | solution.py:318
  105.8 24.8 %all-to-all-start.5 = ((bf16[16,80,128]{2,1,0:T(8,128)(2,1)}), bf16[16,80,128]{2,1,0:T(8,128)(2,1)S(1)}, u32[]{:S(2)}, u32[]{:S(2)}) async-start(bf16[16,80,128]{2,1,0:T(8,128)(2,1)} %shard_map.82), calls=%async_computation.5 | async-start | bytes 655360 | tf_op jit(solution)/shard_map/all_to_all | solution.py:318
  115.8 7.8 %collective-permute-start.4 = (bf16[128,512]{1,0:T(8,128)(2,1)S(1)}, bf16[128,512]{1,0:T(8,128)(2,1)S(1)}, u32[]{:S(2)}, u32[]{:S(2)}) collective-permute-start(bf16[128,512]{1,0:T(8,128)(2,1)S(1)} %get-tuple-element.58), channel_id=1, source_target_pairs={{0,96},{32,0},{64,32},{96,64},{1,97},{33,1},{65,33},{97,65},{2,98}... | collective-permute-start | bytes 393224 | tf_op jit(solution)/shard_map/ppermute | solution.py:415
  118.6 7.2 %collective-permute-start.5 = (bf16[128,512]{1,0:T(8,128)(2,1)S(1)}, bf16[128,512]{1,0:T(8,128)(2,1)S(1)}, u32[]{:S(2)}, u32[]{:S(2)}) collective-permute-start(bf16[128,512]{1,0:T(8,128)(2,1)S(1)} %get-tuple-element.59), channel_id=1, source_target_pairs={{0,64},{32,96},{64,0},{96,32},{1,65},{33,97},{65,1},{97,33},{2,66}... | collective-permute-start | bytes 393224 | tf_op jit(solution)/shard_map/ppermute | solution.py:415
  121.7 7.7 %collective-permute-start.6 = (bf16[128,512]{1,0:T(8,128)(2,1)S(1)}, bf16[128,512]{1,0:T(8,128)(2,1)S(1)}, u32[]{:S(2)}, u32[]{:S(2)}) collective-permute-start(bf16[128,512]{1,0:T(8,128)(2,1)S(1)} %get-tuple-element.60), channel_id=1, source_target_pairs={{0,32},{32,64},{64,96},{96,0},{1,33},{33,65},{65,97},{97,1},{2,34}... | collective-permute-start | bytes 393224 | tf_op jit(solution)/shard_map/ppermute | solution.py:415
  131.5 23.3 %all-to-all-start.6 = ((bf16[32,80,128]{2,1,0:T(8,128)(2,1)}), bf16[32,80,128]{2,1,0:T(8,128)(2,1)S(1)}, u32[]{:S(2)}, u32[]{:S(2)}) async-start(bf16[32,80,128]{2,1,0:T(8,128)(2,1)} %shard_map.83), calls=%async_computation.6 | async-start | bytes 1310720 | tf_op jit(solution)/shard_map/all_to_all | solution.py:318
  141.8 13.0 %copy-start = (bf16[128,2048]{1,0:T(8,128)(2,1)S(1)}, bf16[128,2048]{1,0:T(8,128)(2,1)}, u32[]{:S(2)}) copy-start(bf16[128,2048]{1,0:T(8,128)(2,1)} %r_1_.1) | copy-start | bytes 1572868
